TPU v7x, 32 devices: a whole 2x2x4 slice. The times are simulated.
32 devices in a mesh: space: 8 (over z, y), tm: 4 (over x, core).
Axes of the slice: x: 2, y: 2, z: 4, core: 2. Of those that a mesh axis runs over, the one named last changes fastest.
Arguments:
- field: float32 [8192, 8192], P('space', 'tm'), may hold values from -6 to 6
- range_test: float32 [8192, 256], P('tm'), may hold values from -0.0625 to 0.0625
- corange_test: float32 [512, 8192], P(None, 'space'), may hold values from -0.0625 to 0.0625
Outputs:
- left_factor: float32 [8192, 256], P('space')
- right_factor: float32 [256, 8192], P(None, 'tm')
- residual: float32 [8192, 8192], P('space', 'tm')
All inputs are finite; a program needn't handle non-finite values.
Results may differ from a plain program's by a relative error of at most 0.00017.
Values sent between devices are 32-bit elements; how exact they have to be, the bound alone decides.
No kernel may reach another device: no remote copies, remote signals or barrier semaphores. Data moves between devices by JAX's collectives and lax.ppermute only.
A program may use at most 128 MiB of HBM per device.

v0:
```python
import jax
import jax.numpy as jnp
from jax import lax
from jax.sharding import PartitionSpec as P


def product(left, right):
    return jnp.dot(left, right, preferred_element_type=jnp.float32, precision=lax.Precision.HIGHEST)


def per_device(field, range_test, corange_test):
    sketch = lax.psum(product(field, range_test), "tm")
    gram = lax.psum(product(sketch.T, sketch), "space")
    lower = jnp.linalg.cholesky(gram)
    basis = lax.linalg.triangular_solve(
        lower, sketch, left_side=False, lower=True, transpose_a=True
    )
    core = lax.psum(product(corange_test, basis), "space")
    normal = product(core.T, core)
    factor = jnp.linalg.cholesky(normal)
    projector = product(core.T, corange_test)
    rhs = lax.psum(product(projector, field), "space")
    middle = lax.linalg.triangular_solve(factor, rhs, left_side=True, lower=True)
    right_factor = lax.linalg.triangular_solve(
        factor, middle, left_side=True, lower=True, transpose_a=True
    )
    residual = field - product(basis, right_factor)
    total_cells = basis.shape[0] * lax.axis_size("space")
    left_factor = basis * jnp.sqrt(jnp.float32(total_cells))
    return (left_factor, right_factor, residual)


def solution(mesh):
    return jax.shard_map(
        per_device,
        mesh=mesh,
        in_specs=(P("space", "tm"), P("tm", None), P(None, "space")),
        out_specs=(P("space", None), P(None, "tm"), P("space", "tm")),
        check_vma=False,
    )
```

profile of v0, /device:TPU:0, one launch (start us, length us, event | category | flops | bytes accessed | tf_op | source)
XLA Modules:
  0.0 414.8 jit_solution(5854967375175063858)
XLA Ops:
  7.2 10.7 %fusion.24 = f32[1024,256]{1,0:T(8,128)} fusion(f32[1024,2048]{1,0:T(8,128)} %param.4, f32[2048,256]{1,0:T(8,128)} %param.5), kind=kOutput, calls=%fused_computation.63 | convolution fusion | flops 6442450944 | bytes 11534336 | tf_op jit(solution)/shard_map/dot_general | solution.py:8
  18.0 38.9 %all-reduce.6.cloned.1.call-done = f32[1024,256]{1,0:T(8,128)} async-done(((f32[1024,256]{1,0:T(8,128)}), f32[1024,256]{1,0:T(8,128)}) %all-reduce.6.cloned.1.call-update) | async-done | bytes 1048592 | tf_op jit(solution)/shard_map/psum | solution.py:12
  56.8 4.1 fusion.25
  61.5 70.6 %all-reduce.8.cloned.1.call-done = f32[256,256]{0,1:T(8,128)} async-done(((f32[256,256]{0,1:T(8,128)}), f32[256,256]{0,1:T(8,128)}) %all-reduce.8.cloned.1.call-update) | async-done | bytes 262160 | tf_op jit(solution)/shard_map/psum | solution.py:13
  132.1 1.1 copy.7
  134.1 11.7 %cholesky.130 = f32[128,128]{1,0:T(8,128)S(1)} custom-call(f32[128,128]{1,0:T(8,128)S(1)} %cholesky.194), custom_call_target="Cholesky" | custom-call | tf_op jit(solution)/shard_map/jit(cholesky)/cholesky | solution.py:14
  145.9 9.8 %custom-call.19 = f32[1,128,128]{1,2,0:T(8,128)S(1)} custom-call(f32[1,128,128]{2,1,0:T(8,128)S(1)} %get-tuple-element.50), custom_call_target="InvertDiagBlocksLowerTriangular" | custom-call | tf_op jit(solution)/shard_map/jit(cholesky)/cholesky | solution.py:14
  156.2 11.7 %cholesky.147 = f32[128,128]{1,0:T(8,128)S(1)} custom-call(f32[128,128]{1,0:T(8,128)S(1)} %convolution_subtract_fusion.5), custom_call_target="Cholesky" | custom-call | tf_op jit(solution)/shard_map/jit(cholesky)/cholesky | solution.py:14
  170.0 4.2 %while.2 = (s32[]{:T(128)}, f32[256,256]{1,0:T(8,128)S(1)}, s32[2,2]{1,0:T(2,128)S(1)}, f32[2,128,128]{2,1,0:T(8,128)S(1)}, s32[]{:T(128)}) while((s32[]{:T(128)}, f32[256,256]{1,0:T(8,128)S(1)}, s32[2,2]{1,0:T(2,128)S(1)}, f32[2,128,128]{2,1,0:T(8,128)S(1)}, s32[]{:T(128)}) %tuple.46), condition=%wide.while_cond, body=%wide.while_body.sunk | while | flops 2 | bytes 131189 | solution.py:15
  170.8 1.4 bitcast_dynamic-update-slice_fusion.4
  172.8 1.4 bitcast_dynamic-update-slice_fusion.4
  174.2 19.7 %custom-call.16 = f32[2,128,128]{1,2,0:T(8,128)S(1)} custom-call(f32[2,128,128]{2,1,0:T(8,128)S(1)} %get-tuple-element.11), custom_call_target="InvertDiagBlocksLowerTriangular" | custom-call | tf_op jit(solution)/shard_map/triangular_solve | solution.py:15
  193.9 1.7 fusion.3
  195.6 2.0 convolution_subtract_fusion.3
  198.3 2.7 convolution_bitcast_fusion
  201.1 1.1 fusion.2
  202.1 2.5 copy.9
  204.7 68.1 %all-reduce.10.cloned.1.call-done = f32[512,256]{0,1:T(8,128)} async-done(((f32[512,256]{0,1:T(8,128)}), f32[512,256]{0,1:T(8,128)}) %all-reduce.10.cloned.1.call-update) | async-done | bytes 524304 | tf_op jit(solution)/shard_map/psum | solution.py:18
  272.8 1.8 fusion.26
  275.4 2.9 fusion.27
  278.4 10.7 %fusion.28 = f32[256,2048]{1,0:T(8,128)} fusion(f32[256,1024]{1,0:T(8,128)S(1)} %fusion.27, f32[1024,2048]{1,0:T(8,128)} %param.4), kind=kOutput, calls=%fused_computation.67 | convolution fusion | flops 6442450944 | bytes 11534336 | tf_op jit(solution)/shard_map/dot_general | solution.py:8
  290.8 11.7 %cholesky.164 = f32[128,128]{1,0:T(8,128)S(1)} custom-call(f32[128,128]{1,0:T(8,128)S(1)} %cholesky.197), custom_call_target="Cholesky" | custom-call | tf_op jit(solution)/shard_map/jit(cholesky)/cholesky | solution.py:20
  302.6 9.8 %custom-call.20 = f32[1,128,128]{1,2,0:T(8,128)S(1)} custom-call(f32[1,128,128]{2,1,0:T(8,128)S(1)} %get-tuple-element.46), custom_call_target="InvertDiagBlocksLowerTriangular" | custom-call | tf_op jit(solution)/shard_map/jit(cholesky)/cholesky | solution.py:20
  313.5 1.1 convolution_subtract_fusion.4
  314.6 11.7 %cholesky.181 = f32[128,128]{1,0:T(8,128)S(1)} custom-call(f32[128,128]{1,0:T(8,128)S(1)} %convolution_subtract_fusion.4), custom_call_target="Cholesky" | custom-call | tf_op jit(solution)/shard_map/jit(cholesky)/cholesky | solution.py:20
  329.9 3.9 while.3
  330.5 1.3 bitcast_dynamic-update-slice_fusion.5
  332.5 1.3 bitcast_dynamic-update-slice_fusion.5
  334.5 20.7 %custom-call.17 = f32[2,128,128]{1,2,0:T(8,128)S(1)} custom-call(f32[2,128,128]{2,1,0:T(8,128)} %copy-done.5), custom_call_target="InvertDiagBlocksLowerTriangular" | custom-call | tf_op jit(solution)/shard_map/triangular_solve | solution.py:24
  355.2 35.5 %all-reduce.12.cloned.1.call-done = f32[256,2048]{1,0:T(8,128)} async-done(((f32[256,2048]{1,0:T(8,128)}), f32[256,2048]{1,0:T(8,128)}) %all-reduce.12.cloned.1.call-update) | async-done | bytes 2097168 | tf_op jit(solution)/shard_map/psum | solution.py:22
  390.7 2.4 fusion
  398.5 9.4 %convolution_subtract_fusion = f32[1024,2048]{1,0:T(8,128)} fusion(f32[1024,2048]{1,0:T(8,128)S(1)} %bitcast.82, f32[256,2048]{1,0:T(8,128)S(1)} %pad_maximum_fusion, f32[1024,128]{0,1:T(8,128)S(1)} %fusion.9, f32[1024,128]{0,1:T(8,128)S(1)} %fusion.3), kind=kOutput, calls=%fused_computation.4 | convolution fusion | flops 6444810240 | bytes 19922944 | tf_op jit(solution)/shard_map/dot_general | solution.py:8
  (63 shorter events, 17.9 us)
Async XLA Ops:
  7.2 191.1 %copy-start = (f32[512,1024]{1,0:T(8,128)S(1)}, f32[512,1024]{1,0:T(8,128)}, u32[]{:S(2)}) copy-start(f32[512,1024]{1,0:T(8,128)} %param.6) | copy-start | bytes 6291460
  7.2 49.7 %all-reduce.6.cloned.1.call-start = ((), (), s32[]{:S(2)}) async-start(), calls=%async_computation | async-start | bytes 2097152 | tf_op jit(solution)/shard_map/psum | solution.py:12
  17.9 114.1 %all-reduce.8.cloned.1.call-start = ((), (), s32[]{:S(2)}) async-start(), calls=%async_computation.1 | async-start | bytes 524288 | tf_op jit(solution)/shard_map/psum | solution.py:13
  60.9 211.8 %all-reduce.10.cloned.1.call-start = ((), (), s32[]{:S(2)}) async-start(), calls=%async_computation.2 | async-start | bytes 1048576 | tf_op jit(solution)/shard_map/psum | solution.py:18
  201.0 189.7 %all-reduce.12.cloned.1.call-start = ((), (), s32[]{:S(2)}) async-start(), calls=%async_computation.3 | async-start | bytes 4194304 | tf_op jit(solution)/shard_map/psum | solution.py:22
  290.1 0.7 copy-start.4
  327.0 1.9 copy-start.3
  333.8 0.7 copy-start.5
  390.7 2.4 copy-start.2
  393.1 5.3 %slice-start = ((s8[8388608]{0:T(1024)(128)(4,1)}), s8[4194304]{0:T(1024)(128)(4,1)S(1)}, s32[]{:S(2)}) async-start(s8[8388608]{0:T(1024)(128)(4,1)} %bitcast.81), calls=%async_computation.4 | async-start | bytes 8388608
  396.2 2.2 slice-start.1
  398.5 9.4 %copy-start.1 = (f32[256,2048]{1,0:T(8,128)}, f32[256,2048]{1,0:T(8,128)S(1)}, u32[]{:S(2)}) copy-start(f32[256,2048]{1,0:T(8,128)S(1)} %pad_maximum_fusion) | copy-start | bytes 6291460
Sparse Core Ops, SparseCore 0:
  18.0 38.7 all-reduce.5
  61.1 70.8 all-reduce.7
  201.1 71.5 all-reduce.9
  289.3 101.3 all-reduce.11
where the time goes:
time: 420 us; the launch traced here: 415 us
  waiting for transfers between devices  213 us (51%)
  other arithmetic  113 us (27%)
  matrix products  56.8 us (14%)
  between operations  17.1 us (4%)
  local copies, waits for them, and re-layouts  13.8 us (3%)
    psum x1, waiting for transfers between devices, per_device(): gram = lax.psum(product(sketch.T, sketch), 'space')  70.6 us
    psum x1, waiting for transfers between devices, per_device(): core = lax.psum(product(corange_test, basis), 'space')  68.1 us
    dot_general x7, matrix products, product(): jnp.dot(left, right, preferred_element_type=jnp.float32, precision=lax.Pr...  42.3 us
    psum x1, waiting for transfers between devices, per_device(): sketch = lax.psum(product(field, range_test), 'tm')  38.9 us
    psum x1, waiting for transfers between devices, per_device(): rhs = lax.psum(product(projector, field), 'space')  35.5 us
    another operation x7, other arithmetic, per_device(): factor = jnp.linalg.cholesky(normal)  34.6 us
    another operation x6, other arithmetic, per_device(): lower = jnp.linalg.cholesky(gram)  34 us
    another operation x3, other arithmetic, per_device(): lax.linalg.triangular_solve(factor, middle, left_side=True, lower=True, t...  21.8 us
  transfers between devices with their start and end apart: 4, of which 4 were waited for; matrix products, arithmetic and copies ran while one was open for 16% of the time, Pallas kernels for 0%

commit v1 on v0

v1 whole, which is shorter than its diff:
```python
import functools

import jax
import jax.numpy as jnp
from jax import lax
from jax.experimental import pallas as pl
from jax.experimental.pallas import tpu as pltpu
from jax.sharding import PartitionSpec as P

F32 = jnp.float32
BF16 = jnp.bfloat16
VMEM = pl.BlockSpec(memory_space=pltpu.VMEM)
SMEM = pl.BlockSpec(memory_space=pltpu.SMEM)
PANEL = 64
PARAMS = pltpu.CompilerParams(vmem_limit_bytes=48 * 2**20)


def exact(a, b, dims):
    return lax.dot_general(
        a, b, (dims, ((), ())), precision=lax.Precision.HIGHEST, preferred_element_type=F32
    )


def split(x):
    hi = x.astype(BF16)
    return hi, (x - hi.astype(F32)).astype(BF16)


def three(a, b, dims=((1,), (0,))):
    def one(x, y):
        return lax.dot_general(x, y, (dims, ((), ())), preferred_element_type=F32)

    return one(a[0], b[0]) + (one(a[0], b[1]) + one(a[1], b[0]))


def cost(macs, moved):
    return pl.CostEstimate(flops=2 * macs, bytes_accessed=moved, transcendentals=0)


def shape(*dims, dtype=F32):
    return jax.ShapeDtypeStruct(dims, dtype)


def sketch_kernel(steps, place, field, test, corange, s_send, s_keep, m_send, m_keep, thi, tlo, total):
    i = pl.program_id(0)

    @pl.when(i == 0)
    def _():
        thi[...], tlo[...] = split(test[...])
        total[...] = jnp.zeros_like(total)

    s = three(split(field[...]), (thi[...], tlo[...]))

    @pl.when(i < steps // 2)
    def _():
        s_send[...] = s

    @pl.when(i >= steps // 2)
    def _():
        s_keep[...] = s

    total[...] += three(split(corange[...]), split(s))

    @pl.when(i == steps - 1)
    def _():
        rows = total.shape[0] // 8
        mine = place[steps]
        for out, slots in ((m_send, (1, 5, 3, 7)), (m_keep, (0, 4, 2, 6))):
            for j, slot in enumerate(slots):
                out[j * rows:(j + 1) * rows, :] = total[pl.ds(pl.multiple_of((mine ^ slot) * rows, 8), rows), :]


def sketches(place, steps, field, test, corange):
    cells, times = field.shape
    rank = test.shape[1]
    rows = cells // steps
    half = steps // 2
    wide = corange.shape[0]
    return pl.pallas_call(
        functools.partial(sketch_kernel, steps),
        grid_spec=pltpu.PrefetchScalarGridSpec(
            num_scalar_prefetch=1,
            grid=(steps,),
            in_specs=[
                pl.BlockSpec((rows, times), lambda i, p: (p[i], 0)),
                pl.BlockSpec((times, rank), lambda i, p: (0, 0)),
                pl.BlockSpec((wide, rows), lambda i, p: (0, p[i])),
            ],
            out_specs=[
                pl.BlockSpec((rows, rank), lambda i, p: (jnp.minimum(i, half - 1), 0)),
                pl.BlockSpec((rows, rank), lambda i, p: (jnp.maximum(i - half, 0), 0)),
                pl.BlockSpec((wide // 2, rank), lambda i, p: (0, 0)),
                pl.BlockSpec((wide // 2, rank), lambda i, p: (0, 0)),
            ],
            scratch_shapes=[
                pltpu.VMEM((times, rank), BF16),
                pltpu.VMEM((times, rank), BF16),
                pltpu.VMEM((wide, rank), F32),
            ],
        ),
        out_shape=[shape(cells // 2, rank)] * 2 + [shape(wide // 2, rank)] * 2,
        compiler_params=PARAMS,
        cost_estimate=cost(3 * cells * rank * (times + wide), 4 * cells * times),
        name="sketches",
    )(place, field, test, corange)


def gram_kernel(core, a, b, s, g_send, g_keep, total):
    x = a[...] + b[...]
    s[...] = x
    total[...] = exact(x, x, ((0,), (0,)))
    rows = total.shape[0] // 2
    me = core[0]
    g_keep[...] = total[pl.ds(pl.multiple_of(me * rows, 8), rows), :]
    g_send[...] = total[pl.ds(pl.multiple_of((1 - me) * rows, 8), rows), :]


def gram_of(core, a, b):
    rank = a.shape[1]
    return pl.pallas_call(
        gram_kernel,
        out_shape=[shape(*a.shape), shape(rank // 2, rank), shape(rank // 2, rank)],
        in_specs=[SMEM, VMEM, VMEM],
        out_specs=[VMEM] * 3,
        scratch_shapes=[pltpu.VMEM((rank, rank), F32)],
        cost_estimate=cost(6 * a.shape[0] * rank * rank, 12 * a.shape[0] * rank),
        name="gram",
    )(core, a, b)


ORDER = (0, 4, 2, 6, 1, 5, 3, 7)


def project_kernel(mine, near, far, corange, normal, phi, plo, m, om):
    half = near.shape[0]
    m[:half] = near[...]
    m[half:] = far[...]
    rows = m.shape[0] // 8
    for j, slot in enumerate(ORDER):
        om[j * rows:(j + 1) * rows, :] = corange[pl.ds(pl.multiple_of((mine[0] ^ slot) * rows, 8), rows), :]
    x = m[...]
    normal[...] = exact(x, x, ((0,), (0,)))
    p = three(split(x.T), split(om[...]))
    phi[...], plo[...] = split(p)


def project(mine, near, far, corange):
    wide, cells = corange.shape
    rank = near.shape[1]
    return pl.pallas_call(
        project_kernel,
        out_shape=[shape(rank, rank), shape(rank, cells, dtype=BF16), shape(rank, cells, dtype=BF16)],
        in_specs=[SMEM, VMEM, VMEM, VMEM],
        out_specs=[VMEM] * 3,
        scratch_shapes=[pltpu.VMEM((wide, rank), F32), pltpu.VMEM((wide, cells), F32)],
        compiler_params=PARAMS,
        cost_estimate=cost(6 * wide * rank * rank + 3 * wide * rank * cells, 4 * wide * cells),
        name="project",
    )(mine, near, far, corange)


def rhs_kernel(place, phi, plo, field, *outs):
    i = pl.program_id(0)
    x = three((phi[...], plo[...]), split(field[...]))
    for k, out in enumerate(outs):
        @pl.when(i == k)
        def _():
            out[...] = x


def rhs_blocks(place, phi, plo, field, count, blocks):
    rank, cells = phi.shape
    cols = field.shape[1] // blocks
    return pl.pallas_call(
        rhs_kernel,
        grid_spec=pltpu.PrefetchScalarGridSpec(
            num_scalar_prefetch=1,
            grid=(count,),
            in_specs=[
                pl.BlockSpec((rank, cells), lambda i, p: (0, 0)),
                pl.BlockSpec((rank, cells), lambda i, p: (0, 0)),
                pl.BlockSpec((cells, cols), lambda i, p: (0, p[i])),
            ],
            out_specs=[pl.BlockSpec((rank, cols), lambda i, p: (0, 0))] * count,
        ),
        out_shape=[shape(rank, cols)] * count,
        compiler_params=PARAMS,
        cost_estimate=cost(3 * count * rank * cells * cols, 4 * count * cells * cols),
        name="rhs",
    )(place, phi, plo, field)


def eliminate(blocks):
    width = blocks[0].shape[1]
    groups = PANEL // 8
    mats = [[x[8 * g:8 * g + 8] for g in range(groups)] for x in blocks]
    row = lax.broadcasted_iota(jnp.int32, (8, width), 0)
    for s in range(groups):
        columns = [
            {
                g: [jnp.broadcast_to(m[g][:, 8 * s + j:8 * s + j + 1], (8, width)) for j in range(8)]
                for g in range(s, groups)
            }
            for m in mats
        ]
        for i in range(8):
            for m, c in zip(mats, columns):
                inverse = 1.0 / c[s][i][i:i + 1]
                below = {g: c[g][i] for g in range(s, groups)}
                below[s] = jnp.where(row > i, below[s], 0.0)
                for j in range(i + 1, 8):
                    f = c[s][j][i:i + 1] * inverse
                    for g in range(s, groups):
                        c[g][j] = c[g][j] - below[g] * f
                u = m[s][i:i + 1] * inverse
                for g in range(s, groups):
                    m[g] = m[g] - below[g] * u
    return mats


def iotas(dims):
    return lax.broadcasted_iota(jnp.int32, dims, 0), lax.broadcasted_iota(jnp.int32, dims, 1)


def factor_both(n, tables):
    r, c = iotas((PANEL, PANEL))
    eye = jnp.where(r == c, 1.0, 0.0)
    r, c = iotas((PANEL, 2 * PANEL))
    for k in range(n // PANEL):
        lo, hi = k * PANEL, (k + 1) * PANEL
        blocks = [jnp.concatenate([t[lo:hi, lo:hi], eye], axis=1) for t in tables]
        left = lo // 128 * 128
        right = n + (hi + 127) // 128 * 128
        rest = hi // 128 * 128
        for t, m in zip(tables, eliminate(blocks)):
            x = jnp.concatenate(m, axis=0)
            pivots = jnp.sum(jnp.where(r == c, x, 0.0), axis=1, keepdims=True)
            inverse = (x * lax.rsqrt(pivots))[:, PANEL:]
            panel = exact(inverse, t[lo:hi, left:right], ((1,), (0,)))
            if hi < n:
                update = exact(panel[:, rest - left:n - left], panel[:, rest - left:], ((0,), (0,)))
                t[hi:n, rest:right] = t[hi:n, rest:right] - update[hi - rest:]
            t[lo:hi, left:right] = panel


def factor_kernel(g_near, g_far, core, normal, upper, inverse, normal_inverse, t1, t2):
    n = normal.shape[0]
    half = n // 2
    r, c = iotas((n, n))
    eye = jnp.where(r == c, 1.0, 0.0)
    me = core[0]
    t1[pl.ds(pl.multiple_of(me * half, 8), half), :n] = g_near[...]
    t1[pl.ds(pl.multiple_of((1 - me) * half, 8), half), :n] = g_far[...]
    t1[:, n:] = eye
    t2[:, :n] = normal[...]
    t2[:, n:] = eye
    factor_both(n, (t1, t2))
    upper[...] = jnp.where(r <= c, t1[:, :n], 0.0)
    inverse[...] = t1[:, n:]
    k = t2[:, n:]
    normal_inverse[...] = exact(k, k, ((0,), (0,)))


def factor(core, g_near, g_far, normal):
    n = normal.shape[0]
    return pl.pallas_call(
        factor_kernel,
        out_shape=[shape(n, n)] * 3,
        in_specs=[VMEM, VMEM, SMEM, VMEM],
        out_specs=[VMEM] * 3,
        scratch_shapes=[pltpu.VMEM((n, 2 * n), F32)] * 2,
        compiler_params=PARAMS,
        cost_estimate=cost(7 * 10**9, 4 * n * n * 8),
        name="factor",
    )(g_near, g_far, core, normal)


def solve_kernel(inverse, *refs):
    total = refs[0][...]
    for ref in refs[1:-1]:
        total += ref[...]
    refs[-1][...] = exact(inverse[...], total, ((1,), (0,)))


def solve(inverse, terms):
    return pl.pallas_call(
        solve_kernel,
        out_shape=shape(*terms[0].shape),
        cost_estimate=cost(6 * inverse.shape[0] * terms[0].size, 4 * terms[0].size * (len(terms) + 2)),
        name="solve",
    )(inverse, *terms)


def output_kernel(count, scale, place, s0, s2, s13, upper, inverse, field, *refs):
    blocks = refs[:count]
    left, right, residual, shi, slo, uhi, ulo, z = refs[count:]
    i = pl.program_id(0)
    rows = s0.shape[0]
    tm = place[count]
    pieces = ((0, s0, 0), (2, s2, 0), (1, s13, 0), (3, s13, rows))

    @pl.when(i == 0)
    def _():
        uhi[...], ulo[...] = split(upper[...])
        inv = split(inverse[...])
        for slot, ref, start in pieces:
            at = pl.ds(pl.multiple_of((tm ^ slot) * rows, 16), rows)
            s = split(ref[start:start + rows, :])
            shi[at, :], slo[at, :] = s
            left[at, :] = three(s, inv, ((1,), (1,))) * scale

    for k in range(count):
        @pl.when(i == k)
        def _():
            z[...] = blocks[k][...]

    zs = split(z[...])
    right[...] = three((uhi[...], ulo[...]), zs)
    residual[...] = field[...] - three((shi[...], slo[...]), zs)


def outputs(place, scale, s0, s2, s13, upper, inverse, field, blocks):
    cells, times = field.shape
    rank, cols = blocks[0].shape
    count = len(blocks)
    whole = lambda *dims: pl.BlockSpec(dims, lambda i, p: (0,) * len(dims))
    return pl.pallas_call(
        functools.partial(output_kernel, count, scale),
        grid_spec=pltpu.PrefetchScalarGridSpec(
            num_scalar_prefetch=1,
            grid=(count,),
            in_specs=[whole(*s0.shape), whole(*s2.shape), whole(*s13.shape), whole(rank, rank), whole(rank, rank),
                      pl.BlockSpec((cells, cols), lambda i, p: (0, p[i]))] + [whole(rank, cols)] * count,
            out_specs=[
                whole(cells, rank),
                pl.BlockSpec((rank, cols), lambda i, p: (0, p[i])),
                pl.BlockSpec((cells, cols), lambda i, p: (0, p[i])),
            ],
            scratch_shapes=[pltpu.VMEM((cells, rank), BF16)] * 2
            + [pltpu.VMEM((rank, rank), BF16)] * 2
            + [pltpu.VMEM((rank, cols), F32)],
        ),
        out_shape=[shape(cells, rank), shape(rank, times), shape(cells, times)],
        compiler_params=PARAMS,
        cost_estimate=cost(3 * cells * rank * times, 8 * cells * times),
        name="outputs",
    )(place, s0, s2, s13, upper, inverse, field, *blocks)


def swap(axis, bit):
    n = lax.axis_size(axis)

    def go(x):
        return lax.ppermute(x, axis, [(i, i ^ bit) for i in range(n)])

    return go


def per_device(field, range_test, corange_test):
    spaces, tms = lax.axis_size("space"), lax.axis_size("tm")
    space, tm = lax.axis_index("space"), lax.axis_index("tm")
    scale = float(field.shape[0] * spaces) ** 0.5
    core, y, x = tm & 1, space & 1, (tm >> 1) & 1
    to_core, to_x = swap("tm", 1), swap("tm", 2)
    to_y = swap("space", 1)

    slots = jnp.array([1, 3, 2, 0], jnp.int32)
    rows_at = ((tm ^ slots)[:, None] * 2 + jnp.arange(2, dtype=jnp.int32)[None, :]).reshape(-1)
    mine = (core | (y << 1) | (x << 2)).astype(jnp.int32)
    place = jnp.concatenate([rows_at.astype(jnp.int32), mine[None]])
    core_at = core.astype(jnp.int32)[None]

    s_send, s_keep, m_send, m_keep = sketches(place, 8, field, range_test, corange_test)
    quarter = s_keep.shape[0] // 2

    m = m_keep + to_core(m_send)
    rows = m.shape[0] // 4
    m = m[:2 * rows] + to_y(m[2 * rows:])
    m = m[:rows] + to_x(m[rows:])
    bit = 2
    while bit < spaces:
        m = m + swap("space", bit)(m)
        bit *= 2
    m = jnp.concatenate([m, to_x(m)], axis=0)
    m = jnp.concatenate([m, to_y(m)], axis=0)
    m_far = to_core(m)

    got = to_core(s_send)
    s_x = to_x(s_keep[:quarter] + got[quarter:])
    s0, g_send, g_keep = gram_of(core_at, s_keep[quarter:] + got[:quarter], s_x)
    g = g_keep + to_core(g_send)
    g = g + to_x(g)
    bit = 1
    while bit < spaces:
        g = g + swap("space", bit)(g)
        bit *= 2
    g_far = to_core(g)

    normal, phi, plo = project(mine[None], m, m_far, corange_test)
    count = min(spaces, 8)
    near = space & (count - 1)
    send_at = (near ^ jnp.arange(count - 1, 0, -2, dtype=jnp.int32)).astype(jnp.int32)
    keep_at = (near ^ jnp.arange(count - 2, -1, -2, dtype=jnp.int32)).astype(jnp.int32)
    sent = rhs_blocks(send_at, phi, plo, field, count // 2, count)
    kept = rhs_blocks(keep_at, phi, plo, field, count // 2, count)
    terms = []
    for k, slot in enumerate(range(count - 2, -1, -2)):
        got = to_y(sent[k])
        if slot == 0:
            terms += [kept[k], got]
        else:
            terms.append(swap("space", slot)(kept[k] + got))

    bit = count
    while bit < spaces:
        mine_sum = functools.reduce(jnp.add, terms)
        terms = [mine_sum, swap("space", bit)(mine_sum)]
        bit *= 2

    upper, inverse, normal_inverse = factor(core_at, g, g_far, normal)
    z0 = solve(normal_inverse, terms)

    s2 = to_x(s0)
    s13 = to_core(jnp.concatenate([s0, s2], axis=0))

    blocks = [None] * count
    blocks[0] = z0
    blocks[1] = to_y(z0)
    for slot in range(2, count, 2):
        blocks[slot] = swap("space", slot)(z0)
    for slot in range(2, count, 2):
        blocks[slot + 1] = to_y(blocks[slot])

    at = jnp.concatenate([(near ^ jnp.arange(count, dtype=jnp.int32)).astype(jnp.int32), tm.astype(jnp.int32)[None]])
    return outputs(at, scale, s0, s2, s13, upper, inverse, field, blocks)


def solution(mesh):
    return jax.shard_map(
        per_device,
        mesh=mesh,
        in_specs=(P("space", "tm"), P("tm", None), P(None, "space")),
        out_specs=(P("space", None), P(None, "tm"), P("space", "tm")),
        check_vma=False,
    )
```

time: 420 us -> 160 us (0.38); the launches traced: 415 us -> 160 us
  waiting for transfers between devices: 213 us -> 55.4 us
  other arithmetic: 113 us -> 2.91 us
  matrix products: 56.8 us -> 0 us
  Pallas kernels: 0 us -> 54.4 us
  starting transfers between devices: 0.63 us -> 39.7 us
  between operations: 17.1 us -> 0.89 us
  local copies, waits for them, and re-layouts: 13.8 us -> 6.45 us
    psum x4 -> x0, waiting for transfers between devices: 213 us -> none  [the longest x1 70.6 us: per_device(): gram = lax.psum(product(sketch.T, sketch), 'space')]
    another operation x19 -> x0, other arithmetic: 110 us -> none  [the longest x7 34.6 us: per_device(): factor = jnp.linalg.cholesky(normal)]
    ppermute x0 -> x32, waiting for transfers between devices: none -> 55.4 us  [go(): return lax.ppermute(x, axis, [(i, i ^ bit) for i in range(n)])]
    pallas_call x0 -> x8, Pallas kernels: none -> 54.4 us  [the longest x1 13 us: sketches(): pl.pallas_call(functools.partial(sketch_kernel, steps), grid_spec=pltpu.P...]
    dot_general x7 -> x0, matrix products: 42.3 us -> none  [product(): jnp.dot(left, right, preferred_element_type=jnp.float32, precision=lax.Pr...]
    ppermute x0 -> x32, starting transfers between devices: none -> 39.7 us  [go(): return lax.ppermute(x, axis, [(i, i ^ bit) for i in range(n)])]
    another operation x13 -> x0, matrix products: 14.5 us -> none  [the longest x3 4.46 us: per_device(): lax.linalg.triangular_solve(factor, rhs, left_side=True, lower=True)]
    another operation x17 -> x0, local copies, waits for them, and re-layouts: 7.95 us -> none
  transfers between devices with their start and end apart: 4 -> 32, of which waited for: 4 -> 16; matrix products, arithmetic and copies ran while one was open for 16% -> 1% of each run, Pallas kernels for 0% -> 17%
where the time goes in v1:
time: 160 us
  waiting for transfers between devices  55.4 us (35%)
  Pallas kernels  54.4 us (34%)
  starting transfers between devices  39.7 us (25%)
  local copies, waits for them, and re-layouts  6.45 us (4%)
  other arithmetic  2.91 us (2%)
    ppermute x32, waiting for transfers between devices, go(): return lax.ppermute(x, axis, [(i, i ^ bit) for i in range(n)])  55.4 us
    ppermute x32, starting transfers between devices, go(): return lax.ppermute(x, axis, [(i, i ^ bit) for i in range(n)])  39.7 us
    pallas_call x1, Pallas kernels, sketches(): pl.pallas_call(functools.partial(sketch_kernel, steps), grid_spec=pltpu.P...  13 us
    pallas_call x1, Pallas kernels, factor(): pl.pallas_call(factor_kernel, out_shape=[shape(n, n)] * 3, in_specs=[VMEM...  12.8 us
    pallas_call x1, Pallas kernels, outputs(): pl.pallas_call(functools.partial(output_kernel, count, scale), grid_spec=...  12.5 us
    pallas_call x2, Pallas kernels, rhs_blocks(): pl.pallas_call(rhs_kernel, grid_spec=pltpu.PrefetchScalarGridSpec(num_sca...  10 us
    unnamed x24, local copies, waits for them, and re-layouts  6.34 us
  transfers between devices with their start and end apart: 32, of which 16 were waited for; matrix products, arithmetic and copies ran while one was open for 1% of the time, Pallas kernels for 17%

profile of v1, /device:TPU:0, one launch (start us, length us, event | category | flops | bytes accessed | tf_op | source)
XLA Modules:
  0.0 159.6 jit_solution(13572690507151396786)
XLA Ops:
  1.5 1.6 copy-done.4
  3.1 1.6 copy-done.5
  4.7 13.0 %sketches.1 = (f32[512,256]{1,0:T(8,128)S(1)}, f32[512,256]{1,0:T(8,128)S(1)}, f32[256,256]{1,0:T(8,128)S(1)}, f32[256,256]{1,0:T(8,128)S(1)}) custom-call(s32[9]{0:T(128)S(1)} %pad_add_fusion.1.place, f32[1024,2048]{1,0:T(8,128)} %field.7, f32[2048,256]{1,0:T(8,128)S(1)} %copy-done.4, f32[512,1024]{1,0:T(8,128)S(1)} %copy-done.5), custom_call_target="tpu_custom_call" | custom-call | flops 4026531840 | bytes 8388608 | tf_op jit(solution)/shard_map/sketches/pallas_call | solution.py:79
  19.5 3.0 %collective-permute-start.11 = (f32[128,256]{1,0:T(8,128)S(1)}, f32[128,256]{1,0:T(8,128)S(1)}, u32[]{:S(2)}, u32[]{:S(2)}) collective-permute-start(f32[128,256]{1,0:T(8,128)S(1)} %slice.35), channel_id=1, source_target_pairs={{0,4},{4,0},{8,12},{12,8},{16,20},{20,16},{24,28},{28,24},{1,5},{5... | collective-permute-start | bytes 393224 | tf_op jit(solution)/shard_map/ppermute | solution.py:354
  22.4 3.8 %collective-permute-done.11 = f32[128,256]{1,0:T(8,128)S(1)} collective-permute-done((f32[128,256]{1,0:T(8,128)S(1)}, f32[128,256]{1,0:T(8,128)S(1)}, u32[]{:S(2)}, u32[]{:S(2)}) %collective-permute-start.11) | collective-permute-done | bytes 131104 | tf_op jit(solution)/shard_map/ppermute | solution.py:354
  26.3 1.8 %collective-permute-start.12 = (f32[64,256]{1,0:T(8,128)S(1)}, f32[64,256]{1,0:T(8,128)S(1)}, u32[]{:S(2)}, u32[]{:S(2)}) collective-permute-start(f32[64,256]{1,0:T(8,128)S(1)} %slice.37), channel_id=1, source_target_pairs={{0,2},{1,3},{2,0},{3,1},{4,6},{5,7},{6,4},{7,5},{8,10},{9,11},{10,... | collective-permute-start | bytes 196616 | tf_op jit(solution)/shard_map/ppermute | solution.py:354
  29.1 1.7 %collective-permute-done.12 = f32[64,256]{1,0:T(8,128)S(1)} collective-permute-done((f32[64,256]{1,0:T(8,128)S(1)}, f32[64,256]{1,0:T(8,128)S(1)}, u32[]{:S(2)}, u32[]{:S(2)}) %collective-permute-start.12) | collective-permute-done | bytes 65568 | tf_op jit(solution)/shard_map/ppermute | solution.py:354
  30.8 2.0 %collective-permute-start.13 = (f32[64,256]{1,0:T(8,128)S(1)}, f32[64,256]{1,0:T(8,128)S(1)}, u32[]{:S(2)}, u32[]{:S(2)}) collective-permute-start(f32[64,256]{1,0:T(8,128)S(1)} %slice_add_fusion.3), channel_id=1, source_target_pairs={{0,8},{4,12},{8,0},{12,4},{16,24},{20,28},{24,16},{28,20},{1,9},{5... | collective-permute-start | bytes 196616 | tf_op jit(solution)/shard_map/ppermute | solution.py:354
  32.9 2.3 %collective-permute-done.13 = f32[64,256]{1,0:T(8,128)S(1)} collective-permute-done((f32[64,256]{1,0:T(8,128)S(1)}, f32[64,256]{1,0:T(8,128)S(1)}, u32[]{:S(2)}, u32[]{:S(2)}) %collective-permute-start.13) | collective-permute-done | bytes 65568 | tf_op jit(solution)/shard_map/ppermute | solution.py:354
  35.2 3.6 %collective-permute-start.14 = (f32[64,256]{1,0:T(8,128)S(1)}, f32[64,256]{1,0:T(8,128)S(1)}, u32[]{:S(2)}, u32[]{:S(2)}) collective-permute-start(f32[64,256]{1,0:T(8,128)S(1)} %add.82), channel_id=1, source_target_pairs={{0,16},{4,20},{8,24},{12,28},{16,0},{20,4},{24,8},{28,12},{1,17},{... | collective-permute-start | bytes 196616 | tf_op jit(solution)/shard_map/ppermute | solution.py:354
  38.8 2.2 %collective-permute-done.14 = f32[64,256]{1,0:T(8,128)S(1)} collective-permute-done((f32[64,256]{1,0:T(8,128)S(1)}, f32[64,256]{1,0:T(8,128)S(1)}, u32[]{:S(2)}, u32[]{:S(2)}) %collective-permute-start.14) | collective-permute-done | bytes 65568 | tf_op jit(solution)/shard_map/ppermute | solution.py:354
  41.1 1.9 %collective-permute-start.15 = (f32[64,256]{1,0:T(8,128)S(1)}, f32[64,256]{1,0:T(8,128)S(1)}, u32[]{:S(2)}, u32[]{:S(2)}) collective-permute-start(f32[64,256]{1,0:T(8,128)S(1)} %add.83), channel_id=1, source_target_pairs={{0,2},{1,3},{2,0},{3,1},{4,6},{5,7},{6,4},{7,5},{8,10},{9,11},{10,... | collective-permute-start | bytes 196616 | tf_op jit(solution)/shard_map/ppermute | solution.py:354
  43.6 2.2 %gram.1 = (f32[256,256]{1,0:T(8,128)}, f32[128,256]{1,0:T(8,128)}, f32[128,256]{1,0:T(8,128)}) custom-call(s32[1]{0:T(128)} %bitcast.1.core, f32[256,256]{1,0:T(8,128)} %get-tuple-element.46.a, f32[256,256]{1,0:T(8,128)} %copy-done.11), custom_call_target="tpu_custom_call" | custom-call | flops 201326592 | bytes 786432 | tf_op jit(solution)/shard_map/gram/pallas_call | solution.py:120
  45.8 1.6 collective-permute-start.16
  49.8 2.0 %collective-permute-done.16 = f32[128,256]{1,0:T(8,128)S(1)} collective-permute-done((f32[128,256]{1,0:T(8,128)S(1)}, f32[128,256]{1,0:T(8,128)S(1)}, u32[]{:S(2)}, u32[]{:S(2)}) %collective-permute-start.16) | collective-permute-done | bytes 131104 | tf_op jit(solution)/shard_map/ppermute | solution.py:354
  51.9 2.1 %collective-permute-done.5 = f32[128,256]{1,0:T(8,128)S(1)} collective-permute-done((f32[128,256]{1,0:T(8,128)S(1)}, f32[128,256]{1,0:T(8,128)S(1)}, u32[]{:S(2)}, u32[]{:S(2)}) %collective-permute-start.5) | collective-permute-done | bytes 131104 | tf_op jit(solution)/shard_map/ppermute | solution.py:354
  55.5 3.6 %collective-permute-done.6 = f32[128,256]{1,0:T(8,128)S(1)} collective-permute-done((f32[128,256]{1,0:T(8,128)S(1)}, f32[128,256]{1,0:T(8,128)S(1)}, u32[]{:S(2)}, u32[]{:S(2)}) %collective-permute-start.6) | collective-permute-done | bytes 131104 | tf_op jit(solution)/shard_map/ppermute | solution.py:354
  64.1 3.5 %collective-permute-start.8 = (f32[128,256]{1,0:T(8,128)S(1)}, f32[128,256]{1,0:T(8,128)S(1)}, u32[]{:S(2)}, u32[]{:S(2)}) collective-permute-start(f32[128,256]{1,0:T(8,128)S(1)} %add.77), channel_id=1, source_target_pairs={{0,16},{4,20},{8,24},{12,28},{16,0},{20,4},{24,8},{28,12},{1,17},{... | collective-permute-start | bytes 393224 | tf_op jit(solution)/shard_map/ppermute | solution.py:354
  67.7 4.9 %rhs.3 = (f32[256,256]{1,0:T(8,128)S(1)}, f32[256,256]{1,0:T(8,128)S(1)}, f32[256,256]{1,0:T(8,128)S(1)}, f32[256,256]{1,0:T(8,128)S(1)}) custom-call(s32[4]{0:T(128)S(1)} %get-tuple-element.47.place, bf16[256,1024]{1,0:T(8,128)(2,1)S(1)} %get-tuple-element.35.phi, bf16[256,1024]{1,0:T(8,128)(2,1)S(1)} %get-tuple-element.36.plo, f32[1024,2048]{1,0:T(8,128)} %field.7), custom_call_target="tpu_custom_call" | custom-call | flops 1610612736 | bytes 4194304 | tf_op jit(solution)/shard_map/rhs/pallas_call | solution.py:174
  72.6 1.6 collective-permute-start.18
  76.3 5.1 %rhs.2 = (f32[256,256]{1,0:T(8,128)S(1)}, f32[256,256]{1,0:T(8,128)S(1)}, f32[256,256]{1,0:T(8,128)S(1)}, f32[256,256]{1,0:T(8,128)S(1)}) custom-call(s32[4]{0:T(128)S(1)} %get-tuple-element.48.place, bf16[256,1024]{1,0:T(8,128)(2,1)S(1)} %get-tuple-element.35.phi, bf16[256,1024]{1,0:T(8,128)(2,1)S(1)} %get-tuple-element.36.plo, f32[1024,2048]{1,0:T(8,128)} %field.7), custom_call_target="tpu_custom_call" | custom-call | flops 1610612736 | bytes 4194304 | tf_op jit(solution)/shard_map/rhs/pallas_call | solution.py:174
  82.8 4.0 %collective-permute-done.20 = f32[256,256]{1,0:T(8,128)S(1)} collective-permute-done((f32[256,256]{1,0:T(8,128)S(1)}, f32[256,256]{1,0:T(8,128)S(1)}, u32[]{:S(2)}, u32[]{:S(2)}) %collective-permute-start.20) | collective-permute-done | bytes 262176 | tf_op jit(solution)/shard_map/ppermute | solution.py:354
  87.4 3.9 %collective-permute-done.22 = f32[256,256]{1,0:T(8,128)S(1)} collective-permute-done((f32[256,256]{1,0:T(8,128)S(1)}, f32[256,256]{1,0:T(8,128)S(1)}, u32[]{:S(2)}, u32[]{:S(2)}) %collective-permute-start.22) | collective-permute-done | bytes 262176 | tf_op jit(solution)/shard_map/ppermute | solution.py:354
  91.4 1.6 %collective-permute-start.23 = (f32[256,256]{1,0:T(8,128)S(1)}, f32[256,256]{1,0:T(8,128)S(1)}, u32[]{:S(2)}, u32[]{:S(2)}) collective-permute-start(f32[256,256]{1,0:T(8,128)S(1)} %add.88), channel_id=1, source_target_pairs={{0,8},{4,12},{8,0},{12,4},{16,24},{20,28},{24,16},{28,20},{1,9},{5... | collective-permute-start | bytes 786440 | tf_op jit(solution)/shard_map/ppermute | solution.py:354
  93.0 12.8 %factor.1 = (f32[256,256]{1,0:T(8,128)S(1)}, f32[256,256]{1,0:T(8,128)S(1)}, f32[256,256]{1,0:T(8,128)S(1)}) custom-call(f32[128,256]{1,0:T(8,128)S(1)} %add.78.g_near, f32[128,256]{1,0:T(8,128)S(1)} %collective-permute-done.9.g_far, s32[1]{0:T(128)} %bitcast.1.core, f32[256,256]{1,0:T(8,128)S(1)} %get-tuple-element.31.normal), custom_call_target="tpu_custom_call" | custom-call | flops 14000000000 | bytes 2097152 | tf_op jit(solution)/shard_map/factor/pallas_call | solution.py:266
  108.8 2.5 %solve.1.refs_0_ = f32[256,256]{1,0:T(8,128)} custom-call(f32[256,256]{1,0:T(8,128)} %copy-done.3, f32[256,256]{1,0:T(8,128)} %copy-done.8, f32[256,256]{1,0:T(8,128)} %copy-done.9, f32[256,256]{1,0:T(8,128)} %copy-done.10, f32[256,256]{1,0:T(8,128)} %copy-done.2, f32[256,256]{1,0:T(8,128)} %copy-done.7), custom_call_target="tpu_custom_call" | custom-call | flops 201326592 | bytes 1835008 | tf_op jit(solution)/shard_map/solve/pallas_call | solution.py:286
  112.5 3.2 %collective-permute-start.26 = (f32[256,256]{1,0:T(8,128)}, f32[256,256]{1,0:T(8,128)S(1)}, u32[]{:S(2)}, u32[]{:S(2)}) collective-permute-start(f32[256,256]{1,0:T(8,128)} %solve.1.refs_0_), channel_id=1, source_target_pairs={{0,8},{4,12},{8,0},{12,4},{16,24},{20,28},{24,16},{28,20},{1,9},{5... | collective-permute-start | bytes 786440 | tf_op jit(solution)/shard_map/ppermute | solution.py:354
  117.1 5.6 %collective-permute-done.30.refs_6_ = f32[256,256]{1,0:T(8,128)S(1)} collective-permute-done((f32[256,256]{1,0:T(8,128)}, f32[256,256]{1,0:T(8,128)S(1)}, u32[]{:S(2)}, u32[]{:S(2)}) %collective-permute-start.30) | collective-permute-done | bytes 262176 | tf_op jit(solution)/shard_map/ppermute | solution.py:354
  124.0 10.0 %collective-permute-done.28.refs_4_ = f32[256,256]{1,0:T(8,128)S(1)} collective-permute-done((f32[256,256]{1,0:T(8,128)}, f32[256,256]{1,0:T(8,128)S(1)}, u32[]{:S(2)}, u32[]{:S(2)}) %collective-permute-start.28) | collective-permute-done | bytes 262176 | tf_op jit(solution)/shard_map/ppermute | solution.py:354
  136.2 7.1 %collective-permute-done.29.refs_5_ = f32[256,256]{1,0:T(8,128)S(1)} collective-permute-done((f32[256,256]{1,0:T(8,128)S(1)}, f32[256,256]{1,0:T(8,128)S(1)}, u32[]{:S(2)}, u32[]{:S(2)}) %collective-permute-start.29) | collective-permute-done | bytes 262176 | tf_op jit(solution)/shard_map/ppermute | solution.py:354
  143.3 2.9 %collective-permute-done.27.refs_3_ = f32[256,256]{1,0:T(8,128)S(1)} collective-permute-done((f32[256,256]{1,0:T(8,128)S(1)}, f32[256,256]{1,0:T(8,128)S(1)}, u32[]{:S(2)}, u32[]{:S(2)}) %collective-permute-start.27) | collective-permute-done | bytes 262176 | tf_op jit(solution)/shard_map/ppermute | solution.py:354
  147.2 12.5 %outputs.1 = (f32[1024,256]{1,0:T(8,128)}, f32[256,2048]{1,0:T(8,128)}, f32[1024,2048]{1,0:T(8,128)}) custom-call(s32[9]{0:T(128)S(1)} %pad_add_fusion.place, f32[256,256]{1,0:T(8,128)S(1)} %copy-done.1, f32[256,256]{1,0:T(8,128)S(1)} %collective-permute-done.2.s2, f32[512,256]{1,0:T(8,128)S(1)} %collective-permute-done.3.s13, ...), custom_call_target="tpu_custom_call" | custom-call | flops 3221225472 | bytes 16777216 | tf_op jit(solution)/shard_map/outputs/pallas_call | solution.py:327
  (90 shorter events, 27.7 us)
Async XLA Ops:
  17.7 1.7 %collective-permute-start.10 = (f32[256,256]{1,0:T(8,128)S(1)}, f32[256,256]{1,0:T(8,128)S(1)}, u32[]{:S(2)}, u32[]{:S(2)}) collective-permute-start(f32[256,256]{1,0:T(8,128)S(1)} %get-tuple-element.30), channel_id=1, source_target_pairs={{0,1},{1,0},{2,3},{3,2},{4,5},{5,4},{6,7},{7,6},{8,9},{9,8},{10,11... | collective-permute-start | bytes 786440 | tf_op jit(solution)/shard_map/ppermute | solution.py:354
  18.3 9.8 %collective-permute-start = (f32[512,256]{1,0:T(8,128)S(1)}, f32[512,256]{1,0:T(8,128)S(1)}, u32[]{:S(2)}, u32[]{:S(2)}) collective-permute-start(f32[512,256]{1,0:T(8,128)S(1)} %get-tuple-element.25), channel_id=1, source_target_pairs={{0,1},{1,0},{2,3},{3,2},{4,5},{5,4},{6,7},{7,6},{8,9},{9,8},{10,11... | collective-permute-start | bytes 1572872 | tf_op jit(solution)/shard_map/ppermute | solution.py:354
  19.5 6.8 %collective-permute-start.11 = (f32[128,256]{1,0:T(8,128)S(1)}, f32[128,256]{1,0:T(8,128)S(1)}, u32[]{:S(2)}, u32[]{:S(2)}) collective-permute-start(f32[128,256]{1,0:T(8,128)S(1)} %slice.35), channel_id=1, source_target_pairs={{0,4},{4,0},{8,12},{12,8},{16,20},{20,16},{24,28},{28,24},{1,5},{5... | collective-permute-start | bytes 393224 | tf_op jit(solution)/shard_map/ppermute | solution.py:354
  26.3 4.6 %collective-permute-start.12 = (f32[64,256]{1,0:T(8,128)S(1)}, f32[64,256]{1,0:T(8,128)S(1)}, u32[]{:S(2)}, u32[]{:S(2)}) collective-permute-start(f32[64,256]{1,0:T(8,128)S(1)} %slice.37), channel_id=1, source_target_pairs={{0,2},{1,3},{2,0},{3,1},{4,6},{5,7},{6,4},{7,5},{8,10},{9,11},{10,... | collective-permute-start | bytes 196616 | tf_op jit(solution)/shard_map/ppermute | solution.py:354
  28.8 14.1 %collective-permute-start.1 = (f32[256,256]{1,0:T(8,128)S(1)}, f32[256,256]{1,0:T(8,128)S(1)}, u32[]{:S(2)}, u32[]{:S(2)}) collective-permute-start(f32[256,256]{1,0:T(8,128)S(1)} %get-tuple-element.45), channel_id=1, source_target_pairs={{0,2},{1,3},{2,0},{3,1},{4,6},{5,7},{6,4},{7,5},{8,10},{9,11},{10,... | collective-permute-start | bytes 786440 | tf_op jit(solution)/shard_map/ppermute | solution.py:354
  30.8 4.3 %collective-permute-start.13 = (f32[64,256]{1,0:T(8,128)S(1)}, f32[64,256]{1,0:T(8,128)S(1)}, u32[]{:S(2)}, u32[]{:S(2)}) collective-permute-start(f32[64,256]{1,0:T(8,128)S(1)} %slice_add_fusion.3), channel_id=1, source_target_pairs={{0,8},{4,12},{8,0},{12,4},{16,24},{20,28},{24,16},{28,20},{1,9},{5... | collective-permute-start | bytes 196616 | tf_op jit(solution)/shard_map/ppermute | solution.py:354
  35.2 5.9 %collective-permute-start.14 = (f32[64,256]{1,0:T(8,128)S(1)}, f32[64,256]{1,0:T(8,128)S(1)}, u32[]{:S(2)}, u32[]{:S(2)}) collective-permute-start(f32[64,256]{1,0:T(8,128)S(1)} %add.82), channel_id=1, source_target_pairs={{0,16},{4,20},{8,24},{12,28},{16,0},{20,4},{24,8},{28,12},{1,17},{... | collective-permute-start | bytes 196616 | tf_op jit(solution)/shard_map/ppermute | solution.py:354
  41.1 4.7 %collective-permute-start.15 = (f32[64,256]{1,0:T(8,128)S(1)}, f32[64,256]{1,0:T(8,128)S(1)}, u32[]{:S(2)}, u32[]{:S(2)}) collective-permute-start(f32[64,256]{1,0:T(8,128)S(1)} %add.83), channel_id=1, source_target_pairs={{0,2},{1,3},{2,0},{3,1},{4,6},{5,7},{6,4},{7,5},{8,10},{9,11},{10,... | collective-permute-start | bytes 196616 | tf_op jit(solution)/shard_map/ppermute | solution.py:354
  45.8 1.6 %collective-permute-start.4 = (f32[128,256]{1,0:T(8,128)}, f32[128,256]{1,0:T(8,128)S(1)}, u32[]{:S(2)}, u32[]{:S(2)}) collective-permute-start(f32[128,256]{1,0:T(8,128)} %get-tuple-element.28), channel_id=1, source_target_pairs={{0,1},{1,0},{2,3},{3,2},{4,5},{5,4},{6,7},{7,6},{8,9},{9,8},{10,11... | collective-permute-start | bytes 393224 | tf_op jit(solution)/shard_map/ppermute | solution.py:354
  45.8 6.0 %collective-permute-start.16 = (f32[128,256]{1,0:T(8,128)S(1)}, f32[128,256]{1,0:T(8,128)S(1)}, u32[]{:S(2)}, u32[]{:S(2)}) collective-permute-start(f32[128,256]{1,0:T(8,128)S(1)} %pad_maximum_fusion.2), channel_id=1, source_target_pairs={{0,4},{4,0},{8,12},{12,8},{16,20},{20,16},{24,28},{28,24},{1,5},{5... | collective-permute-start | bytes 393224 | tf_op jit(solution)/shard_map/ppermute | solution.py:354
  48.3 5.7 %collective-permute-start.5 = (f32[128,256]{1,0:T(8,128)S(1)}, f32[128,256]{1,0:T(8,128)S(1)}, u32[]{:S(2)}, u32[]{:S(2)}) collective-permute-start(f32[128,256]{1,0:T(8,128)S(1)} %add.74), channel_id=1, source_target_pairs={{0,2},{1,3},{2,0},{3,1},{4,6},{5,7},{6,4},{7,5},{8,10},{9,11},{10,... | collective-permute-start | bytes 393224 | tf_op jit(solution)/shard_map/ppermute | solution.py:354
  51.8 9.4 %collective-permute-start.17 = (f32[256,256]{1,0:T(8,128)S(1)}, f32[256,256]{1,0:T(8,128)S(1)}, u32[]{:S(2)}, u32[]{:S(2)}) collective-permute-start(f32[256,256]{1,0:T(8,128)S(1)} %pad_maximum_fusion.1.near), channel_id=1, source_target_pairs={{0,1},{1,0},{2,3},{3,2},{4,5},{5,4},{6,7},{7,6},{8,9},{9,8},{10,11... | collective-permute-start | bytes 786440 | tf_op jit(solution)/shard_map/ppermute | solution.py:354
  54.0 5.0 %collective-permute-start.6 = (f32[128,256]{1,0:T(8,128)S(1)}, f32[128,256]{1,0:T(8,128)S(1)}, u32[]{:S(2)}, u32[]{:S(2)}) collective-permute-start(f32[128,256]{1,0:T(8,128)S(1)} %add.75), channel_id=1, source_target_pairs={{0,4},{4,0},{8,12},{12,8},{16,20},{20,16},{24,28},{28,24},{1,5},{5... | collective-permute-start | bytes 393224 | tf_op jit(solution)/shard_map/ppermute | solution.py:354
  59.1 5.0 %collective-permute-start.7 = (f32[128,256]{1,0:T(8,128)S(1)}, f32[128,256]{1,0:T(8,128)S(1)}, u32[]{:S(2)}, u32[]{:S(2)}) collective-permute-start(f32[128,256]{1,0:T(8,128)S(1)} %add.76), channel_id=1, source_target_pairs={{0,8},{4,12},{8,0},{12,4},{16,24},{20,28},{24,16},{28,20},{1,9},{5... | collective-permute-start | bytes 393224 | tf_op jit(solution)/shard_map/ppermute | solution.py:354
  60.4 21.0 %collective-permute-start.2 = (f32[256,256]{1,0:T(8,128)}, f32[256,256]{1,0:T(8,128)S(1)}, u32[]{:S(2)}, u32[]{:S(2)}) collective-permute-start(f32[256,256]{1,0:T(8,128)} %get-tuple-element.26.s0), channel_id=1, source_target_pairs={{0,2},{1,3},{2,0},{3,1},{4,6},{5,7},{6,4},{7,5},{8,10},{9,11},{10,... | collective-permute-start | bytes 786440 | tf_op jit(solution)/shard_map/ppermute | solution.py:354
  64.1 12.0 %collective-permute-start.8 = (f32[128,256]{1,0:T(8,128)S(1)}, f32[128,256]{1,0:T(8,128)S(1)}, u32[]{:S(2)}, u32[]{:S(2)}) collective-permute-start(f32[128,256]{1,0:T(8,128)S(1)} %add.77), channel_id=1, source_target_pairs={{0,16},{4,20},{8,24},{12,28},{16,0},{20,4},{24,8},{28,12},{1,17},{... | collective-permute-start | bytes 393224 | tf_op jit(solution)/shard_map/ppermute | solution.py:354
  72.6 9.5 %collective-permute-start.18 = (f32[256,256]{1,0:T(8,128)S(1)}, f32[256,256]{1,0:T(8,128)S(1)}, u32[]{:S(2)}, u32[]{:S(2)}) collective-permute-start(f32[256,256]{1,0:T(8,128)S(1)} %get-tuple-element.38), channel_id=1, source_target_pairs={{0,4},{4,0},{8,12},{12,8},{16,20},{20,16},{24,28},{28,24},{1,5},{5... | collective-permute-start | bytes 786440 | tf_op jit(solution)/shard_map/ppermute | solution.py:354
  74.1 12.6 %collective-permute-start.20 = (f32[256,256]{1,0:T(8,128)S(1)}, f32[256,256]{1,0:T(8,128)S(1)}, u32[]{:S(2)}, u32[]{:S(2)}) collective-permute-start(f32[256,256]{1,0:T(8,128)S(1)} %get-tuple-element.40), channel_id=1, source_target_pairs={{0,4},{4,0},{8,12},{12,8},{16,20},{20,16},{24,28},{28,24},{1,5},{5... | collective-permute-start | bytes 786440 | tf_op jit(solution)/shard_map/ppermute | solution.py:354
  74.7 16.6 %collective-permute-start.22 = (f32[256,256]{1,0:T(8,128)S(1)}, f32[256,256]{1,0:T(8,128)S(1)}, u32[]{:S(2)}, u32[]{:S(2)}) collective-permute-start(f32[256,256]{1,0:T(8,128)S(1)} %get-tuple-element.42), channel_id=1, source_target_pairs={{0,4},{4,0},{8,12},{12,8},{16,20},{20,16},{24,28},{28,24},{1,5},{5... | collective-permute-start | bytes 786440 | tf_op jit(solution)/shard_map/ppermute | solution.py:354
  76.2 16.8 %collective-permute-start.9 = (f32[128,256]{1,0:T(8,128)S(1)}, f32[128,256]{1,0:T(8,128)S(1)}, u32[]{:S(2)}, u32[]{:S(2)}) collective-permute-start(f32[128,256]{1,0:T(8,128)S(1)} %add.78.g_near), channel_id=1, source_target_pairs={{0,1},{1,0},{2,3},{3,2},{4,5},{5,4},{6,7},{7,6},{8,9},{9,8},{10,11... | collective-permute-start | bytes 393224 | tf_op jit(solution)/shard_map/ppermute | solution.py:354
  81.4 25.0 %collective-permute-start.24 = (f32[256,256]{1,0:T(8,128)S(1)}, f32[256,256]{1,0:T(8,128)S(1)}, u32[]{:S(2)}, u32[]{:S(2)}) collective-permute-start(f32[256,256]{1,0:T(8,128)S(1)} %get-tuple-element.44), channel_id=1, source_target_pairs={{0,4},{4,0},{8,12},{12,8},{16,20},{20,16},{24,28},{28,24},{1,5},{5... | collective-permute-start | bytes 786440 | tf_op jit(solution)/shard_map/ppermute | solution.py:354
  82.1 24.3 %collective-permute-start.19 = (f32[256,256]{1,0:T(8,128)S(1)}, f32[256,256]{1,0:T(8,128)S(1)}, u32[]{:S(2)}, u32[]{:S(2)}) collective-permute-start(f32[256,256]{1,0:T(8,128)S(1)} %add.86), channel_id=1, source_target_pairs={{0,24},{4,28},{8,16},{12,20},{16,8},{20,12},{24,0},{28,4},{1,25},{... | collective-permute-start | bytes 786440 | tf_op jit(solution)/shard_map/ppermute | solution.py:354
  86.8 21.2 %collective-permute-start.21 = (f32[256,256]{1,0:T(8,128)S(1)}, f32[256,256]{1,0:T(8,128)S(1)}, u32[]{:S(2)}, u32[]{:S(2)}) collective-permute-start(f32[256,256]{1,0:T(8,128)S(1)} %add.87), channel_id=1, source_target_pairs={{0,16},{4,20},{8,24},{12,28},{16,0},{20,4},{24,8},{28,12},{1,17},{... | collective-permute-start | bytes 786440 | tf_op jit(solution)/shard_map/ppermute | solution.py:354
  91.4 16.7 %collective-permute-start.23 = (f32[256,256]{1,0:T(8,128)S(1)}, f32[256,256]{1,0:T(8,128)S(1)}, u32[]{:S(2)}, u32[]{:S(2)}) collective-permute-start(f32[256,256]{1,0:T(8,128)S(1)} %add.88), channel_id=1, source_target_pairs={{0,8},{4,12},{8,0},{12,4},{16,24},{20,28},{24,16},{28,20},{1,9},{5... | collective-permute-start | bytes 786440 | tf_op jit(solution)/shard_map/ppermute | solution.py:354
  111.3 11.4 %collective-permute-start.30 = (f32[256,256]{1,0:T(8,128)}, f32[256,256]{1,0:T(8,128)S(1)}, u32[]{:S(2)}, u32[]{:S(2)}) collective-permute-start(f32[256,256]{1,0:T(8,128)} %solve.1.refs_0_), channel_id=1, source_target_pairs={{0,24},{4,28},{8,16},{12,20},{16,8},{20,12},{24,0},{28,4},{1,25},{... | collective-permute-start | bytes 786440 | tf_op jit(solution)/shard_map/ppermute | solution.py:354
  112.5 23.7 %collective-permute-start.3 = (f32[512,256]{1,0:T(8,128)S(1)}, f32[512,256]{1,0:T(8,128)S(1)}, u32[]{:S(2)}, u32[]{:S(2)}) collective-permute-start(f32[512,256]{1,0:T(8,128)S(1)} %pad_maximum_fusion), channel_id=1, source_target_pairs={{0,1},{1,0},{2,3},{3,2},{4,5},{5,4},{6,7},{7,6},{8,9},{9,8},{10,11... | collective-permute-start | bytes 1572872 | tf_op jit(solution)/shard_map/ppermute | solution.py:354
  112.5 21.6 %collective-permute-start.28 = (f32[256,256]{1,0:T(8,128)}, f32[256,256]{1,0:T(8,128)S(1)}, u32[]{:S(2)}, u32[]{:S(2)}) collective-permute-start(f32[256,256]{1,0:T(8,128)} %solve.1.refs_0_), channel_id=1, source_target_pairs={{0,16},{4,20},{8,24},{12,28},{16,0},{20,4},{24,8},{28,12},{1,17},{... | collective-permute-start | bytes 786440 | tf_op jit(solution)/shard_map/ppermute | solution.py:354
  112.5 23.0 %collective-permute-start.26 = (f32[256,256]{1,0:T(8,128)}, f32[256,256]{1,0:T(8,128)S(1)}, u32[]{:S(2)}, u32[]{:S(2)}) collective-permute-start(f32[256,256]{1,0:T(8,128)} %solve.1.refs_0_), channel_id=1, source_target_pairs={{0,8},{4,12},{8,0},{12,4},{16,24},{20,28},{24,16},{28,20},{1,9},{5... | collective-permute-start | bytes 786440 | tf_op jit(solution)/shard_map/ppermute | solution.py:354
  115.7 20.5 %collective-permute-start.25 = (f32[256,256]{1,0:T(8,128)}, f32[256,256]{1,0:T(8,128)S(1)}, u32[]{:S(2)}, u32[]{:S(2)}) collective-permute-start(f32[256,256]{1,0:T(8,128)} %solve.1.refs_0_), channel_id=1, source_target_pairs={{0,4},{4,0},{8,12},{12,8},{16,20},{20,16},{24,28},{28,24},{1,5},{5... | collective-permute-start | bytes 786440 | tf_op jit(solution)/shard_map/ppermute | solution.py:354
  122.6 13.5 %collective-permute-start.31 = (f32[256,256]{1,0:T(8,128)S(1)}, f32[256,256]{1,0:T(8,128)S(1)}, u32[]{:S(2)}, u32[]{:S(2)}) collective-permute-start(f32[256,256]{1,0:T(8,128)S(1)} %collective-permute-done.30.refs_6_), channel_id=1, source_target_pairs={{0,4},{4,0},{8,12},{12,8},{16,20},{20,16},{24,28},{28,24},{1,5},{5... | collective-permute-start | bytes 786440 | tf_op jit(solution)/shard_map/ppermute | solution.py:354
  134.1 9.2 %collective-permute-start.29 = (f32[256,256]{1,0:T(8,128)S(1)}, f32[256,256]{1,0:T(8,128)S(1)}, u32[]{:S(2)}, u32[]{:S(2)}) collective-permute-start(f32[256,256]{1,0:T(8,128)S(1)} %collective-permute-done.28.refs_4_), channel_id=1, source_target_pairs={{0,4},{4,0},{8,12},{12,8},{16,20},{20,16},{24,28},{28,24},{1,5},{5... | collective-permute-start | bytes 786440 | tf_op jit(solution)/shard_map/ppermute | solution.py:354
  135.5 10.7 %collective-permute-start.27 = (f32[256,256]{1,0:T(8,128)S(1)}, f32[256,256]{1,0:T(8,128)S(1)}, u32[]{:S(2)}, u32[]{:S(2)}) collective-permute-start(f32[256,256]{1,0:T(8,128)S(1)} %collective-permute-done.26.refs_2_), channel_id=1, source_target_pairs={{0,4},{4,0},{8,12},{12,8},{16,20},{20,16},{24,28},{28,24},{1,5},{5... | collective-permute-start | bytes 786440 | tf_op jit(solution)/shard_map/ppermute | solution.py:354
  (12 other events, 73.4 us)

commit v2 on v1

v2 whole, which is shorter than its diff:
```python
import functools

import jax
import jax.numpy as jnp
from jax import lax
from jax.experimental import pallas as pl
from jax.experimental.pallas import tpu as pltpu
from jax.sharding import PartitionSpec as P

F32 = jnp.float32
BF16 = jnp.bfloat16
VMEM = pl.BlockSpec(memory_space=pltpu.VMEM)
SMEM = pl.BlockSpec(memory_space=pltpu.SMEM)
PANEL = 64
HBM = pl.BlockSpec(memory_space=pltpu.HBM)

CORE, MINE, TM = 8, 9, 10


def params(mib):
    return pltpu.CompilerParams(vmem_limit_bytes=mib * 2**20)


def exact(a, b, dims):
    return lax.dot_general(
        a, b, (dims, ((), ())), precision=lax.Precision.HIGHEST, preferred_element_type=F32
    )


def split(x):
    hi = x.astype(BF16)
    return hi, (x - hi.astype(F32)).astype(BF16)


def three(a, b, dims=((1,), (0,))):
    def one(x, y):
        return lax.dot_general(x, y, (dims, ((), ())), preferred_element_type=F32)

    return one(a[0], b[0]) + (one(a[0], b[1]) + one(a[1], b[0]))


def cost(macs, moved):
    return pl.CostEstimate(flops=macs // 8, bytes_accessed=moved // 16, transcendentals=0)


def pick(table, slots, i):
    step = slots[1] - slots[0] if len(slots) > 1 else 0
    return table[slots[0] + step * i]


def shape(*dims, dtype=F32):
    return jax.ShapeDtypeStruct(dims, dtype)


def sketch_kernel(steps, table, field, test, corange, s_send, s_keep, m_send, m_keep, t, om, thi, tlo, total, sems):
    i = pl.program_id(0)
    rank = t.shape[1]
    rows = field.shape[0]
    copies = (pltpu.make_async_copy(test, t, sems.at[0]), pltpu.make_async_copy(corange, om, sems.at[1]))

    @pl.when(i == 0)
    def _():
        for copy in copies:
            copy.start()
        copies[0].wait()
        thi[...], tlo[...] = split(t[...])
        copies[1].wait()
        total[...] = jnp.zeros_like(total)

    s = three(split(field[...]), (thi[...], tlo[...]))
    half = steps // 2
    at = pl.ds(pl.multiple_of((i % half) * rows, 8), rows)

    @pl.when(i < half)
    def _():
        s_send[at, :] = s

    @pl.when(i >= half)
    def _():
        s_keep[at, :] = s

    slot = jnp.where(i == 0, 1, jnp.where(i == 1, 3, jnp.where(i == 2, 2, 0)))
    here = pl.multiple_of((table[TM] ^ slot) * rows, 128)
    total[...] += three(split(om[:, pl.ds(here, rows)]), split(s))

    @pl.when(i == steps - 1)
    def _():
        part = total.shape[0] // 8
        for out, slots in ((m_send, (1, 5, 3, 7)), (m_keep, (0, 4, 2, 6))):
            for j, k in enumerate(slots):
                from_ = pl.multiple_of((table[MINE] ^ k) * part, 8)
                out[j * part:(j + 1) * part, :] = total[pl.ds(from_, part), :]


def sketches(table, field, test, corange):
    cells, times = field.shape
    rank = test.shape[1]
    steps = 4
    rows = cells // steps
    wide = corange.shape[0]

    def block(i, p):
        return (p[TM] ^ jnp.where(i == 0, 1, jnp.where(i == 1, 3, jnp.where(i == 2, 2, 0))), 0)

    return pl.pallas_call(
        functools.partial(sketch_kernel, steps),
        grid_spec=pltpu.PrefetchScalarGridSpec(
            num_scalar_prefetch=1,
            grid=(steps,),
            in_specs=[pl.BlockSpec((rows, times), block), HBM, HBM],
            out_specs=[VMEM] * 4,
            scratch_shapes=[
                pltpu.VMEM((times, rank), F32),
                pltpu.VMEM((wide, cells), F32),
                pltpu.VMEM((times, rank), BF16),
                pltpu.VMEM((times, rank), BF16),
                pltpu.VMEM((wide, rank), F32),
                pltpu.SemaphoreType.DMA((2,)),
            ],
        ),
        out_shape=[shape(cells // 2, rank)] * 2 + [shape(wide // 2, rank)] * 2,
        compiler_params=params(36),
        cost_estimate=cost(3 * cells * rank * (times + wide), 4 * cells * times),
        name="sketches",
    )(table, field, test, corange)


def gram_kernel(table, a, b, s, g_send, g_keep, total):
    x = a[...] + b[...]
    s[...] = x
    total[...] = exact(x, x, ((0,), (0,)))
    rows = total.shape[0] // 2
    me = table[CORE]
    g_keep[...] = total[pl.ds(pl.multiple_of(me * rows, 8), rows), :]
    g_send[...] = total[pl.ds(pl.multiple_of((1 - me) * rows, 8), rows), :]


def gram_of(table, a, b):
    rank = a.shape[1]
    return pl.pallas_call(
        gram_kernel,
        out_shape=[shape(*a.shape), shape(rank // 2, rank), shape(rank // 2, rank)],
        in_specs=[SMEM, VMEM, VMEM],
        out_specs=[VMEM] * 3,
        scratch_shapes=[pltpu.VMEM((rank, rank), F32)],
        cost_estimate=cost(6 * a.shape[0] * rank * rank, 12 * a.shape[0] * rank),
        name="gram",
    )(table, a, b)


ORDER = (0, 4, 2, 6, 1, 5, 3, 7)


def stack_rows(parts):
    return jnp.concatenate([parts[0], parts[1], parts[0]], axis=0)


def rhs_kernel(slots, first, table, *refs):
    count = len(slots)
    i = pl.program_id(0)
    if first:
        near, far, corange, field = refs[:4]
        outs, (p, m, om) = refs[4:-3], refs[-3:]

        @pl.when(i == 0)
        def _():
            half = near.shape[0]
            rows = half // 4
            m[:half] = near[...]
            m[half:] = far[...]
            for j, slot in enumerate(ORDER):
                at = pl.multiple_of((table[MINE] ^ slot) * rows, 8)
                om[j * rows:(j + 1) * rows, :] = corange[pl.ds(at, rows), :]
            cells = om.shape[1]
            p[:, :cells], p[:, 2 * cells:] = split(three(split(m[...].T), split(om[...])))
            p[:, cells:2 * cells] = p[:, :cells]
    else:
        p, field = refs[:2]
        outs = refs[2:]
    x = jnp.dot(p[...], stack_rows(split(field[...])), preferred_element_type=F32)
    for k in range(count):
        @pl.when(i == k)
        def _():
            outs[k][...] = x


def rhs_blocks(table, slots, operands, field, blocks):
    count = len(slots)
    first = len(operands) > 1
    rank = operands[0].shape[1] if first else operands[0].shape[0]
    cells = field.shape[0]
    cols = field.shape[1] // blocks
    wide = operands[2].shape[0] if first else 0
    whole = lambda dims: pl.BlockSpec(dims, lambda i, p: (0, 0))
    return pl.pallas_call(
        functools.partial(rhs_kernel, slots, first),
        grid_spec=pltpu.PrefetchScalarGridSpec(
            num_scalar_prefetch=1,
            grid=(count,),
            in_specs=[whole(x.shape) for x in operands] + [pl.BlockSpec((cells, cols), lambda i, p: (0, pick(p, slots, i)))],
            out_specs=[whole((rank, cols))] * count + [whole((rank, 3 * cells))] * first,
            scratch_shapes=[pltpu.VMEM((wide, rank), F32), pltpu.VMEM((wide, cells), F32)] * first,
        ),
        out_shape=[shape(rank, cols)] * count + [shape(rank, 3 * cells, dtype=BF16)] * first,
        compiler_params=params(32),
        cost_estimate=cost(3 * count * rank * cells * cols, 4 * count * cells * cols),
        name="rhs",
    )(table, *operands, field)


def eliminate(blocks):
    width = blocks[0].shape[1]
    groups = PANEL // 8
    mats = [[x[8 * g:8 * g + 8] for g in range(groups)] for x in blocks]
    row = lax.broadcasted_iota(jnp.int32, (8, width), 0)
    for s in range(groups):
        columns = [
            {
                g: [jnp.broadcast_to(m[g][:, 8 * s + j:8 * s + j + 1], (8, width)) for j in range(8)]
                for g in range(s, groups)
            }
            for m in mats
        ]
        for i in range(8):
            for m, c in zip(mats, columns):
                inverse = 1.0 / c[s][i][i:i + 1]
                below = {g: c[g][i] for g in range(s, groups)}
                below[s] = jnp.where(row > i, below[s], 0.0)
                for j in range(i + 1, 8):
                    f = c[s][j][i:i + 1] * inverse
                    for g in range(s, groups):
                        c[g][j] = c[g][j] - below[g] * f
                u = m[s][i:i + 1] * inverse
                for g in range(s, groups):
                    m[g] = m[g] - below[g] * u
    return mats


def iotas(dims):
    return lax.broadcasted_iota(jnp.int32, dims, 0), lax.broadcasted_iota(jnp.int32, dims, 1)


def factor_both(n, tables):
    r, c = iotas((PANEL, PANEL))
    eye = jnp.where(r == c, 1.0, 0.0)
    r, c = iotas((PANEL, 2 * PANEL))
    for k in range(n // PANEL):
        lo, hi = k * PANEL, (k + 1) * PANEL
        blocks = [jnp.concatenate([t[lo:hi, lo:hi], eye], axis=1) for t in tables]
        left = lo // 128 * 128
        right = n + (hi + 127) // 128 * 128
        rest = hi // 128 * 128
        for t, m in zip(tables, eliminate(blocks)):
            x = jnp.concatenate(m, axis=0)
            pivots = jnp.sum(jnp.where(r == c, x, 0.0), axis=1, keepdims=True)
            inverse = (x * lax.rsqrt(pivots))[:, PANEL:]
            panel = exact(inverse, t[lo:hi, left:right], ((1,), (0,)))
            if hi < n:
                update = exact(panel[:, rest - left:n - left], panel[:, rest - left:], ((0,), (0,)))
                t[hi:n, rest:right] = t[hi:n, rest:right] - update[hi - rest:]
            t[lo:hi, left:right] = panel


def factor_kernel(table, g_near, g_far, m_near, m_far, upper, inverse, normal_inverse, t1, t2):
    n = g_near.shape[1]
    half = n // 2
    r, c = iotas((n, n))
    eye = jnp.where(r == c, 1.0, 0.0)
    me = table[CORE]
    t1[pl.ds(pl.multiple_of(me * half, 8), half), :n] = g_near[...]
    t1[pl.ds(pl.multiple_of((1 - me) * half, 8), half), :n] = g_far[...]
    t1[:, n:] = eye
    t2[:, :n] = exact(m_near[...], m_near[...], ((0,), (0,))) + exact(m_far[...], m_far[...], ((0,), (0,)))
    t2[:, n:] = eye
    factor_both(n, (t1, t2))
    upper[...] = jnp.where(r <= c, t1[:, :n], 0.0)
    inverse[...] = t1[:, n:]
    k = t2[:, n:]
    normal_inverse[...] = exact(k, k, ((0,), (0,)))


def factor(table, g_near, g_far, m_near, m_far):
    n = g_near.shape[1]
    return pl.pallas_call(
        factor_kernel,
        out_shape=[shape(n, n)] * 3,
        in_specs=[SMEM] + [VMEM] * 4,
        out_specs=[VMEM] * 3,
        scratch_shapes=[pltpu.VMEM((n, 2 * n), F32)] * 2,
        compiler_params=params(20),
        cost_estimate=cost(5 * 10**9, 4 * n * n * 8),
        name="factor",
    )(table, g_near, g_far, m_near, m_far)


def solve_kernel(projector, *refs):
    total = refs[0][...]
    for ref in refs[1:-1]:
        total += ref[...]
    refs[-1][...] = three(split(projector[...]), split(total))


def solve(projector, terms):
    return pl.pallas_call(
        solve_kernel,
        out_shape=shape(projector.shape[0], terms[0].shape[1]),
        in_specs=[VMEM] * (len(terms) + 1),
        out_specs=VMEM,
        compiler_params=params(16),
        cost_estimate=cost(3 * projector.shape[0] * terms[0].size, 4 * terms[0].size * (len(terms) + 2)),
        name="solve",
    )(projector, *terms)


def output_kernel(slots, scale, table, *refs):
    count = len(slots)
    first = scale is not None
    i = pl.program_id(0)
    if first:
        s0, s2, s13, upper, inverse, field = refs[:6]
        blocks = refs[6:6 + count]
        left, sparts, uparts, right, residual, z = refs[6 + count:]
        rows, rank = s0.shape

        @pl.when(i == 0)
        def _():
            uparts[:, :rank], uparts[:, 2 * rank:] = split(upper[...])
            uparts[:, rank:2 * rank] = uparts[:, :rank]
            inv = split(inverse[...])
            for slot, ref, start in ((0, s0, 0), (2, s2, 0), (1, s13, 0), (3, s13, rows)):
                at = pl.ds(pl.multiple_of((table[TM] ^ slot) * rows, 16), rows)
                hi, lo = split(ref[start:start + rows, :])
                sparts[at, :rank] = hi
                sparts[at, rank:2 * rank] = hi
                sparts[at, 2 * rank:] = lo
                left[at, :] = three((hi, lo), inv, ((1,), (1,))) * scale
    else:
        sparts, uparts, field = refs[:3]
        blocks = refs[3:3 + count]
        right, residual, z = refs[5 + count:]

    for k in range(count):
        @pl.when(i == k)
        def _():
            z[...] = stack_rows(split(blocks[k][...]))

    right[...] = jnp.dot(uparts[...], z[...], preferred_element_type=F32)
    residual[...] = field[...] - jnp.dot(sparts[...], z[...], preferred_element_type=F32)


def outputs(table, slots, scale, operands, field, blocks, before=()):
    cells, times = field.shape
    rank, cols = blocks[0].shape
    count = len(slots)
    first = scale is not None
    whole = lambda *dims: pl.BlockSpec(dims, lambda i, p: (0,) * len(dims))
    ahead = 1 + len(operands) + 1 + count
    return pl.pallas_call(
        functools.partial(output_kernel, slots, scale),
        grid_spec=pltpu.PrefetchScalarGridSpec(
            num_scalar_prefetch=1,
            grid=(count,),
            in_specs=[whole(*x.shape) for x in operands]
            + [pl.BlockSpec((cells, cols), lambda i, p: (0, pick(p, slots, i)))]
            + [whole(rank, cols)] * count
            + [pl.BlockSpec(memory_space=pl.ANY)] * len(before),
            out_specs=[whole(cells, rank), whole(cells, 3 * rank), whole(rank, 3 * rank)] * first + [
                pl.BlockSpec((rank, cols), lambda i, p: (0, pick(p, slots, i))),
                pl.BlockSpec((cells, cols), lambda i, p: (0, pick(p, slots, i))),
            ],
            scratch_shapes=[pltpu.VMEM((3 * rank, cols), BF16)],
        ),
        out_shape=[shape(cells, rank), shape(cells, 3 * rank, dtype=BF16), shape(rank, 3 * rank, dtype=BF16)] * first
        + [shape(rank, times), shape(cells, times)],
        input_output_aliases={} if first else {ahead: 0, ahead + 1: 1},
        compiler_params=params(36),
        cost_estimate=cost(3 * cells * rank * cols * count, 8 * cells * cols * count),
        name="outputs",
    )(table, *operands, field, *blocks, *before)


def swap(axis, bit):
    n = lax.axis_size(axis)

    def go(x):
        return lax.ppermute(x, axis, [(i, i ^ bit) for i in range(n)])

    return go


def tie(*arrays):
    return lax.optimization_barrier(arrays)


def along_z(v):
    spaces = lax.axis_size("space")
    bit = 2
    if spaces >= 8:
        v = (v + swap("space", 2)(v)) + (swap("space", 4)(v) + swap("space", 6)(v))
        bit = 8
    while bit < spaces:
        v = v + swap("space", bit)(v)
        bit *= 2
    return v


def per_device(field, range_test, corange_test):
    spaces, tms = lax.axis_size("space"), lax.axis_size("tm")
    space, tm = lax.axis_index("space"), lax.axis_index("tm")
    scale = float(field.shape[0] * spaces) ** 0.5
    core, y, x = tm & 1, space & 1, (tm >> 1) & 1
    to_core, to_x = swap("tm", 1), swap("tm", 2)
    to_y = swap("space", 1)

    def to_xy(v):
        pairs = [(s * tms + t, (s ^ 1) * tms + (t ^ 2)) for s in range(spaces) for t in range(tms)]
        return lax.ppermute(v, ("space", "tm"), pairs)


    count = min(spaces, 8)
    near = space & (count - 1)
    mine = core | (y << 1) | (x << 2)
    numbers = jnp.array([core, mine, tm])
    table = jnp.concatenate([near ^ jnp.arange(8, dtype=jnp.int32), numbers]).astype(jnp.int32)

    s_send, s_keep, m_send, m_keep = sketches(table, field, range_test, corange_test)
    quarter = s_keep.shape[0] // 2

    m = m_keep + to_core(m_send)
    got = to_core(s_send)
    s_far, s_near = s_keep[:quarter] + got[quarter:], s_keep[quarter:] + got[:quarter]
    m, s_far, s_near = tie(m, s_far, s_near)
    rows = m.shape[0] // 4
    k0, kx, ky, kxy = (m[i * rows:(i + 1) * rows] for i in range(4))
    s_x = to_x(s_far)
    m = (k0 + to_x(kx)) + (to_y(ky) + to_xy(kxy))
    m, s_x = tie(m, s_x)
    s0, g_send, g = gram_of(table, s_near, s_x)
    g_got = to_core(g_send)
    m = along_z(m)
    m, g, g_got = tie(m, g, g_got)
    g = g + g_got
    g_got = to_x(g)
    m = jnp.concatenate([m, to_x(m), to_y(m), to_xy(m)], axis=0)
    m, g, g_got = tie(m, g, g_got)
    g = g + g_got
    m_far = to_core(m)
    g_got = to_y(g)

    send_slots, keep_slots = list(range(count - 1, 0, -2)), list(range(count - 2, -1, -2))
    cut = (len(send_slots) + 1) // 2
    *sent, p = rhs_blocks(table, send_slots[:cut], (m, m_far, corange_test), field, count)
    p, g, g_got = tie(p, g, g_got)
    g = along_z(g + g_got)
    if send_slots[cut:]:
        sent += rhs_blocks(table, send_slots[cut:], (p,), field, count)
    kept = list(rhs_blocks(table, keep_slots, (p,), field, count))
    terms = []
    for k, slot in enumerate(keep_slots):
        got = to_y(sent[k])
        if slot == 0:
            terms += [kept[k], got]
        else:
            total = kept[k] + got
            if k == 0:
                total, g = tie(total, g)
            terms.append(swap("space", slot)(total))
    bit = count
    while bit < spaces:
        mine_sum = functools.reduce(jnp.add, terms)
        terms = [mine_sum, swap("space", bit)(mine_sum)]
        bit *= 2
    g_far = to_core(g)
    s2 = to_x(s0)
    s13 = to_core(jnp.concatenate([s0, s2], axis=0))

    upper, inverse, inverse_normal = factor(table, g, g_far, m, m_far)
    z0 = solve(inverse_normal, terms)

    blocks = {0: z0, 1: to_y(z0)}
    for slot in range(2, count, 2):
        blocks[slot] = swap("space", slot)(z0)
    for slot in range(2, count, 2):
        blocks[slot + 1] = to_y(blocks[slot])

    left, sparts, uparts, *done = outputs(
        table, [0, 1, 2][:count], scale, (s0, s2, s13, upper, inverse), field, [blocks[k] for k in range(min(3, count))])
    for slots in ([4, 6], [3, 5, 7]):
        if count > slots[-1]:
            done = outputs(table, slots, None, (sparts, uparts), field, [blocks[k] for k in slots], tuple(done))
    return (left, *done)


def solution(mesh):
    return jax.shard_map(
        per_device,
        mesh=mesh,
        in_specs=(P("space", "tm"), P("tm", None), P(None, "space")),
        out_specs=(P("space", None), P(None, "tm"), P("space", "tm")),
        check_vma=False,
    )
```

time: 160 us -> 143 us (0.89)
  waiting for transfers between devices: 55.4 us -> 41 us
  Pallas kernels: 54.4 us -> 45.5 us
  starting transfers between devices: 39.7 us -> 43.3 us
  local copies, waits for them, and re-layouts: 6.45 us -> 9.98 us
    ppermute x32 -> x34, waiting for transfers between devices: 55.4 us -> 35.4 us  [go(): return lax.ppermute(x, axis, [(i, i ^ bit) for i in range(n)])]
    ppermute x0 -> x2, waiting for transfers between devices: none -> 5.53 us  [to_xy(): return lax.ppermute(v, ('space', 'tm'), pairs)]
    pallas_call x1, Pallas kernels: 13 us -> 8.43 us  [sketches(): pl.pallas_call(functools.partial(sketch_kernel, steps), grid_spec=pltpu.P...]
    pallas_call x6 -> x8, Pallas kernels: 39.2 us -> 34.9 us  [the longest x1 13.3 us: factor(): pl.pallas_call(factor_kernel, out_shape=[shape(n, n)] * 3, in_specs=[SMEM...]
    unnamed x24 -> x22, local copies, waits for them, and re-layouts: 6.34 us -> 9.97 us
    ppermute x32 -> x34, starting transfers between devices: 39.7 us -> 42.4 us  [go(): return lax.ppermute(x, axis, [(i, i ^ bit) for i in range(n)])]
  transfers between devices with their start and end apart: 32 -> 36, of which waited for: 16 -> 16; matrix products, arithmetic and copies ran while one was open for 1% -> 1% of each run, Pallas kernels for 17% -> 23%
where the time goes in v2:
time: 143 us
  Pallas kernels  45.5 us (32%)
  starting transfers between devices  43.3 us (30%)
  waiting for transfers between devices  41 us (29%)
  local copies, waits for them, and re-layouts  9.98 us (7%)
  other arithmetic  2.07 us (1%)
    ppermute x34, starting transfers between devices, go(): return lax.ppermute(x, axis, [(i, i ^ bit) for i in range(n)])  42.4 us
    ppermute x34, waiting for transfers between devices, go(): return lax.ppermute(x, axis, [(i, i ^ bit) for i in range(n)])  35.4 us
    pallas_call x1, Pallas kernels, factor(): pl.pallas_call(factor_kernel, out_shape=[shape(n, n)] * 3, in_specs=[SMEM...  13.3 us
    pallas_call x3, Pallas kernels, outputs(): pl.pallas_call(functools.partial(output_kernel, slots, scale), grid_spec=...  12.6 us
    unnamed x22, local copies, waits for them, and re-layouts  9.97 us
    pallas_call x3, Pallas kernels, rhs_blocks(): pl.pallas_call(functools.partial(rhs_kernel, slots, first), grid_spec=plt...  8.7 us
    pallas_call x1, Pallas kernels, sketches(): pl.pallas_call(functools.partial(sketch_kernel, steps), grid_spec=pltpu.P...  8.43 us
    ppermute x2, waiting for transfers between devices, to_xy(): return lax.ppermute(v, ('space', 'tm'), pairs)  5.53 us
  transfers between devices with their start and end apart: 36, of which 16 were waited for; matrix products, arithmetic and copies ran while one was open for 1% of the time, Pallas kernels for 23%

profile of v2, /device:TPU:0, one launch (start us, length us, event | category | flops | bytes accessed | tf_op | source)
XLA Modules:
  0.0 142.8 jit_solution(4645184426399813008)
XLA Ops:
  0.7 3.4 %copy-done = f32[1024,2048]{1,0:T(8,128)S(1)} copy-done((f32[1024,2048]{1,0:T(8,128)S(1)}, f32[1024,2048]{1,0:T(8,128)}, u32[]{:S(2)}) %copy-start) | copy-done | bytes 8388632
  4.1 1.6 %copy-done.2 = f32[512,1024]{1,0:T(8,128)S(1)} copy-done((f32[512,1024]{1,0:T(8,128)S(1)}, f32[512,1024]{1,0:T(8,128)}, u32[]{:S(2)}) %copy-start.2) | copy-done | bytes 2097176
  5.7 1.6 %copy-done.4 = f32[2048,256]{1,0:T(8,128)S(1)} copy-done((f32[2048,256]{1,0:T(8,128)S(1)}, f32[2048,256]{1,0:T(8,128)}, u32[]{:S(2)}) %copy-start.4) | copy-done | bytes 2097176
  7.3 8.4 %sketches.1 = (f32[512,256]{1,0:T(8,128)S(1)}, f32[512,256]{1,0:T(8,128)S(1)}, f32[256,256]{1,0:T(8,128)S(1)}, f32[256,256]{1,0:T(8,128)S(1)}) custom-call(s32[11]{0:T(128)S(1)} %pad_add_fusion.table, f32[1024,2048]{1,0:T(8,128)S(1)} %copy-done, f32[2048,256]{1,0:T(8,128)S(1)} %copy-done.4, f32[512,1024]{1,0:T(8,128)S(1)} %copy-done.2), custom_call_target="tpu_custom_call" | custom-call | flops 251658240 | bytes 524288 | tf_op jit(solution)/shard_map/sketches/pallas_call | solution.py:105
  16.4 1.8 %collective-permute-done = f32[256,256]{1,0:T(8,128)S(1)} collective-permute-done((f32[256,256]{1,0:T(8,128)S(1)}, f32[256,256]{1,0:T(8,128)S(1)}, u32[]{:S(2)}, u32[]{:S(2)}) %collective-permute-start) | collective-permute-done | bytes 262176 | tf_op jit(solution)/shard_map/ppermute | solution.py:386
  19.0 2.9 %collective-permute-start.2 = (f32[64,256]{1,0:T(8,128)S(1)}, f32[64,256]{1,0:T(8,128)S(1)}, u32[]{:S(2)}, u32[]{:S(2)}) collective-permute-start(f32[64,256]{1,0:T(8,128)S(1)} %get-tuple-element.93), channel_id=1, source_target_pairs={{0,2},{1,3},{2,0},{3,1},{4,6},{5,7},{6,4},{7,5},{8,10},{9,11},{10,... | collective-permute-start | bytes 196616 | tf_op jit(solution)/shard_map/ppermute | solution.py:386
  22.0 1.5 %collective-permute-start.3 = (f32[64,256]{1,0:T(8,128)S(1)}, f32[64,256]{1,0:T(8,128)S(1)}, u32[]{:S(2)}, u32[]{:S(2)}) collective-permute-start(f32[64,256]{1,0:T(8,128)S(1)} %get-tuple-element.95), channel_id=1, source_target_pairs={{0,4},{4,0},{8,12},{12,8},{16,20},{20,16},{24,28},{28,24},{1,5},{5... | collective-permute-start | bytes 196616 | tf_op jit(solution)/shard_map/ppermute | solution.py:386
  23.5 1.9 %collective-permute-start.5 = (f32[256,256]{1,0:T(8,128)S(1)}, f32[256,256]{1,0:T(8,128)S(1)}, u32[]{:S(2)}, u32[]{:S(2)}) collective-permute-start(f32[256,256]{1,0:T(8,128)S(1)} %get-tuple-element.53), channel_id=1, source_target_pairs={{0,2},{1,3},{2,0},{3,1},{4,6},{5,7},{6,4},{7,5},{8,10},{9,11},{10,... | collective-permute-start | bytes 786440 | tf_op jit(solution)/shard_map/ppermute | solution.py:386
  26.2 3.2 %collective-permute-done.4 = f32[64,256]{1,0:T(8,128)S(1)} collective-permute-done((f32[64,256]{1,0:T(8,128)S(1)}, f32[64,256]{1,0:T(8,128)S(1)}, u32[]{:S(2)}, u32[]{:S(2)}) %collective-permute-start.4) | collective-permute-done | bytes 65568 | tf_op jit(solution)/shard_map/ppermute | solution.py:417
  29.4 3.2 %collective-permute-done.5.b = f32[256,256]{1,0:T(8,128)S(1)} collective-permute-done((f32[256,256]{1,0:T(8,128)S(1)}, f32[256,256]{1,0:T(8,128)S(1)}, u32[]{:S(2)}, u32[]{:S(2)}) %collective-permute-start.5) | collective-permute-done | bytes 262176 | tf_op jit(solution)/shard_map/ppermute | solution.py:386
  32.6 3.6 %collective-permute-start.10 = (f32[64,256]{1,0:T(8,128)S(1)}, f32[64,256]{1,0:T(8,128)S(1)}, u32[]{:S(2)}, u32[]{:S(2)}) collective-permute-start(f32[64,256]{1,0:T(8,128)S(1)} %add_add_fusion.2), channel_id=1, source_target_pairs={{0,24},{4,28},{8,16},{12,20},{16,8},{20,12},{24,0},{28,4},{1,25},{... | collective-permute-start | bytes 196616 | tf_op jit(solution)/shard_map/ppermute | solution.py:386
  37.0 2.2 %gram.1 = (f32[256,256]{1,0:T(8,128)}, f32[128,256]{1,0:T(8,128)}, f32[128,256]{1,0:T(8,128)}) custom-call(s32[11]{0:T(128)} %copy-done.6, f32[256,256]{1,0:T(8,128)} %get-tuple-element.51.a, f32[256,256]{1,0:T(8,128)} %copy-done.8), custom_call_target="tpu_custom_call" | custom-call | flops 12582912 | bytes 49152 | tf_op jit(solution)/shard_map/gram/pallas_call | solution.py:140
  42.5 1.5 %collective-permute-start.13 = (f32[64,256]{1,0:T(8,128)S(1)}, f32[64,256]{1,0:T(8,128)S(1)}, u32[]{:S(2)}, u32[]{:S(2)}) collective-permute-start(f32[64,256]{1,0:T(8,128)S(1)} %add_add_fusion.1), channel_id=1, source_target_pairs={{0,4},{4,0},{8,12},{12,8},{16,20},{20,16},{24,28},{28,24},{1,5},{5... | collective-permute-start | bytes 196616 | tf_op jit(solution)/shard_map/ppermute | solution.py:386
  47.5 2.4 %collective-permute-done.14 = f32[64,256]{1,0:T(8,128)S(1)} collective-permute-done((f32[64,256]{1,0:T(8,128)S(1)}, f32[64,256]{1,0:T(8,128)S(1)}, u32[]{:S(2)}, u32[]{:S(2)}) %collective-permute-start.14) | collective-permute-done | bytes 65568 | tf_op jit(solution)/shard_map/ppermute | solution.py:417
  50.9 1.6 %collective-permute-start.17 = (f32[128,256]{1,0:T(8,128)S(1)}, f32[128,256]{1,0:T(8,128)S(1)}, u32[]{:S(2)}, u32[]{:S(2)}) collective-permute-start(f32[128,256]{1,0:T(8,128)S(1)} %add.64), channel_id=1, source_target_pairs={{0,4},{4,0},{8,12},{12,8},{16,20},{20,16},{24,28},{28,24},{1,5},{5... | collective-permute-start | bytes 393224 | tf_op jit(solution)/shard_map/ppermute | solution.py:386
  52.6 3.4 %copy-done.1 = f32[1024,2048]{1,0:T(8,128)S(1)} copy-done((f32[1024,2048]{1,0:T(8,128)S(1)}, f32[1024,2048]{1,0:T(8,128)}, u32[]{:S(2)}) %copy-start.1) | copy-done | bytes 8388632
  55.9 3.0 %rhs.3 = (f32[256,256]{1,0:T(8,128)S(1)}, f32[256,256]{1,0:T(8,128)S(1)}, bf16[256,3072]{1,0:T(8,128)(2,1)S(1)}) custom-call(s32[11]{0:T(128)S(1)} %copy-done.7, f32[256,256]{1,0:T(8,128)S(1)} %pad_maximum_fusion.1.refs_0_.m_near, f32[256,256]{1,0:T(8,128)S(1)} %collective-permute-done.16.refs_1_.m_far, f32[512,1024]{1,0:T(8,128)S(1)} %copy-done.3, ...), custom_call_target="tpu_custom_call" | custom-call | flops 50331648 | bytes 131072 | tf_op jit(solution)/shard_map/rhs/pallas_call | solution.py:195
  59.0 2.1 %collective-permute-start.19 = (f32[128,256]{1,0:T(8,128)S(1)}, f32[128,256]{1,0:T(8,128)S(1)}, u32[]{:S(2)}, u32[]{:S(2)}) collective-permute-start(f32[128,256]{1,0:T(8,128)S(1)} %add.66), channel_id=1, source_target_pairs={{0,8},{4,12},{8,0},{12,4},{16,24},{20,28},{24,16},{28,20},{1,9},{5... | collective-permute-start | bytes 393224 | tf_op jit(solution)/shard_map/ppermute | solution.py:386
  61.1 1.8 %collective-permute-start.20 = (f32[128,256]{1,0:T(8,128)S(1)}, f32[128,256]{1,0:T(8,128)S(1)}, u32[]{:S(2)}, u32[]{:S(2)}) collective-permute-start(f32[128,256]{1,0:T(8,128)S(1)} %add.66), channel_id=1, source_target_pairs={{0,16},{4,20},{8,24},{12,28},{16,0},{20,4},{24,8},{28,12},{1,17},{... | collective-permute-start | bytes 393224 | tf_op jit(solution)/shard_map/ppermute | solution.py:386
  63.6 2.0 %rhs.5 = (f32[256,256]{1,0:T(8,128)S(1)}, f32[256,256]{1,0:T(8,128)S(1)}) custom-call(s32[11]{0:T(128)S(1)} %copy-done.7, bf16[256,3072]{1,0:T(8,128)(2,1)S(1)} %get-tuple-element.66.refs_0_, f32[1024,2048]{1,0:T(8,128)S(1)} %copy-done.1), custom_call_target="tpu_custom_call" | custom-call | flops 50331648 | bytes 131072 | tf_op jit(solution)/shard_map/rhs/pallas_call | solution.py:195
  69.1 3.7 %rhs.4 = (f32[256,256]{1,0:T(8,128)S(1)}, f32[256,256]{1,0:T(8,128)S(1)}, f32[256,256]{1,0:T(8,128)S(1)}, f32[256,256]{1,0:T(8,128)S(1)}) custom-call(s32[11]{0:T(128)S(1)} %copy-done.7, bf16[256,3072]{1,0:T(8,128)(2,1)S(1)} %get-tuple-element.66.refs_0_, f32[1024,2048]{1,0:T(8,128)S(1)} %copy-done.1), custom_call_target="tpu_custom_call" | custom-call | flops 100663296 | bytes 262144 | tf_op jit(solution)/shard_map/rhs/pallas_call | solution.py:195
  77.9 2.6 %collective-permute-done.24 = f32[256,256]{1,0:T(8,128)S(1)} collective-permute-done((f32[256,256]{1,0:T(8,128)S(1)}, f32[256,256]{1,0:T(8,128)S(1)}, u32[]{:S(2)}, u32[]{:S(2)}) %collective-permute-start.24) | collective-permute-done | bytes 262176 | tf_op jit(solution)/shard_map/ppermute | solution.py:386
  81.5 4.6 %collective-permute-done.18 = f32[256,256]{1,0:T(8,128)S(1)} collective-permute-done((f32[256,256]{1,0:T(8,128)S(1)}, f32[256,256]{1,0:T(8,128)S(1)}, u32[]{:S(2)}, u32[]{:S(2)}) %collective-permute-start.18) | collective-permute-done | bytes 262176 | tf_op jit(solution)/shard_map/ppermute | solution.py:386
  86.1 3.3 %collective-permute-start.23 = (f32[256,256]{1,0:T(8,128)S(1)}, f32[256,256]{1,0:T(8,128)S(1)}, u32[]{:S(2)}, u32[]{:S(2)}) collective-permute-start(f32[256,256]{1,0:T(8,128)S(1)} %add.65), channel_id=1, source_target_pairs={{0,24},{4,28},{8,16},{12,20},{16,8},{20,12},{24,0},{28,4},{1,25},{... | collective-permute-start | bytes 786440 | tf_op jit(solution)/shard_map/ppermute | solution.py:386
  90.9 13.3 %factor.1 = (f32[256,256]{1,0:T(8,128)S(1)}, f32[256,256]{1,0:T(8,128)S(1)}, f32[256,256]{1,0:T(8,128)S(1)}) custom-call(s32[11]{0:T(128)S(1)} %copy-done.7, f32[128,256]{1,0:T(8,128)S(1)} %add_add_fusion.g_near, f32[128,256]{1,0:T(8,128)S(1)} %collective-permute-done.22.g_far, f32[256,256]{1,0:T(8,128)S(1)} %pad_maximum_fusion.1.refs_0_.m_near, ...), custom_call_target="tpu_custom_call" | custom-call | flops 625000000 | bytes 131072 | tf_op jit(solution)/shard_map/factor/pallas_call | solution.py:284
  106.1 2.9 %collective-permute-start.34 = (f32[256,256]{1,0:T(8,128)S(1)}, f32[256,256]{1,0:T(8,128)S(1)}, u32[]{:S(2)}, u32[]{:S(2)}) collective-permute-start(f32[256,256]{1,0:T(8,128)S(1)} %solve.1.refs_6_), channel_id=1, source_target_pairs={{0,24},{4,28},{8,16},{12,20},{16,8},{20,12},{24,0},{28,4},{1,25},{... | collective-permute-start | bytes 786440 | tf_op jit(solution)/shard_map/ppermute | solution.py:386
  110.5 7.6 %collective-permute-done.30.refs_8_ = f32[256,256]{1,0:T(8,128)S(1)} collective-permute-done((f32[256,256]{1,0:T(8,128)S(1)}, f32[256,256]{1,0:T(8,128)S(1)}, u32[]{:S(2)}, u32[]{:S(2)}) %collective-permute-start.30) | collective-permute-done | bytes 262176 | tf_op jit(solution)/shard_map/ppermute | solution.py:386
  119.5 6.8 %collective-permute-done.32.refs_3_ = f32[256,256]{1,0:T(8,128)S(1)} collective-permute-done((f32[256,256]{1,0:T(8,128)S(1)}, f32[256,256]{1,0:T(8,128)S(1)}, u32[]{:S(2)}, u32[]{:S(2)}) %collective-permute-start.32) | collective-permute-done | bytes 262176 | tf_op jit(solution)/shard_map/ppermute | solution.py:386
  128.4 5.3 %outputs.3 = (f32[1024,256]{1,0:T(8,128)}, bf16[1024,768]{1,0:T(8,128)(2,1)S(1)}, bf16[256,768]{1,0:T(8,128)(2,1)S(1)}, f32[256,2048]{1,0:T(8,128)}, f32[1024,2048]{1,0:T(8,128)}) custom-call(s32[11]{0:T(128)S(1)} %copy-done.7, f32[256,256]{1,0:T(8,128)S(1)} %copy-done.5, f32[256,256]{1,0:T(8,128)S(1)} %collective-permute-done.6.refs_1_, ...), custom_call_target="tpu_custom_call" | custom-call | flops 75497472 | bytes 393216 | tf_op jit(solution)/shard_map/outputs/pallas_call | solution.py:358
  133.6 3.2 %outputs.4 = (f32[256,2048]{1,0:T(8,128)}, f32[1024,2048]{1,0:T(8,128)}) custom-call(s32[11]{0:T(128)S(1)} %copy-done.7, bf16[1024,768]{1,0:T(8,128)(2,1)S(1)} %get-tuple-element.83.refs_0_, bf16[256,768]{1,0:T(8,128)(2,1)S(1)} %get-tuple-element.84.refs_1_, f32[1024,2048]{1,0:T(8,128)S(1)} %bitcast.4, ...), custom_call_target="tpu_custom_call", output_to_operand_aliasing={{0}: (6, {}), {1}: (7, {})} | custom-call | flops 50331648 | bytes 262144 | tf_op jit(solution)/shard_map/outputs/pallas_call | solution.py:358
  136.8 1.8 %collective-permute-done.35.refs_5_ = f32[256,256]{1,0:T(8,128)S(1)} collective-permute-done((f32[256,256]{1,0:T(8,128)S(1)}, f32[256,256]{1,0:T(8,128)S(1)}, u32[]{:S(2)}, u32[]{:S(2)}) %collective-permute-start.35) | collective-permute-done | bytes 262176 | tf_op jit(solution)/shard_map/ppermute | solution.py:386
  138.7 4.1 %outputs.5 = (f32[256,2048]{1,0:T(8,128)}, f32[1024,2048]{1,0:T(8,128)}) custom-call(s32[11]{0:T(128)S(1)} %copy-done.7, bf16[1024,768]{1,0:T(8,128)(2,1)S(1)} %get-tuple-element.83.refs_0_, bf16[256,768]{1,0:T(8,128)(2,1)S(1)} %get-tuple-element.84.refs_1_, f32[1024,2048]{1,0:T(8,128)S(1)} %bitcast.4, ...), custom_call_target="tpu_custom_call", output_to_operand_aliasing={{0}: (7, {}), {1}: (8, {})} | custom-call | flops 75497472 | bytes 393216 | tf_op jit(solution)/shard_map/outputs/pallas_call | solution.py:358
  (89 shorter events, 29.6 us)
Async XLA Ops:
  15.8 2.5 %collective-permute-start.1 = (f32[512,256]{1,0:T(8,128)S(1)}, f32[512,256]{1,0:T(8,128)S(1)}, u32[]{:S(2)}, u32[]{:S(2)}) collective-permute-start(f32[512,256]{1,0:T(8,128)S(1)} %get-tuple-element.50), channel_id=1, source_target_pairs={{0,1},{1,0},{2,3},{3,2},{4,5},{5,4},{6,7},{7,6},{8,9},{9,8},{10,11... | collective-permute-start | bytes 1572872 | tf_op jit(solution)/shard_map/ppermute | solution.py:386
  19.0 6.4 %collective-permute-start.2 = (f32[64,256]{1,0:T(8,128)S(1)}, f32[64,256]{1,0:T(8,128)S(1)}, u32[]{:S(2)}, u32[]{:S(2)}) collective-permute-start(f32[64,256]{1,0:T(8,128)S(1)} %get-tuple-element.93), channel_id=1, source_target_pairs={{0,2},{1,3},{2,0},{3,1},{4,6},{5,7},{6,4},{7,5},{8,10},{9,11},{10,... | collective-permute-start | bytes 196616 | tf_op jit(solution)/shard_map/ppermute | solution.py:386
  22.0 4.3 %collective-permute-start.3 = (f32[64,256]{1,0:T(8,128)S(1)}, f32[64,256]{1,0:T(8,128)S(1)}, u32[]{:S(2)}, u32[]{:S(2)}) collective-permute-start(f32[64,256]{1,0:T(8,128)S(1)} %get-tuple-element.95), channel_id=1, source_target_pairs={{0,4},{4,0},{8,12},{12,8},{16,20},{20,16},{24,28},{28,24},{1,5},{5... | collective-permute-start | bytes 196616 | tf_op jit(solution)/shard_map/ppermute | solution.py:386
  23.5 5.9 %collective-permute-start.4 = (f32[64,256]{1,0:T(8,128)S(1)}, f32[64,256]{1,0:T(8,128)S(1)}, u32[]{:S(2)}, u32[]{:S(2)}) collective-permute-start(f32[64,256]{1,0:T(8,128)S(1)} %get-tuple-element.94), channel_id=1, source_target_pairs={{0,6},{1,7},{2,4},{3,5},{4,2},{5,3},{6,0},{7,1},{8,14},{9,15},{10,... | collective-permute-start | bytes 196616 | tf_op jit(solution)/shard_map/ppermute | solution.py:417
  23.5 9.1 %collective-permute-start.5 = (f32[256,256]{1,0:T(8,128)S(1)}, f32[256,256]{1,0:T(8,128)S(1)}, u32[]{:S(2)}, u32[]{:S(2)}) collective-permute-start(f32[256,256]{1,0:T(8,128)S(1)} %get-tuple-element.53), channel_id=1, source_target_pairs={{0,2},{1,3},{2,0},{3,1},{4,6},{5,7},{6,4},{7,5},{8,10},{9,11},{10,... | collective-permute-start | bytes 786440 | tf_op jit(solution)/shard_map/ppermute | solution.py:386
  32.6 6.6 %collective-permute-start.10 = (f32[64,256]{1,0:T(8,128)S(1)}, f32[64,256]{1,0:T(8,128)S(1)}, u32[]{:S(2)}, u32[]{:S(2)}) collective-permute-start(f32[64,256]{1,0:T(8,128)S(1)} %add_add_fusion.2), channel_id=1, source_target_pairs={{0,24},{4,28},{8,16},{12,20},{16,8},{20,12},{24,0},{28,4},{1,25},{... | collective-permute-start | bytes 196616 | tf_op jit(solution)/shard_map/ppermute | solution.py:386
  36.2 4.3 %collective-permute-start.8 = (f32[64,256]{1,0:T(8,128)S(1)}, f32[64,256]{1,0:T(8,128)S(1)}, u32[]{:S(2)}, u32[]{:S(2)}) collective-permute-start(f32[64,256]{1,0:T(8,128)S(1)} %add_add_fusion.2), channel_id=1, source_target_pairs={{0,8},{4,12},{8,0},{12,4},{16,24},{20,28},{24,16},{28,20},{1,9},{5... | collective-permute-start | bytes 196616 | tf_op jit(solution)/shard_map/ppermute | solution.py:386
  36.2 5.2 %collective-permute-start.9 = (f32[64,256]{1,0:T(8,128)S(1)}, f32[64,256]{1,0:T(8,128)S(1)}, u32[]{:S(2)}, u32[]{:S(2)}) collective-permute-start(f32[64,256]{1,0:T(8,128)S(1)} %add_add_fusion.2), channel_id=1, source_target_pairs={{0,16},{4,20},{8,24},{12,28},{16,0},{20,4},{24,8},{28,12},{1,17},{... | collective-permute-start | bytes 196616 | tf_op jit(solution)/shard_map/ppermute | solution.py:386
  41.4 5.6 %collective-permute-start.12 = (f32[64,256]{1,0:T(8,128)S(1)}, f32[64,256]{1,0:T(8,128)S(1)}, u32[]{:S(2)}, u32[]{:S(2)}) collective-permute-start(f32[64,256]{1,0:T(8,128)S(1)} %add_add_fusion.1), channel_id=1, source_target_pairs={{0,2},{1,3},{2,0},{3,1},{4,6},{5,7},{6,4},{7,5},{8,10},{9,11},{10,... | collective-permute-start | bytes 196616 | tf_op jit(solution)/shard_map/ppermute | solution.py:386
  42.5 5.0 %collective-permute-start.13 = (f32[64,256]{1,0:T(8,128)S(1)}, f32[64,256]{1,0:T(8,128)S(1)}, u32[]{:S(2)}, u32[]{:S(2)}) collective-permute-start(f32[64,256]{1,0:T(8,128)S(1)} %add_add_fusion.1), channel_id=1, source_target_pairs={{0,4},{4,0},{8,12},{12,8},{16,20},{20,16},{24,28},{28,24},{1,5},{5... | collective-permute-start | bytes 196616 | tf_op jit(solution)/shard_map/ppermute | solution.py:386
  44.1 5.8 %collective-permute-start.14 = (f32[64,256]{1,0:T(8,128)S(1)}, f32[64,256]{1,0:T(8,128)S(1)}, u32[]{:S(2)}, u32[]{:S(2)}) collective-permute-start(f32[64,256]{1,0:T(8,128)S(1)} %add_add_fusion.1), channel_id=1, source_target_pairs={{0,6},{1,7},{2,4},{3,5},{4,2},{5,3},{6,0},{7,1},{8,14},{9,15},{10,... | collective-permute-start | bytes 196616 | tf_op jit(solution)/shard_map/ppermute | solution.py:417
  45.9 5.0 %collective-permute-start.15 = (f32[128,256]{1,0:T(8,128)S(1)}, f32[128,256]{1,0:T(8,128)S(1)}, u32[]{:S(2)}, u32[]{:S(2)}) collective-permute-start(f32[128,256]{1,0:T(8,128)S(1)} %add.63), channel_id=1, source_target_pairs={{0,2},{1,3},{2,0},{3,1},{4,6},{5,7},{6,4},{7,5},{8,10},{9,11},{10,... | collective-permute-start | bytes 393224 | tf_op jit(solution)/shard_map/ppermute | solution.py:386
  50.9 8.0 %collective-permute-start.17 = (f32[128,256]{1,0:T(8,128)S(1)}, f32[128,256]{1,0:T(8,128)S(1)}, u32[]{:S(2)}, u32[]{:S(2)}) collective-permute-start(f32[128,256]{1,0:T(8,128)S(1)} %add.64), channel_id=1, source_target_pairs={{0,4},{4,0},{8,12},{12,8},{16,20},{20,16},{24,28},{28,24},{1,5},{5... | collective-permute-start | bytes 393224 | tf_op jit(solution)/shard_map/ppermute | solution.py:386
  59.0 8.6 %collective-permute-start.19 = (f32[128,256]{1,0:T(8,128)S(1)}, f32[128,256]{1,0:T(8,128)S(1)}, u32[]{:S(2)}, u32[]{:S(2)}) collective-permute-start(f32[128,256]{1,0:T(8,128)S(1)} %add.66), channel_id=1, source_target_pairs={{0,8},{4,12},{8,0},{12,4},{16,24},{20,28},{24,16},{28,20},{1,9},{5... | collective-permute-start | bytes 393224 | tf_op jit(solution)/shard_map/ppermute | solution.py:386
  61.1 12.9 %collective-permute-start.20 = (f32[128,256]{1,0:T(8,128)S(1)}, f32[128,256]{1,0:T(8,128)S(1)}, u32[]{:S(2)}, u32[]{:S(2)}) collective-permute-start(f32[128,256]{1,0:T(8,128)S(1)} %add.66), channel_id=1, source_target_pairs={{0,16},{4,20},{8,24},{12,28},{16,0},{20,4},{24,8},{28,12},{1,17},{... | collective-permute-start | bytes 393224 | tf_op jit(solution)/shard_map/ppermute | solution.py:386
  63.0 12.1 %collective-permute-start.21 = (f32[128,256]{1,0:T(8,128)S(1)}, f32[128,256]{1,0:T(8,128)S(1)}, u32[]{:S(2)}, u32[]{:S(2)}) collective-permute-start(f32[128,256]{1,0:T(8,128)S(1)} %add.66), channel_id=1, source_target_pairs={{0,24},{4,28},{8,16},{12,20},{16,8},{20,12},{24,0},{28,4},{1,25},{... | collective-permute-start | bytes 393224 | tf_op jit(solution)/shard_map/ppermute | solution.py:386
  65.6 11.0 %collective-permute-start.26 = (f32[256,256]{1,0:T(8,128)S(1)}, f32[256,256]{1,0:T(8,128)S(1)}, u32[]{:S(2)}, u32[]{:S(2)}) collective-permute-start(f32[256,256]{1,0:T(8,128)S(1)} %get-tuple-element.79), channel_id=1, source_target_pairs={{0,4},{4,0},{8,12},{12,8},{16,20},{20,16},{24,28},{28,24},{1,5},{5... | collective-permute-start | bytes 786440 | tf_op jit(solution)/shard_map/ppermute | solution.py:386
  67.1 13.4 %collective-permute-start.24 = (f32[256,256]{1,0:T(8,128)S(1)}, f32[256,256]{1,0:T(8,128)S(1)}, u32[]{:S(2)}, u32[]{:S(2)}) collective-permute-start(f32[256,256]{1,0:T(8,128)S(1)} %get-tuple-element.77), channel_id=1, source_target_pairs={{0,4},{4,0},{8,12},{12,8},{16,20},{20,16},{24,28},{28,24},{1,5},{5... | collective-permute-start | bytes 786440 | tf_op jit(solution)/shard_map/ppermute | solution.py:386
  67.7 18.4 %collective-permute-start.18 = (f32[256,256]{1,0:T(8,128)S(1)}, f32[256,256]{1,0:T(8,128)S(1)}, u32[]{:S(2)}, u32[]{:S(2)}) collective-permute-start(f32[256,256]{1,0:T(8,128)S(1)} %get-tuple-element.68), channel_id=1, source_target_pairs={{0,4},{4,0},{8,12},{12,8},{16,20},{20,16},{24,28},{28,24},{1,5},{5... | collective-permute-start | bytes 786440 | tf_op jit(solution)/shard_map/ppermute | solution.py:386
  74.0 15.4 %collective-permute-start.6 = (f32[256,256]{1,0:T(8,128)S(1)}, f32[256,256]{1,0:T(8,128)S(1)}, u32[]{:S(2)}, u32[]{:S(2)}) collective-permute-start(f32[256,256]{1,0:T(8,128)S(1)} %copy-done.5), channel_id=1, source_target_pairs={{0,2},{1,3},{2,0},{3,1},{4,6},{5,7},{6,4},{7,5},{8,10},{9,11},{10,... | collective-permute-start | bytes 786440 | tf_op jit(solution)/shard_map/ppermute | solution.py:386
  75.1 29.2 %collective-permute-start.28 = (f32[256,256]{1,0:T(8,128)S(1)}, f32[256,256]{1,0:T(8,128)S(1)}, u32[]{:S(2)}, u32[]{:S(2)}) collective-permute-start(f32[256,256]{1,0:T(8,128)S(1)} %get-tuple-element.81), channel_id=1, source_target_pairs={{0,4},{4,0},{8,12},{12,8},{16,20},{20,16},{24,28},{28,24},{1,5},{5... | collective-permute-start | bytes 786440 | tf_op jit(solution)/shard_map/ppermute | solution.py:386
  76.6 27.7 %collective-permute-start.27 = (f32[256,256]{1,0:T(8,128)S(1)}, f32[256,256]{1,0:T(8,128)S(1)}, u32[]{:S(2)}, u32[]{:S(2)}) collective-permute-start(f32[256,256]{1,0:T(8,128)S(1)} %add.71), channel_id=1, source_target_pairs={{0,8},{4,12},{8,0},{12,4},{16,24},{20,28},{24,16},{28,20},{1,9},{5... | collective-permute-start | bytes 786440 | tf_op jit(solution)/shard_map/ppermute | solution.py:386
  80.5 23.8 %collective-permute-start.25 = (f32[256,256]{1,0:T(8,128)S(1)}, f32[256,256]{1,0:T(8,128)S(1)}, u32[]{:S(2)}, u32[]{:S(2)}) collective-permute-start(f32[256,256]{1,0:T(8,128)S(1)} %add.70), channel_id=1, source_target_pairs={{0,16},{4,20},{8,24},{12,28},{16,0},{20,4},{24,8},{28,12},{1,17},{... | collective-permute-start | bytes 786440 | tf_op jit(solution)/shard_map/ppermute | solution.py:386
  86.1 18.2 %collective-permute-start.23 = (f32[256,256]{1,0:T(8,128)S(1)}, f32[256,256]{1,0:T(8,128)S(1)}, u32[]{:S(2)}, u32[]{:S(2)}) collective-permute-start(f32[256,256]{1,0:T(8,128)S(1)} %add.65), channel_id=1, source_target_pairs={{0,24},{4,28},{8,16},{12,20},{16,8},{20,12},{24,0},{28,4},{1,25},{... | collective-permute-start | bytes 786440 | tf_op jit(solution)/shard_map/ppermute | solution.py:386
  90.8 37.5 %collective-permute-start.7 = (f32[512,256]{1,0:T(8,128)S(1)}, f32[512,256]{1,0:T(8,128)S(1)}, u32[]{:S(2)}, u32[]{:S(2)}) collective-permute-start(f32[512,256]{1,0:T(8,128)S(1)} %pad_maximum_fusion), channel_id=1, source_target_pairs={{0,1},{1,0},{2,3},{3,2},{4,5},{5,4},{6,7},{7,6},{8,9},{9,8},{10,11... | collective-permute-start | bytes 1572872 | tf_op jit(solution)/shard_map/ppermute | solution.py:386
  104.6 13.5 %collective-permute-start.30 = (f32[256,256]{1,0:T(8,128)S(1)}, f32[256,256]{1,0:T(8,128)S(1)}, u32[]{:S(2)}, u32[]{:S(2)}) collective-permute-start(f32[256,256]{1,0:T(8,128)S(1)} %solve.1.refs_6_), channel_id=1, source_target_pairs={{0,8},{4,12},{8,0},{12,4},{16,24},{20,28},{24,16},{28,20},{1,9},{5... | collective-permute-start | bytes 786440 | tf_op jit(solution)/shard_map/ppermute | solution.py:386
  105.0 21.3 %collective-permute-start.32 = (f32[256,256]{1,0:T(8,128)S(1)}, f32[256,256]{1,0:T(8,128)S(1)}, u32[]{:S(2)}, u32[]{:S(2)}) collective-permute-start(f32[256,256]{1,0:T(8,128)S(1)} %solve.1.refs_6_), channel_id=1, source_target_pairs={{0,16},{4,20},{8,24},{12,28},{16,0},{20,4},{24,8},{28,12},{1,17},{... | collective-permute-start | bytes 786440 | tf_op jit(solution)/shard_map/ppermute | solution.py:386
  106.1 21.4 %collective-permute-start.34 = (f32[256,256]{1,0:T(8,128)S(1)}, f32[256,256]{1,0:T(8,128)S(1)}, u32[]{:S(2)}, u32[]{:S(2)}) collective-permute-start(f32[256,256]{1,0:T(8,128)S(1)} %solve.1.refs_6_), channel_id=1, source_target_pairs={{0,24},{4,28},{8,16},{12,20},{16,8},{20,12},{24,0},{28,4},{1,25},{... | collective-permute-start | bytes 786440 | tf_op jit(solution)/shard_map/ppermute | solution.py:386
  109.1 19.3 %collective-permute-start.29 = (f32[256,256]{1,0:T(8,128)S(1)}, f32[256,256]{1,0:T(8,128)S(1)}, u32[]{:S(2)}, u32[]{:S(2)}) collective-permute-start(f32[256,256]{1,0:T(8,128)S(1)} %solve.1.refs_6_), channel_id=1, source_target_pairs={{0,4},{4,0},{8,12},{12,8},{16,20},{20,16},{24,28},{28,24},{1,5},{5... | collective-permute-start | bytes 786440 | tf_op jit(solution)/shard_map/ppermute | solution.py:386
  118.1 18.7 %collective-permute-start.31 = (f32[256,256]{1,0:T(8,128)S(1)}, f32[256,256]{1,0:T(8,128)S(1)}, u32[]{:S(2)}, u32[]{:S(2)}) collective-permute-start(f32[256,256]{1,0:T(8,128)S(1)} %collective-permute-done.30.refs_8_), channel_id=1, source_target_pairs={{0,4},{4,0},{8,12},{12,8},{16,20},{20,16},{24,28},{28,24},{1,5},{5... | collective-permute-start | bytes 786440 | tf_op jit(solution)/shard_map/ppermute | solution.py:386
  126.3 10.5 %collective-permute-start.33 = (f32[256,256]{1,0:T(8,128)S(1)}, f32[256,256]{1,0:T(8,128)S(1)}, u32[]{:S(2)}, u32[]{:S(2)}) collective-permute-start(f32[256,256]{1,0:T(8,128)S(1)} %collective-permute-done.32.refs_3_), channel_id=1, source_target_pairs={{0,4},{4,0},{8,12},{12,8},{16,20},{20,16},{24,28},{28,24},{1,5},{5... | collective-permute-start | bytes 786440 | tf_op jit(solution)/shard_map/ppermute | solution.py:386
  127.5 11.1 %collective-permute-start.35 = (f32[256,256]{1,0:T(8,128)S(1)}, f32[256,256]{1,0:T(8,128)S(1)}, u32[]{:S(2)}, u32[]{:S(2)}) collective-permute-start(f32[256,256]{1,0:T(8,128)S(1)} %collective-permute-done.34.refs_4_), channel_id=1, source_target_pairs={{0,4},{4,0},{8,12},{12,8},{16,20},{20,16},{24,28},{28,24},{1,5},{5... | collective-permute-start | bytes 786440 | tf_op jit(solution)/shard_map/ppermute | solution.py:386
  (15 other events, 230.3 us)

commit v3 on v2

--- a/solution.py
+++ b/solution.py
@@ -44,82 +44,71 @@
 
 
 def pick(table, slots, i):
-    step = slots[1] - slots[0] if len(slots) > 1 else 0
-    return table[slots[0] + step * i]
+    slot = slots[-1]
+    for k in range(len(slots) - 1):
+        slot = jnp.where(i == k, slots[k], slot)
+    return table[slot]
 
 
 def shape(*dims, dtype=F32):
     return jax.ShapeDtypeStruct(dims, dtype)
 
 
-def sketch_kernel(steps, table, field, test, corange, s_send, s_keep, m_send, m_keep, t, om, thi, tlo, total, sems):
-    i = pl.program_id(0)
-    rank = t.shape[1]
-    rows = field.shape[0]
-    copies = (pltpu.make_async_copy(test, t, sems.at[0]), pltpu.make_async_copy(corange, om, sems.at[1]))
-
-    @pl.when(i == 0)
-    def _():
-        for copy in copies:
-            copy.start()
-        copies[0].wait()
-        thi[...], tlo[...] = split(t[...])
-        copies[1].wait()
-        total[...] = jnp.zeros_like(total)
-
-    s = three(split(field[...]), (thi[...], tlo[...]))
-    half = steps // 2
-    at = pl.ds(pl.multiple_of((i % half) * rows, 8), rows)
-
-    @pl.when(i < half)
-    def _():
-        s_send[at, :] = s
-
-    @pl.when(i >= half)
-    def _():
-        s_keep[at, :] = s
-
-    slot = jnp.where(i == 0, 1, jnp.where(i == 1, 3, jnp.where(i == 2, 2, 0)))
-    here = pl.multiple_of((table[TM] ^ slot) * rows, 128)
-    total[...] += three(split(om[:, pl.ds(here, rows)]), split(s))
-
-    @pl.when(i == steps - 1)
-    def _():
-        part = total.shape[0] // 8
-        for out, slots in ((m_send, (1, 5, 3, 7)), (m_keep, (0, 4, 2, 6))):
-            for j, k in enumerate(slots):
-                from_ = pl.multiple_of((table[MINE] ^ k) * part, 8)
-                out[j * part:(j + 1) * part, :] = total[pl.ds(from_, part), :]
+def sketch_kernel(table, field, test, corange, s_send, s_keep, m_send, m_keep, fhi, flo, f, t, om, total, sems):
+    cells, times = field.shape
+    steps = f.shape[0]
+    rows = cells // steps
+    starts = [pl.multiple_of((table[TM] ^ slot) * rows, 128) for slot in (1, 3, 2, 0)]
+    first = pltpu.make_async_copy(test, t, sems.at[steps])
+    second = pltpu.make_async_copy(corange, om, sems.at[steps + 1])
+    blocks = [pltpu.make_async_copy(field.at[pl.ds(at, rows), :], f.at[i], sems.at[i]) for i, at in enumerate(starts)]
+    first.start()
+    blocks[0].start()
+    second.start()
+    for block in blocks[1:]:
+        block.start()
+    first.wait()
+    right = split(t[...])
+    for i, at in enumerate(starts):
+        blocks[i].wait()
+        left = split(f[i])
+        fhi[pl.ds(at, rows), :], flo[pl.ds(at, rows), :] = left
+        s = three(left, right)
+        out, half = (s_send, s_keep)[i // 2], i % 2
+        out[half * rows:(half + 1) * rows, :] = s
+        if i == 0:
+            second.wait()
+        part = three(split(om[:, pl.ds(at, rows)]), split(s))
+        if i == 0:
+            total[...] = part
+        else:
+            total[...] += part
+    part = total.shape[0] // 8
+    for out, slots in ((m_send, (1, 5, 3, 7)), (m_keep, (0, 4, 2, 6))):
+        for j, k in enumerate(slots):
+            at = pl.multiple_of((table[MINE] ^ k) * part, 8)
+            out[j * part:(j + 1) * part, :] = total[pl.ds(at, part), :]
 
 
 def sketches(table, field, test, corange):
     cells, times = field.shape
     rank = test.shape[1]
     steps = 4
-    rows = cells // steps
     wide = corange.shape[0]
-
-    def block(i, p):
-        return (p[TM] ^ jnp.where(i == 0, 1, jnp.where(i == 1, 3, jnp.where(i == 2, 2, 0))), 0)
-
-    return pl.pallas_call(
-        functools.partial(sketch_kernel, steps),
-        grid_spec=pltpu.PrefetchScalarGridSpec(
-            num_scalar_prefetch=1,
-            grid=(steps,),
-            in_specs=[pl.BlockSpec((rows, times), block), HBM, HBM],
-            out_specs=[VMEM] * 4,
-            scratch_shapes=[
-                pltpu.VMEM((times, rank), F32),
-                pltpu.VMEM((wide, cells), F32),
-                pltpu.VMEM((times, rank), BF16),
-                pltpu.VMEM((times, rank), BF16),
-                pltpu.VMEM((wide, rank), F32),
-                pltpu.SemaphoreType.DMA((2,)),
-            ],
-        ),
-        out_shape=[shape(cells // 2, rank)] * 2 + [shape(wide // 2, rank)] * 2,
-        compiler_params=params(36),
+    anywhere = pl.BlockSpec(memory_space=pl.ANY)
+    return pl.pallas_call(
+        sketch_kernel,
+        in_specs=[SMEM] + [anywhere] * 3,
+        out_specs=[VMEM] * 6,
+        scratch_shapes=[
+            pltpu.VMEM((steps, cells // steps, times), F32),
+            pltpu.VMEM((times, rank), F32),
+            pltpu.VMEM((wide, cells), F32),
+            pltpu.VMEM((wide, rank), F32),
+            pltpu.SemaphoreType.DMA((steps + 2,)),
+        ],
+        out_shape=[shape(cells // 2, rank)] * 2 + [shape(wide // 2, rank)] * 2 + [shape(cells, times, dtype=BF16)] * 2,
+        compiler_params=params(52),
         cost_estimate=cost(3 * cells * rank * (times + wide), 4 * cells * times),
         name="sketches",
     )(table, field, test, corange)
@@ -143,6 +132,7 @@
         in_specs=[SMEM, VMEM, VMEM],
         out_specs=[VMEM] * 3,
         scratch_shapes=[pltpu.VMEM((rank, rank), F32)],
+        compiler_params=params(8),
         cost_estimate=cost(6 * a.shape[0] * rank * rank, 12 * a.shape[0] * rank),
         name="gram",
     )(table, a, b)
@@ -156,56 +146,43 @@
 
 
 def rhs_kernel(slots, first, table, *refs):
+    if first:
+        near, far, corange, fhi, flo = refs[:5]
+        outs, (phi, plo, m, om) = refs[5:-4], refs[-4:]
+        half = near.shape[0]
+        rows = half // 4
+        m[:half] = near[...]
+        m[half:] = far[...]
+        for j, slot in enumerate(ORDER):
+            at = pl.multiple_of((table[MINE] ^ slot) * rows, 8)
+            om[j * rows:(j + 1) * rows, :] = corange[pl.ds(at, rows), :]
+        phi[...], plo[...] = split(three(split(m[...].T), split(om[...])))
+    else:
+        phi, plo, fhi, flo = refs[:4]
+        outs = refs[4:]
+    cols = outs[0].shape[1]
+    for k, slot in enumerate(slots):
+        at = pl.ds(pl.multiple_of(table[slot] * cols, 128), cols)
+        outs[k][...] = three((phi[...], plo[...]), (fhi[:, at], flo[:, at]))
+
+
+def rhs_blocks(table, slots, operands, parts, blocks):
     count = len(slots)
-    i = pl.program_id(0)
-    if first:
-        near, far, corange, field = refs[:4]
-        outs, (p, m, om) = refs[4:-3], refs[-3:]
-
-        @pl.when(i == 0)
-        def _():
-            half = near.shape[0]
-            rows = half // 4
-            m[:half] = near[...]
-            m[half:] = far[...]
-            for j, slot in enumerate(ORDER):
-                at = pl.multiple_of((table[MINE] ^ slot) * rows, 8)
-                om[j * rows:(j + 1) * rows, :] = corange[pl.ds(at, rows), :]
-            cells = om.shape[1]
-            p[:, :cells], p[:, 2 * cells:] = split(three(split(m[...].T), split(om[...])))
-            p[:, cells:2 * cells] = p[:, :cells]
-    else:
-        p, field = refs[:2]
-        outs = refs[2:]
-    x = jnp.dot(p[...], stack_rows(split(field[...])), preferred_element_type=F32)
-    for k in range(count):
-        @pl.when(i == k)
-        def _():
-            outs[k][...] = x
-
-
-def rhs_blocks(table, slots, operands, field, blocks):
-    count = len(slots)
-    first = len(operands) > 1
+    first = len(operands) > 2
     rank = operands[0].shape[1] if first else operands[0].shape[0]
-    cells = field.shape[0]
-    cols = field.shape[1] // blocks
+    cells, times = parts[0].shape
+    cols = times // blocks
     wide = operands[2].shape[0] if first else 0
-    whole = lambda dims: pl.BlockSpec(dims, lambda i, p: (0, 0))
     return pl.pallas_call(
         functools.partial(rhs_kernel, slots, first),
-        grid_spec=pltpu.PrefetchScalarGridSpec(
-            num_scalar_prefetch=1,
-            grid=(count,),
-            in_specs=[whole(x.shape) for x in operands] + [pl.BlockSpec((cells, cols), lambda i, p: (0, pick(p, slots, i)))],
-            out_specs=[whole((rank, cols))] * count + [whole((rank, 3 * cells))] * first,
-            scratch_shapes=[pltpu.VMEM((wide, rank), F32), pltpu.VMEM((wide, cells), F32)] * first,
-        ),
-        out_shape=[shape(rank, cols)] * count + [shape(rank, 3 * cells, dtype=BF16)] * first,
-        compiler_params=params(32),
+        in_specs=[SMEM] + [VMEM] * (len(operands) + 2),
+        out_specs=[VMEM] * (count + 2 * first),
+        scratch_shapes=[pltpu.VMEM((wide, rank), F32), pltpu.VMEM((wide, cells), F32)] * first,
+        out_shape=[shape(rank, cols)] * count + [shape(rank, cells, dtype=BF16)] * (2 * first),
+        compiler_params=params(20),
         cost_estimate=cost(3 * count * rank * cells * cols, 4 * count * cells * cols),
         name="rhs",
-    )(table, *operands, field)
+    )(table, *operands, *parts)
 
 
 def eliminate(blocks):
@@ -240,11 +217,11 @@
     return lax.broadcasted_iota(jnp.int32, dims, 0), lax.broadcasted_iota(jnp.int32, dims, 1)
 
 
-def factor_both(n, tables):
+def factor_both(n, tables, panels):
     r, c = iotas((PANEL, PANEL))
     eye = jnp.where(r == c, 1.0, 0.0)
     r, c = iotas((PANEL, 2 * PANEL))
-    for k in range(n // PANEL):
+    for k in panels:
         lo, hi = k * PANEL, (k + 1) * PANEL
         blocks = [jnp.concatenate([t[lo:hi, lo:hi], eye], axis=1) for t in tables]
         left = lo // 128 * 128
@@ -261,7 +238,7 @@
             t[lo:hi, left:right] = panel
 
 
-def factor_kernel(table, g_near, g_far, m_near, m_far, upper, inverse, normal_inverse, t1, t2):
+def factor_head(panels, table, g_near, g_far, m_near, m_far, t1, t2):
     n = g_near.shape[1]
     half = n // 2
     r, c = iotas((n, n))
@@ -272,25 +249,46 @@
     t1[:, n:] = eye
     t2[:, :n] = exact(m_near[...], m_near[...], ((0,), (0,))) + exact(m_far[...], m_far[...], ((0,), (0,)))
     t2[:, n:] = eye
-    factor_both(n, (t1, t2))
+    factor_both(n, (t1, t2), panels)
+
+
+def factor_tail(panels, head1, head2, upper, inverse, normal_inverse, t1, t2):
+    n = upper.shape[0]
+    t1[...] = head1[...]
+    t2[...] = head2[...]
+    factor_both(n, (t1, t2), panels)
+    r, c = iotas((n, n))
     upper[...] = jnp.where(r <= c, t1[:, :n], 0.0)
     inverse[...] = t1[:, n:]
     k = t2[:, n:]
     normal_inverse[...] = exact(k, k, ((0,), (0,)))
 
 
-def factor(table, g_near, g_far, m_near, m_far):
+def factor_start(table, g_near, g_far, m_near, m_far):
     n = g_near.shape[1]
     return pl.pallas_call(
-        factor_kernel,
+        functools.partial(factor_head, range(n // PANEL // 2)),
+        out_shape=[shape(n, 2 * n)] * 2,
+        in_specs=[SMEM] + [VMEM] * 4,
+        out_specs=[VMEM] * 2,
+        compiler_params=params(16),
+        cost_estimate=cost(3 * 10**9, 4 * n * n * 8),
+        name="factor",
+    )(table, g_near, g_far, m_near, m_far)
+
+
+def factor_end(t1, t2):
+    n = t1.shape[0]
+    return pl.pallas_call(
+        functools.partial(factor_tail, range(n // PANEL // 2, n // PANEL)),
         out_shape=[shape(n, n)] * 3,
-        in_specs=[SMEM] + [VMEM] * 4,
+        in_specs=[VMEM] * 2,
         out_specs=[VMEM] * 3,
         scratch_shapes=[pltpu.VMEM((n, 2 * n), F32)] * 2,
-        compiler_params=params(20),
-        cost_estimate=cost(5 * 10**9, 4 * n * n * 8),
+        compiler_params=params(16),
+        cost_estimate=cost(3 * 10**9, 4 * n * n * 8),
         name="factor",
-    )(table, g_near, g_far, m_near, m_far)
+    )(t1, t2)
 
 
 def solve_kernel(projector, *refs):
@@ -392,12 +390,15 @@
     return lax.optimization_barrier(arrays)
 
 
-def along_z(v):
+def z_parts(v):
+    return [v] + [swap("space", bit)(v) for bit in (2, 4, 6)] if lax.axis_size("space") >= 8 else [v]
+
+
+def z_sum(parts):
     spaces = lax.axis_size("space")
-    bit = 2
-    if spaces >= 8:
-        v = (v + swap("space", 2)(v)) + (swap("space", 4)(v) + swap("space", 6)(v))
-        bit = 8
+    v, bit = parts[0], 2
+    if len(parts) > 1:
+        v, bit = (v + parts[1]) + (parts[2] + parts[3]), 8
     while bit < spaces:
         v = v + swap("space", bit)(v)
         bit *= 2
@@ -423,7 +424,7 @@
     numbers = jnp.array([core, mine, tm])
     table = jnp.concatenate([near ^ jnp.arange(8, dtype=jnp.int32), numbers]).astype(jnp.int32)
 
-    s_send, s_keep, m_send, m_keep = sketches(table, field, range_test, corange_test)
+    s_send, s_keep, m_send, m_keep, *parts = sketches(table, field, range_test, corange_test)
     quarter = s_keep.shape[0] // 2
 
     m = m_keep + to_core(m_send)
@@ -437,7 +438,7 @@
     m, s_x = tie(m, s_x)
     s0, g_send, g = gram_of(table, s_near, s_x)
     g_got = to_core(g_send)
-    m = along_z(m)
+    m = z_sum(z_parts(m))
     m, g, g_got = tie(m, g, g_got)
     g = g + g_got
     g_got = to_x(g)
@@ -448,33 +449,39 @@
     g_got = to_y(g)
 
     send_slots, keep_slots = list(range(count - 1, 0, -2)), list(range(count - 2, -1, -2))
-    cut = (len(send_slots) + 1) // 2
-    *sent, p = rhs_blocks(table, send_slots[:cut], (m, m_far, corange_test), field, count)
-    p, g, g_got = tie(p, g, g_got)
-    g = along_z(g + g_got)
-    if send_slots[cut:]:
-        sent += rhs_blocks(table, send_slots[cut:], (p,), field, count)
-    kept = list(rhs_blocks(table, keep_slots, (p,), field, count))
-    terms = []
+    *sent, phi, plo = rhs_blocks(table, send_slots, (m, m_far, corange_test), parts, count)
+    *sent, g, g_got = tie(*sent, g, g_got)
+    g_parts = z_parts(g + g_got)
+    kept = list(rhs_blocks(table, keep_slots, (phi, plo), parts, count))
+    terms, tables = [], ()
     for k, slot in enumerate(keep_slots):
         got = to_y(sent[k])
         if slot == 0:
             terms += [kept[k], got]
-        else:
-            total = kept[k] + got
-            if k == 0:
-                total, g = tie(total, g)
-            terms.append(swap("space", slot)(total))
+            continue
+        total = kept[k] + got
+        if slot == 2 and tables:
+            total, *tables = tie(total, *tables)
+        terms.append(swap("space", slot)(total))
+        if slot == 6:
+            *g_parts, _ = tie(*g_parts, total)
+        if slot == 2:
+            g = z_sum(g_parts)
+            g_far = to_core(g)
+            m, g, g_far, _ = tie(m, g, g_far, total)
+            tables = factor_start(table, g, g_far, m, m_far)
+    if not tables:
+        g = z_sum(g_parts)
+        tables = factor_start(table, g, to_core(g), m, m_far)
     bit = count
     while bit < spaces:
         mine_sum = functools.reduce(jnp.add, terms)
         terms = [mine_sum, swap("space", bit)(mine_sum)]
         bit *= 2
-    g_far = to_core(g)
     s2 = to_x(s0)
     s13 = to_core(jnp.concatenate([s0, s2], axis=0))
 
-    upper, inverse, inverse_normal = factor(table, g, g_far, m, m_far)
+    upper, inverse, inverse_normal = factor_end(*tables)
     z0 = solve(inverse_normal, terms)
 
     blocks = {0: z0, 1: to_y(z0)}
@@ -485,8 +492,8 @@
 
     left, sparts, uparts, *done = outputs(
         table, [0, 1, 2][:count], scale, (s0, s2, s13, upper, inverse), field, [blocks[k] for k in range(min(3, count))])
-    for slots in ([4, 6], [3, 5, 7]):
-        if count > slots[-1]:
+    for slots in ([4, 6, 3], [5, 7]):
+        if count > max(slots):
             done = outputs(table, slots, None, (sparts, uparts), field, [blocks[k] for k in slots], tuple(done))
     return (left, *done)
 

time: 143 us -> 137 us (0.958)
  local copies, waits for them, and re-layouts: 9.98 us -> 2.21 us
  starting transfers between devices: 43.3 us -> 45.7 us
  other arithmetic: 2.07 us -> 0.46 us
    unnamed x22 -> x10, local copies, waits for them, and re-layouts: 9.97 us -> 2.2 us
    ppermute x34, starting transfers between devices: 42.4 us -> 44.7 us  [go(): return lax.ppermute(x, axis, [(i, i ^ bit) for i in range(n)])]
    pallas_call x5, Pallas kernels: 30.4 us -> 32.6 us  [the longest x1 13.7 us: sketches(): pl.pallas_call(sketch_kernel, in_specs=[SMEM] + [anywhere] * 3, out_specs...]
  transfers between devices with their start and end apart: 36 -> 36, of which waited for: 16 -> 17; matrix products, arithmetic and copies ran while one was open for 1% -> 0% of each run, Pallas kernels for 23% -> 22%
where the time goes in v3:
time: 137 us; the launch traced here: 136 us
  Pallas kernels  46.6 us (34%)
  starting transfers between devices  45.7 us (33%)
  waiting for transfers between devices  40 us (29%)
  local copies, waits for them, and re-layouts  2.21 us (2%)
    ppermute x34, starting transfers between devices, go(): return lax.ppermute(x, axis, [(i, i ^ bit) for i in range(n)])  44.7 us
    ppermute x34, waiting for transfers between devices, go(): return lax.ppermute(x, axis, [(i, i ^ bit) for i in range(n)])  34.4 us
    pallas_call x1, Pallas kernels, sketches(): pl.pallas_call(sketch_kernel, in_specs=[SMEM] + [anywhere] * 3, out_specs...  13.7 us
    pallas_call x3, Pallas kernels, outputs(): pl.pallas_call(functools.partial(output_kernel, slots, scale), grid_spec=...  12.6 us
    pallas_call x1, Pallas kernels, factor_start(): pl.pallas_call(functools.partial(factor_head, range(n // PANEL // 2)), ou...  7.36 us
    pallas_call x1, Pallas kernels, factor_end(): pl.pallas_call(functools.partial(factor_tail, range(n // PANEL // 2, n //...  5.93 us
    pallas_call x2, Pallas kernels, rhs_blocks(): pl.pallas_call(functools.partial(rhs_kernel, slots, first), in_specs=[SME...  5.62 us
    ppermute x2, waiting for transfers between devices, to_xy(): return lax.ppermute(v, ('space', 'tm'), pairs)  5.59 us
  transfers between devices with their start and end apart: 36, of which 17 were waited for; matrix products, arithmetic and copies ran while one was open for 0% of the time, Pallas kernels for 22%

profile of v3, /device:TPU:0, one launch (start us, length us, event | category | flops | bytes accessed | tf_op | source)
XLA Modules:
  0.0 135.8 jit_solution(1839822796950708483)
XLA Ops:
  0.7 13.7 %sketches.1 = (f32[512,256]{1,0:T(8,128)S(1)}, f32[512,256]{1,0:T(8,128)S(1)}, f32[256,256]{1,0:T(8,128)S(1)}, f32[256,256]{1,0:T(8,128)S(1)}, bf16[1024,2048]{1,0:T(8,128)(2,1)}, /*index=5*/bf16[1024,2048]{1,0:T(8,128)(2,1)}) custom-call(s32[11]{0:T(128)S(1)} %pad_add_fusion.table, f32[1024,2048]{1,0:T(8,128)} %refs_2_.5, f32[2048,256]{1,0:T(8,128)} %test.1, ...), custom_call_target="tpu_custom_call" | custom-call | flops 251658240 | bytes 524288 | tf_op jit(solution)/shard_map/sketches/pallas_call | solution.py:99
  15.3 1.8 %collective-permute-done = f32[256,256]{1,0:T(8,128)S(1)} collective-permute-done((f32[256,256]{1,0:T(8,128)S(1)}, f32[256,256]{1,0:T(8,128)S(1)}, u32[]{:S(2)}, u32[]{:S(2)}) %collective-permute-start) | collective-permute-done | bytes 262176 | tf_op jit(solution)/shard_map/ppermute | solution.py:384
  17.2 2.6 %collective-permute-start.2 = (f32[64,256]{1,0:T(8,128)S(1)}, f32[64,256]{1,0:T(8,128)S(1)}, u32[]{:S(2)}, u32[]{:S(2)}) collective-permute-start(f32[64,256]{1,0:T(8,128)S(1)} %get-tuple-element.119), channel_id=1, source_target_pairs={{0,2},{1,3},{2,0},{3,1},{4,6},{5,7},{6,4},{7,5},{8,10},{9,11},{10,... | collective-permute-start | bytes 196616 | tf_op jit(solution)/shard_map/ppermute | solution.py:384
  19.9 1.5 %collective-permute-start.3 = (f32[64,256]{1,0:T(8,128)S(1)}, f32[64,256]{1,0:T(8,128)S(1)}, u32[]{:S(2)}, u32[]{:S(2)}) collective-permute-start(f32[64,256]{1,0:T(8,128)S(1)} %get-tuple-element.121), channel_id=1, source_target_pairs={{0,4},{4,0},{8,12},{12,8},{16,20},{20,16},{24,28},{28,24},{1,5},{5... | collective-permute-start | bytes 196616 | tf_op jit(solution)/shard_map/ppermute | solution.py:384
  21.5 1.9 %collective-permute-start.5 = (f32[256,256]{1,0:T(8,128)S(1)}, f32[256,256]{1,0:T(8,128)S(1)}, u32[]{:S(2)}, u32[]{:S(2)}) collective-permute-start(f32[256,256]{1,0:T(8,128)S(1)} %get-tuple-element.66), channel_id=1, source_target_pairs={{0,2},{1,3},{2,0},{3,1},{4,6},{5,7},{6,4},{7,5},{8,10},{9,11},{10,... | collective-permute-start | bytes 786440 | tf_op jit(solution)/shard_map/ppermute | solution.py:384
  24.1 3.2 %collective-permute-done.4 = f32[64,256]{1,0:T(8,128)S(1)} collective-permute-done((f32[64,256]{1,0:T(8,128)S(1)}, f32[64,256]{1,0:T(8,128)S(1)}, u32[]{:S(2)}, u32[]{:S(2)}) %collective-permute-start.4) | collective-permute-done | bytes 65568 | tf_op jit(solution)/shard_map/ppermute | solution.py:418
  27.3 3.2 %collective-permute-done.5.b = f32[256,256]{1,0:T(8,128)S(1)} collective-permute-done((f32[256,256]{1,0:T(8,128)S(1)}, f32[256,256]{1,0:T(8,128)S(1)}, u32[]{:S(2)}, u32[]{:S(2)}) %collective-permute-start.5) | collective-permute-done | bytes 262176 | tf_op jit(solution)/shard_map/ppermute | solution.py:384
  30.5 3.6 %collective-permute-start.10 = (f32[64,256]{1,0:T(8,128)S(1)}, f32[64,256]{1,0:T(8,128)S(1)}, u32[]{:S(2)}, u32[]{:S(2)}) collective-permute-start(f32[64,256]{1,0:T(8,128)S(1)} %add_add_fusion.2), channel_id=1, source_target_pairs={{0,24},{4,28},{8,16},{12,20},{16,8},{20,12},{24,0},{28,4},{1,25},{... | collective-permute-start | bytes 196616 | tf_op jit(solution)/shard_map/ppermute | solution.py:384
  36.7 1.7 %collective-permute-done.8 = f32[64,256]{1,0:T(8,128)S(1)} collective-permute-done((f32[64,256]{1,0:T(8,128)S(1)}, f32[64,256]{1,0:T(8,128)S(1)}, u32[]{:S(2)}, u32[]{:S(2)}) %collective-permute-start.8) | collective-permute-done | bytes 65568 | tf_op jit(solution)/shard_map/ppermute | solution.py:384
  40.4 1.5 %collective-permute-start.13 = (f32[64,256]{1,0:T(8,128)S(1)}, f32[64,256]{1,0:T(8,128)S(1)}, u32[]{:S(2)}, u32[]{:S(2)}) collective-permute-start(f32[64,256]{1,0:T(8,128)S(1)} %add_add_fusion.1), channel_id=1, source_target_pairs={{0,4},{4,0},{8,12},{12,8},{16,20},{20,16},{24,28},{28,24},{1,5},{5... | collective-permute-start | bytes 196616 | tf_op jit(solution)/shard_map/ppermute | solution.py:384
  44.7 2.4 %collective-permute-done.14 = f32[64,256]{1,0:T(8,128)S(1)} collective-permute-done((f32[64,256]{1,0:T(8,128)S(1)}, f32[64,256]{1,0:T(8,128)S(1)}, u32[]{:S(2)}, u32[]{:S(2)}) %collective-permute-start.14) | collective-permute-done | bytes 65568 | tf_op jit(solution)/shard_map/ppermute | solution.py:418
  48.0 1.6 %collective-permute-start.17 = (f32[128,256]{1,0:T(8,128)S(1)}, f32[128,256]{1,0:T(8,128)S(1)}, u32[]{:S(2)}, u32[]{:S(2)}) collective-permute-start(f32[128,256]{1,0:T(8,128)S(1)} %add.64), channel_id=1, source_target_pairs={{0,4},{4,0},{8,12},{12,8},{16,20},{20,16},{24,28},{28,24},{1,5},{5... | collective-permute-start | bytes 393224 | tf_op jit(solution)/shard_map/ppermute | solution.py:384
  49.6 2.2 %copy-done.1 = bf16[1024,2048]{1,0:T(8,128)(2,1)S(1)} copy-done((bf16[1024,2048]{1,0:T(8,128)(2,1)S(1)}, bf16[1024,2048]{1,0:T(8,128)(2,1)}, u32[]{:S(2)}) %copy-start.1) | copy-done | bytes 4194328
  51.7 3.3 %rhs.2 = (f32[256,256]{1,0:T(8,128)S(1)}, f32[256,256]{1,0:T(8,128)S(1)}, f32[256,256]{1,0:T(8,128)S(1)}, f32[256,256]{1,0:T(8,128)S(1)}, bf16[256,1024]{1,0:T(8,128)(2,1)S(1)}, /*index=5*/bf16[256,1024]{1,0:T(8,128)(2,1)S(1)}) custom-call(s32[11]{0:T(128)S(1)} %pad_add_fusion.table, f32[256,256]{1,0:T(8,128)S(1)} %pad_maximum_fusion.1.refs_0_.m_near, ...), custom_call_target="tpu_custom_call" | custom-call | flops 100663296 | bytes 262144 | tf_op jit(solution)/shard_map/rhs/pallas_call | solution.py:176
  55.0 1.5 %collective-permute-start.25 = (f32[256,256]{1,0:T(8,128)S(1)}, f32[256,256]{1,0:T(8,128)S(1)}, u32[]{:S(2)}, u32[]{:S(2)}) collective-permute-start(f32[256,256]{1,0:T(8,128)S(1)} %get-tuple-element.105), channel_id=1, source_target_pairs={{0,4},{4,0},{8,12},{12,8},{16,20},{20,16},{24,28},{28,24},{1,5},{5... | collective-permute-start | bytes 786440 | tf_op jit(solution)/shard_map/ppermute | solution.py:384
  57.1 1.4 %collective-permute-start.23 = (f32[256,256]{1,0:T(8,128)S(1)}, f32[256,256]{1,0:T(8,128)S(1)}, u32[]{:S(2)}, u32[]{:S(2)}) collective-permute-start(f32[256,256]{1,0:T(8,128)S(1)} %get-tuple-element.95), channel_id=1, source_target_pairs={{0,4},{4,0},{8,12},{12,8},{16,20},{20,16},{24,28},{28,24},{1,5},{5... | collective-permute-start | bytes 786440 | tf_op jit(solution)/shard_map/ppermute | solution.py:384
  58.6 2.1 %collective-permute-start.18 = (f32[128,256]{1,0:T(8,128)S(1)}, f32[128,256]{1,0:T(8,128)S(1)}, u32[]{:S(2)}, u32[]{:S(2)}) collective-permute-start(f32[128,256]{1,0:T(8,128)S(1)} %add.65), channel_id=1, source_target_pairs={{0,8},{4,12},{8,0},{12,4},{16,24},{20,28},{24,16},{28,20},{1,9},{5... | collective-permute-start | bytes 393224 | tf_op jit(solution)/shard_map/ppermute | solution.py:384
  62.1 2.2 %collective-permute-done.25 = f32[256,256]{1,0:T(8,128)S(1)} collective-permute-done((f32[256,256]{1,0:T(8,128)S(1)}, f32[256,256]{1,0:T(8,128)S(1)}, u32[]{:S(2)}, u32[]{:S(2)}) %collective-permute-start.25) | collective-permute-done | bytes 262176 | tf_op jit(solution)/shard_map/ppermute | solution.py:384
  64.2 2.9 %collective-permute-start.20 = (f32[128,256]{1,0:T(8,128)S(1)}, f32[128,256]{1,0:T(8,128)S(1)}, u32[]{:S(2)}, u32[]{:S(2)}) collective-permute-start(f32[128,256]{1,0:T(8,128)S(1)} %add.65), channel_id=1, source_target_pairs={{0,24},{4,28},{8,16},{12,20},{16,8},{20,12},{24,0},{28,4},{1,25},{... | collective-permute-start | bytes 393224 | tf_op jit(solution)/shard_map/ppermute | solution.py:384
  67.1 2.8 %collective-permute-done.21 = f32[256,256]{1,0:T(8,128)S(1)} collective-permute-done((f32[256,256]{1,0:T(8,128)S(1)}, f32[256,256]{1,0:T(8,128)S(1)}, u32[]{:S(2)}, u32[]{:S(2)}) %collective-permute-start.21) | collective-permute-done | bytes 262176 | tf_op jit(solution)/shard_map/ppermute | solution.py:384
  70.9 2.3 %rhs.3 = (f32[256,256]{1,0:T(8,128)S(1)}, f32[256,256]{1,0:T(8,128)S(1)}, f32[256,256]{1,0:T(8,128)S(1)}, f32[256,256]{1,0:T(8,128)S(1)}) custom-call(s32[11]{0:T(128)S(1)} %pad_add_fusion.table, bf16[256,1024]{1,0:T(8,128)(2,1)S(1)} %get-tuple-element.86.refs_0_, bf16[256,1024]{1,0:T(8,128)(2,1)S(1)} %get-tuple-element.87.refs_1_, ...), custom_call_target="tpu_custom_call" | custom-call | flops 100663296 | bytes 262144 | tf_op jit(solution)/shard_map/rhs/pallas_call | solution.py:176
  73.4 1.5 %collective-permute-start.28 = (f32[256,256]{1,0:T(8,128)S(1)}, f32[256,256]{1,0:T(8,128)S(1)}, u32[]{:S(2)}, u32[]{:S(2)}) collective-permute-start(f32[256,256]{1,0:T(8,128)S(1)} %get-tuple-element.107), channel_id=1, source_target_pairs={{0,4},{4,0},{8,12},{12,8},{16,20},{20,16},{24,28},{28,24},{1,5},{5... | collective-permute-start | bytes 786440 | tf_op jit(solution)/shard_map/ppermute | solution.py:384
  74.9 1.8 %collective-permute-start.26 = (f32[256,256]{1,0:T(8,128)S(1)}, f32[256,256]{1,0:T(8,128)S(1)}, u32[]{:S(2)}, u32[]{:S(2)}) collective-permute-start(f32[256,256]{1,0:T(8,128)S(1)} %add.71), channel_id=1, source_target_pairs={{0,16},{4,20},{8,24},{12,28},{16,0},{20,4},{24,8},{28,12},{1,17},{... | collective-permute-start | bytes 786440 | tf_op jit(solution)/shard_map/ppermute | solution.py:384
  76.7 2.6 %collective-permute-start.24 = (f32[256,256]{1,0:T(8,128)S(1)}, f32[256,256]{1,0:T(8,128)S(1)}, u32[]{:S(2)}, u32[]{:S(2)}) collective-permute-start(f32[256,256]{1,0:T(8,128)S(1)} %add.66), channel_id=1, source_target_pairs={{0,24},{4,28},{8,16},{12,20},{16,8},{20,12},{24,0},{28,4},{1,25},{... | collective-permute-start | bytes 786440 | tf_op jit(solution)/shard_map/ppermute | solution.py:384
  81.2 7.4 %factor.2 = (f32[256,512]{1,0:T(8,128)S(1)}, f32[256,512]{1,0:T(8,128)S(1)}) custom-call(s32[11]{0:T(128)S(1)} %pad_add_fusion.table, f32[128,256]{1,0:T(8,128)S(1)} %add_add_fusion.g_near, f32[128,256]{1,0:T(8,128)S(1)} %collective-permute-done.22.g_far, f32[256,256]{1,0:T(8,128)S(1)} %pad_maximum_fusion.1.refs_0_.m_near, ...), custom_call_target="tpu_custom_call" | custom-call | flops 375000000 | bytes 131072 | tf_op jit(solution)/shard_map/factor/pallas_call | solution.py:269
  88.6 5.9 %factor.3 = (f32[256,256]{1,0:T(8,128)S(1)}, f32[256,256]{1,0:T(8,128)S(1)}, f32[256,256]{1,0:T(8,128)S(1)}) custom-call(f32[256,512]{1,0:T(8,128)S(1)} %get-tuple-element.99.head1, f32[256,512]{1,0:T(8,128)S(1)} %get-tuple-element.100.head2), custom_call_target="tpu_custom_call" | custom-call | flops 375000000 | bytes 131072 | tf_op jit(solution)/shard_map/factor/pallas_call | solution.py:282
  95.2 4.6 %collective-permute-start.30 = (f32[256,256]{1,0:T(8,128)S(1)}, f32[256,256]{1,0:T(8,128)S(1)}, u32[]{:S(2)}, u32[]{:S(2)}) collective-permute-start(f32[256,256]{1,0:T(8,128)S(1)} %solve.1.refs_6_), channel_id=1, source_target_pairs={{0,8},{4,12},{8,0},{12,4},{16,24},{20,28},{24,16},{28,20},{1,9},{5... | collective-permute-start | bytes 786440 | tf_op jit(solution)/shard_map/ppermute | solution.py:384
  103.2 7.4 %collective-permute-done.30.refs_8_ = f32[256,256]{1,0:T(8,128)S(1)} collective-permute-done((f32[256,256]{1,0:T(8,128)S(1)}, f32[256,256]{1,0:T(8,128)S(1)}, u32[]{:S(2)}, u32[]{:S(2)}) %collective-permute-start.30) | collective-permute-done | bytes 262176 | tf_op jit(solution)/shard_map/ppermute | solution.py:384
  111.3 9.8 %collective-permute-done.31.refs_3_ = f32[256,256]{1,0:T(8,128)S(1)} collective-permute-done((f32[256,256]{1,0:T(8,128)S(1)}, f32[256,256]{1,0:T(8,128)S(1)}, u32[]{:S(2)}, u32[]{:S(2)}) %collective-permute-start.31) | collective-permute-done | bytes 262176 | tf_op jit(solution)/shard_map/ppermute | solution.py:384
  123.2 5.3 %outputs.3 = (f32[1024,256]{1,0:T(8,128)}, bf16[1024,768]{1,0:T(8,128)(2,1)S(1)}, bf16[256,768]{1,0:T(8,128)(2,1)S(1)}, f32[256,2048]{1,0:T(8,128)}, f32[1024,2048]{1,0:T(8,128)}) custom-call(s32[11]{0:T(128)S(1)} %pad_add_fusion.table, f32[256,256]{1,0:T(8,128)S(1)} %get-tuple-element.68.refs_0_, f32[256,256]{1,0:T(8,128)S(1)} %collective-permute-done.6.refs_1_, ...), custom_call_target="tpu_custom_call" | custom-call | flops 75497472 | bytes 393216 | tf_op jit(solution)/shard_map/outputs/pallas_call | solution.py:356
  128.5 4.1 %outputs.4 = (f32[256,2048]{1,0:T(8,128)}, f32[1024,2048]{1,0:T(8,128)}) custom-call(s32[11]{0:T(128)S(1)} %pad_add_fusion.table, bf16[1024,768]{1,0:T(8,128)(2,1)S(1)} %get-tuple-element.109.refs_0_, bf16[256,768]{1,0:T(8,128)(2,1)S(1)} %get-tuple-element.110.refs_1_, f32[1024,2048]{1,0:T(8,128)S(1)} %bitcast.4, ...), custom_call_target="tpu_custom_call", output_to_operand_aliasing={{0}: (7, {}), {1}: (8, {})} | custom-call | flops 75497472 | bytes 393216 | tf_op jit(solution)/shard_map/outputs/pallas_call | solution.py:356
  132.6 3.2 %outputs.5 = (f32[256,2048]{1,0:T(8,128)}, f32[1024,2048]{1,0:T(8,128)}) custom-call(s32[11]{0:T(128)S(1)} %pad_add_fusion.table, bf16[1024,768]{1,0:T(8,128)(2,1)S(1)} %get-tuple-element.109.refs_0_, bf16[256,768]{1,0:T(8,128)(2,1)S(1)} %get-tuple-element.110.refs_1_, f32[1024,2048]{1,0:T(8,128)S(1)} %bitcast.4, ...), custom_call_target="tpu_custom_call", output_to_operand_aliasing={{0}: (6, {}), {1}: (7, {})} | custom-call | flops 50331648 | bytes 262144 | tf_op jit(solution)/shard_map/outputs/pallas_call | solution.py:356
  (77 shorter events, 21.8 us)
Async XLA Ops:
  17.2 6.1 %collective-permute-start.2 = (f32[64,256]{1,0:T(8,128)S(1)}, f32[64,256]{1,0:T(8,128)S(1)}, u32[]{:S(2)}, u32[]{:S(2)}) collective-permute-start(f32[64,256]{1,0:T(8,128)S(1)} %get-tuple-element.119), channel_id=1, source_target_pairs={{0,2},{1,3},{2,0},{3,1},{4,6},{5,7},{6,4},{7,5},{8,10},{9,11},{10,... | collective-permute-start | bytes 196616 | tf_op jit(solution)/shard_map/ppermute | solution.py:384
  19.9 4.3 %collective-permute-start.3 = (f32[64,256]{1,0:T(8,128)S(1)}, f32[64,256]{1,0:T(8,128)S(1)}, u32[]{:S(2)}, u32[]{:S(2)}) collective-permute-start(f32[64,256]{1,0:T(8,128)S(1)} %get-tuple-element.121), channel_id=1, source_target_pairs={{0,4},{4,0},{8,12},{12,8},{16,20},{20,16},{24,28},{28,24},{1,5},{5... | collective-permute-start | bytes 196616 | tf_op jit(solution)/shard_map/ppermute | solution.py:384
  21.4 5.9 %collective-permute-start.4 = (f32[64,256]{1,0:T(8,128)S(1)}, f32[64,256]{1,0:T(8,128)S(1)}, u32[]{:S(2)}, u32[]{:S(2)}) collective-permute-start(f32[64,256]{1,0:T(8,128)S(1)} %get-tuple-element.120), channel_id=1, source_target_pairs={{0,6},{1,7},{2,4},{3,5},{4,2},{5,3},{6,0},{7,1},{8,14},{9,15},{10,... | collective-permute-start | bytes 196616 | tf_op jit(solution)/shard_map/ppermute | solution.py:418
  21.5 9.0 %collective-permute-start.5 = (f32[256,256]{1,0:T(8,128)S(1)}, f32[256,256]{1,0:T(8,128)S(1)}, u32[]{:S(2)}, u32[]{:S(2)}) collective-permute-start(f32[256,256]{1,0:T(8,128)S(1)} %get-tuple-element.66), channel_id=1, source_target_pairs={{0,2},{1,3},{2,0},{3,1},{4,6},{5,7},{6,4},{7,5},{8,10},{9,11},{10,... | collective-permute-start | bytes 786440 | tf_op jit(solution)/shard_map/ppermute | solution.py:384
  30.5 6.1 %collective-permute-start.10 = (f32[64,256]{1,0:T(8,128)S(1)}, f32[64,256]{1,0:T(8,128)S(1)}, u32[]{:S(2)}, u32[]{:S(2)}) collective-permute-start(f32[64,256]{1,0:T(8,128)S(1)} %add_add_fusion.2), channel_id=1, source_target_pairs={{0,24},{4,28},{8,16},{12,20},{16,8},{20,12},{24,0},{28,4},{1,25},{... | collective-permute-start | bytes 196616 | tf_op jit(solution)/shard_map/ppermute | solution.py:384
  34.1 4.3 %collective-permute-start.8 = (f32[64,256]{1,0:T(8,128)S(1)}, f32[64,256]{1,0:T(8,128)S(1)}, u32[]{:S(2)}, u32[]{:S(2)}) collective-permute-start(f32[64,256]{1,0:T(8,128)S(1)} %add_add_fusion.2), channel_id=1, source_target_pairs={{0,8},{4,12},{8,0},{12,4},{16,24},{20,28},{24,16},{28,20},{1,9},{5... | collective-permute-start | bytes 196616 | tf_op jit(solution)/shard_map/ppermute | solution.py:384
  34.1 5.2 %collective-permute-start.9 = (f32[64,256]{1,0:T(8,128)S(1)}, f32[64,256]{1,0:T(8,128)S(1)}, u32[]{:S(2)}, u32[]{:S(2)}) collective-permute-start(f32[64,256]{1,0:T(8,128)S(1)} %add_add_fusion.2), channel_id=1, source_target_pairs={{0,16},{4,20},{8,24},{12,28},{16,0},{20,4},{24,8},{28,12},{1,17},{... | collective-permute-start | bytes 196616 | tf_op jit(solution)/shard_map/ppermute | solution.py:384
  35.9 3.4 %collective-permute-start.11 = (f32[128,256]{1,0:T(8,128)S(1)}, f32[128,256]{1,0:T(8,128)S(1)}, u32[]{:S(2)}, u32[]{:S(2)}) collective-permute-start(f32[128,256]{1,0:T(8,128)S(1)} %get-tuple-element.71), channel_id=1, source_target_pairs={{0,1},{1,0},{2,3},{3,2},{4,5},{5,4},{6,7},{7,6},{8,9},{9,8},{10,11... | collective-permute-start | bytes 393224 | tf_op jit(solution)/shard_map/ppermute | solution.py:384
  39.3 5.0 %collective-permute-start.12 = (f32[64,256]{1,0:T(8,128)S(1)}, f32[64,256]{1,0:T(8,128)S(1)}, u32[]{:S(2)}, u32[]{:S(2)}) collective-permute-start(f32[64,256]{1,0:T(8,128)S(1)} %add_add_fusion.1), channel_id=1, source_target_pairs={{0,2},{1,3},{2,0},{3,1},{4,6},{5,7},{6,4},{7,5},{8,10},{9,11},{10,... | collective-permute-start | bytes 196616 | tf_op jit(solution)/shard_map/ppermute | solution.py:384
  40.4 4.3 %collective-permute-start.13 = (f32[64,256]{1,0:T(8,128)S(1)}, f32[64,256]{1,0:T(8,128)S(1)}, u32[]{:S(2)}, u32[]{:S(2)}) collective-permute-start(f32[64,256]{1,0:T(8,128)S(1)} %add_add_fusion.1), channel_id=1, source_target_pairs={{0,4},{4,0},{8,12},{12,8},{16,20},{20,16},{24,28},{28,24},{1,5},{5... | collective-permute-start | bytes 196616 | tf_op jit(solution)/shard_map/ppermute | solution.py:384
  42.0 5.2 %collective-permute-start.14 = (f32[64,256]{1,0:T(8,128)S(1)}, f32[64,256]{1,0:T(8,128)S(1)}, u32[]{:S(2)}, u32[]{:S(2)}) collective-permute-start(f32[64,256]{1,0:T(8,128)S(1)} %add_add_fusion.1), channel_id=1, source_target_pairs={{0,6},{1,7},{2,4},{3,5},{4,2},{5,3},{6,0},{7,1},{8,14},{9,15},{10,... | collective-permute-start | bytes 196616 | tf_op jit(solution)/shard_map/ppermute | solution.py:418
  42.9 5.0 %collective-permute-start.15 = (f32[128,256]{1,0:T(8,128)S(1)}, f32[128,256]{1,0:T(8,128)S(1)}, u32[]{:S(2)}, u32[]{:S(2)}) collective-permute-start(f32[128,256]{1,0:T(8,128)S(1)} %add.63), channel_id=1, source_target_pairs={{0,2},{1,3},{2,0},{3,1},{4,6},{5,7},{6,4},{7,5},{8,10},{9,11},{10,... | collective-permute-start | bytes 393224 | tf_op jit(solution)/shard_map/ppermute | solution.py:384
  48.0 7.1 %collective-permute-start.17 = (f32[128,256]{1,0:T(8,128)S(1)}, f32[128,256]{1,0:T(8,128)S(1)}, u32[]{:S(2)}, u32[]{:S(2)}) collective-permute-start(f32[128,256]{1,0:T(8,128)S(1)} %add.64), channel_id=1, source_target_pairs={{0,4},{4,0},{8,12},{12,8},{16,20},{20,16},{24,28},{28,24},{1,5},{5... | collective-permute-start | bytes 393224 | tf_op jit(solution)/shard_map/ppermute | solution.py:384
  55.0 9.2 %collective-permute-start.25 = (f32[256,256]{1,0:T(8,128)S(1)}, f32[256,256]{1,0:T(8,128)S(1)}, u32[]{:S(2)}, u32[]{:S(2)}) collective-permute-start(f32[256,256]{1,0:T(8,128)S(1)} %get-tuple-element.105), channel_id=1, source_target_pairs={{0,4},{4,0},{8,12},{12,8},{16,20},{20,16},{24,28},{28,24},{1,5},{5... | collective-permute-start | bytes 786440 | tf_op jit(solution)/shard_map/ppermute | solution.py:384
  56.5 13.3 %collective-permute-start.21 = (f32[256,256]{1,0:T(8,128)S(1)}, f32[256,256]{1,0:T(8,128)S(1)}, u32[]{:S(2)}, u32[]{:S(2)}) collective-permute-start(f32[256,256]{1,0:T(8,128)S(1)} %get-tuple-element.89), channel_id=1, source_target_pairs={{0,4},{4,0},{8,12},{12,8},{16,20},{20,16},{24,28},{28,24},{1,5},{5... | collective-permute-start | bytes 786440 | tf_op jit(solution)/shard_map/ppermute | solution.py:384
  57.1 22.2 %collective-permute-start.23 = (f32[256,256]{1,0:T(8,128)S(1)}, f32[256,256]{1,0:T(8,128)S(1)}, u32[]{:S(2)}, u32[]{:S(2)}) collective-permute-start(f32[256,256]{1,0:T(8,128)S(1)} %get-tuple-element.95), channel_id=1, source_target_pairs={{0,4},{4,0},{8,12},{12,8},{16,20},{20,16},{24,28},{28,24},{1,5},{5... | collective-permute-start | bytes 786440 | tf_op jit(solution)/shard_map/ppermute | solution.py:384
  58.6 14.8 %collective-permute-start.18 = (f32[128,256]{1,0:T(8,128)S(1)}, f32[128,256]{1,0:T(8,128)S(1)}, u32[]{:S(2)}, u32[]{:S(2)}) collective-permute-start(f32[128,256]{1,0:T(8,128)S(1)} %add.65), channel_id=1, source_target_pairs={{0,8},{4,12},{8,0},{12,4},{16,24},{20,28},{24,16},{28,20},{1,9},{5... | collective-permute-start | bytes 393224 | tf_op jit(solution)/shard_map/ppermute | solution.py:384
  60.7 14.2 %collective-permute-start.19 = (f32[128,256]{1,0:T(8,128)S(1)}, f32[128,256]{1,0:T(8,128)S(1)}, u32[]{:S(2)}, u32[]{:S(2)}) collective-permute-start(f32[128,256]{1,0:T(8,128)S(1)} %add.65), channel_id=1, source_target_pairs={{0,16},{4,20},{8,24},{12,28},{16,0},{20,4},{24,8},{28,12},{1,17},{... | collective-permute-start | bytes 393224 | tf_op jit(solution)/shard_map/ppermute | solution.py:384
  64.2 12.5 %collective-permute-start.20 = (f32[128,256]{1,0:T(8,128)S(1)}, f32[128,256]{1,0:T(8,128)S(1)}, u32[]{:S(2)}, u32[]{:S(2)}) collective-permute-start(f32[128,256]{1,0:T(8,128)S(1)} %add.65), channel_id=1, source_target_pairs={{0,24},{4,28},{8,16},{12,20},{16,8},{20,12},{24,0},{28,4},{1,25},{... | collective-permute-start | bytes 393224 | tf_op jit(solution)/shard_map/ppermute | solution.py:384
  69.9 9.8 %collective-permute-start.6 = (f32[256,256]{1,0:T(8,128)S(1)}, f32[256,256]{1,0:T(8,128)S(1)}, u32[]{:S(2)}, u32[]{:S(2)}) collective-permute-start(f32[256,256]{1,0:T(8,128)S(1)} %get-tuple-element.68.refs_0_), channel_id=1, source_target_pairs={{0,2},{1,3},{2,0},{3,1},{4,6},{5,7},{6,4},{7,5},{8,10},{9,11},{10,... | collective-permute-start | bytes 786440 | tf_op jit(solution)/shard_map/ppermute | solution.py:384
  73.4 21.1 %collective-permute-start.28 = (f32[256,256]{1,0:T(8,128)S(1)}, f32[256,256]{1,0:T(8,128)S(1)}, u32[]{:S(2)}, u32[]{:S(2)}) collective-permute-start(f32[256,256]{1,0:T(8,128)S(1)} %get-tuple-element.107), channel_id=1, source_target_pairs={{0,4},{4,0},{8,12},{12,8},{16,20},{20,16},{24,28},{28,24},{1,5},{5... | collective-permute-start | bytes 786440 | tf_op jit(solution)/shard_map/ppermute | solution.py:384
  74.9 19.9 %collective-permute-start.26 = (f32[256,256]{1,0:T(8,128)S(1)}, f32[256,256]{1,0:T(8,128)S(1)}, u32[]{:S(2)}, u32[]{:S(2)}) collective-permute-start(f32[256,256]{1,0:T(8,128)S(1)} %add.71), channel_id=1, source_target_pairs={{0,16},{4,20},{8,24},{12,28},{16,0},{20,4},{24,8},{28,12},{1,17},{... | collective-permute-start | bytes 786440 | tf_op jit(solution)/shard_map/ppermute | solution.py:384
  76.7 18.1 %collective-permute-start.24 = (f32[256,256]{1,0:T(8,128)S(1)}, f32[256,256]{1,0:T(8,128)S(1)}, u32[]{:S(2)}, u32[]{:S(2)}) collective-permute-start(f32[256,256]{1,0:T(8,128)S(1)} %add.66), channel_id=1, source_target_pairs={{0,24},{4,28},{8,16},{12,20},{16,8},{20,12},{24,0},{28,4},{1,25},{... | collective-permute-start | bytes 786440 | tf_op jit(solution)/shard_map/ppermute | solution.py:384
  79.3 15.5 %collective-permute-start.27 = (f32[256,256]{1,0:T(8,128)S(1)}, f32[256,256]{1,0:T(8,128)S(1)}, u32[]{:S(2)}, u32[]{:S(2)}) collective-permute-start(f32[256,256]{1,0:T(8,128)S(1)} %add.70), channel_id=1, source_target_pairs={{0,8},{4,12},{8,0},{12,4},{16,24},{20,28},{24,16},{28,20},{1,9},{5... | collective-permute-start | bytes 786440 | tf_op jit(solution)/shard_map/ppermute | solution.py:384
  81.1 42.1 %collective-permute-start.7 = (f32[512,256]{1,0:T(8,128)S(1)}, f32[512,256]{1,0:T(8,128)S(1)}, u32[]{:S(2)}, u32[]{:S(2)}) collective-permute-start(f32[512,256]{1,0:T(8,128)S(1)} %pad_maximum_fusion), channel_id=1, source_target_pairs={{0,1},{1,0},{2,3},{3,2},{4,5},{5,4},{6,7},{7,6},{8,9},{9,8},{10,11... | collective-permute-start | bytes 1572872 | tf_op jit(solution)/shard_map/ppermute | solution.py:384
  95.2 15.4 %collective-permute-start.30 = (f32[256,256]{1,0:T(8,128)S(1)}, f32[256,256]{1,0:T(8,128)S(1)}, u32[]{:S(2)}, u32[]{:S(2)}) collective-permute-start(f32[256,256]{1,0:T(8,128)S(1)} %solve.1.refs_6_), channel_id=1, source_target_pairs={{0,8},{4,12},{8,0},{12,4},{16,24},{20,28},{24,16},{28,20},{1,9},{5... | collective-permute-start | bytes 786440 | tf_op jit(solution)/shard_map/ppermute | solution.py:384
  99.7 21.4 %collective-permute-start.31 = (f32[256,256]{1,0:T(8,128)S(1)}, f32[256,256]{1,0:T(8,128)S(1)}, u32[]{:S(2)}, u32[]{:S(2)}) collective-permute-start(f32[256,256]{1,0:T(8,128)S(1)} %solve.1.refs_6_), channel_id=1, source_target_pairs={{0,16},{4,20},{8,24},{12,28},{16,0},{20,4},{24,8},{28,12},{1,17},{... | collective-permute-start | bytes 786440 | tf_op jit(solution)/shard_map/ppermute | solution.py:384
  101.1 20.8 %collective-permute-start.33 = (f32[256,256]{1,0:T(8,128)S(1)}, f32[256,256]{1,0:T(8,128)S(1)}, u32[]{:S(2)}, u32[]{:S(2)}) collective-permute-start(f32[256,256]{1,0:T(8,128)S(1)} %solve.1.refs_6_), channel_id=1, source_target_pairs={{0,24},{4,28},{8,16},{12,20},{16,8},{20,12},{24,0},{28,4},{1,25},{... | collective-permute-start | bytes 786440 | tf_op jit(solution)/shard_map/ppermute | solution.py:384
  102.4 20.7 %collective-permute-start.29 = (f32[256,256]{1,0:T(8,128)S(1)}, f32[256,256]{1,0:T(8,128)S(1)}, u32[]{:S(2)}, u32[]{:S(2)}) collective-permute-start(f32[256,256]{1,0:T(8,128)S(1)} %solve.1.refs_6_), channel_id=1, source_target_pairs={{0,4},{4,0},{8,12},{12,8},{16,20},{20,16},{24,28},{28,24},{1,5},{5... | collective-permute-start | bytes 786440 | tf_op jit(solution)/shard_map/ppermute | solution.py:384
  110.6 17.9 %collective-permute-start.35 = (f32[256,256]{1,0:T(8,128)S(1)}, f32[256,256]{1,0:T(8,128)S(1)}, u32[]{:S(2)}, u32[]{:S(2)}) collective-permute-start(f32[256,256]{1,0:T(8,128)S(1)} %collective-permute-done.30.refs_8_), channel_id=1, source_target_pairs={{0,4},{4,0},{8,12},{12,8},{16,20},{20,16},{24,28},{28,24},{1,5},{5... | collective-permute-start | bytes 786440 | tf_op jit(solution)/shard_map/ppermute | solution.py:384
  121.1 11.5 %collective-permute-start.32 = (f32[256,256]{1,0:T(8,128)S(1)}, f32[256,256]{1,0:T(8,128)S(1)}, u32[]{:S(2)}, u32[]{:S(2)}) collective-permute-start(f32[256,256]{1,0:T(8,128)S(1)} %collective-permute-done.31.refs_3_), channel_id=1, source_target_pairs={{0,4},{4,0},{8,12},{12,8},{16,20},{20,16},{24,28},{28,24},{1,5},{5... | collective-permute-start | bytes 786440 | tf_op jit(solution)/shard_map/ppermute | solution.py:384
  121.9 10.7 %collective-permute-start.34 = (f32[256,256]{1,0:T(8,128)S(1)}, f32[256,256]{1,0:T(8,128)S(1)}, u32[]{:S(2)}, u32[]{:S(2)}) collective-permute-start(f32[256,256]{1,0:T(8,128)S(1)} %collective-permute-done.33.refs_4_), channel_id=1, source_target_pairs={{0,4},{4,0},{8,12},{12,8},{16,20},{20,16},{24,28},{28,24},{1,5},{5... | collective-permute-start | bytes 786440 | tf_op jit(solution)/shard_map/ppermute | solution.py:384
  (9 other events, 198.2 us)

commit v4 on v3

--- a/solution.py
+++ b/solution.py
@@ -435,7 +435,7 @@
     k0, kx, ky, kxy = (m[i * rows:(i + 1) * rows] for i in range(4))
     s_x = to_x(s_far)
     m = (k0 + to_x(kx)) + (to_y(ky) + to_xy(kxy))
-    m, s_x = tie(m, s_x)
+    s_x, _ = tie(s_x, m)
     s0, g_send, g = gram_of(table, s_near, s_x)
     g_got = to_core(g_send)
     m = z_sum(z_parts(m))
@@ -443,7 +443,7 @@
     g = g + g_got
     g_got = to_x(g)
     m = jnp.concatenate([m, to_x(m), to_y(m), to_xy(m)], axis=0)
-    m, g, g_got = tie(m, g, g_got)
+    g, g_got, _ = tie(g, g_got, m)
     g = g + g_got
     m_far = to_core(m)
     g_got = to_y(g)

time: 137 us -> 135 us (0.985)
  starting transfers between devices: 45.7 us -> 42.2 us
  waiting for transfers between devices: 40 us -> 41.8 us
    ppermute x34, starting transfers between devices: 44.7 us -> 39.7 us  [go(): return lax.ppermute(x, axis, [(i, i ^ bit) for i in range(n)])]
    ppermute x34, waiting for transfers between devices: 34.4 us -> 37.3 us  [go(): return lax.ppermute(x, axis, [(i, i ^ bit) for i in range(n)])]
    ppermute x2, starting transfers between devices: 1.01 us -> 2.48 us  [to_xy(): return lax.ppermute(v, ('space', 'tm'), pairs)]
  transfers between devices with their start and end apart: 36 -> 36, of which waited for: 17 -> 15; matrix products, arithmetic and copies ran while one was open for 0% -> 0% of each run, Pallas kernels for 22% -> 22%
where the time goes in v4:
time: 135 us; the launch traced here: 134 us
  Pallas kernels  46.6 us (35%)
  starting transfers between devices  42.2 us (31%)
  waiting for transfers between devices  41.8 us (31%)
  local copies, waits for them, and re-layouts  2.23 us (2%)
    ppermute x34, starting transfers between devices, go(): return lax.ppermute(x, axis, [(i, i ^ bit) for i in range(n)])  39.7 us
    ppermute x34, waiting for transfers between devices, go(): return lax.ppermute(x, axis, [(i, i ^ bit) for i in range(n)])  37.3 us
    pallas_call x1, Pallas kernels, sketches(): pl.pallas_call(sketch_kernel, in_specs=[SMEM] + [anywhere] * 3, out_specs...  13.7 us
    pallas_call x3, Pallas kernels, outputs(): pl.pallas_call(functools.partial(output_kernel, slots, scale), grid_spec=...  12.6 us
    pallas_call x1, Pallas kernels, factor_start(): pl.pallas_call(functools.partial(factor_head, range(n // PANEL // 2)), ou...  7.36 us
    pallas_call x1, Pallas kernels, factor_end(): pl.pallas_call(functools.partial(factor_tail, range(n // PANEL // 2, n //...  5.93 us
    pallas_call x2, Pallas kernels, rhs_blocks(): pl.pallas_call(functools.partial(rhs_kernel, slots, first), in_specs=[SME...  5.61 us
    ppermute x2, waiting for transfers between devices, to_xy(): return lax.ppermute(v, ('space', 'tm'), pairs)  4.57 us
  transfers between devices with their start and end apart: 36, of which 15 were waited for; matrix products, arithmetic and copies ran while one was open for 0% of the time, Pallas kernels for 22%

profile of v4, /device:TPU:0, one launch (start us, length us, event | category | flops | bytes accessed | tf_op | source)
XLA Modules:
  0.0 134.4 jit_solution(15080999770469453611)
XLA Ops:
  0.7 13.7 %sketches.1 = (f32[512,256]{1,0:T(8,128)S(1)}, f32[512,256]{1,0:T(8,128)S(1)}, f32[256,256]{1,0:T(8,128)S(1)}, f32[256,256]{1,0:T(8,128)S(1)}, bf16[1024,2048]{1,0:T(8,128)(2,1)}, /*index=5*/bf16[1024,2048]{1,0:T(8,128)(2,1)}) custom-call(s32[11]{0:T(128)S(1)} %pad_add_fusion.table, f32[1024,2048]{1,0:T(8,128)} %refs_2_.5, f32[2048,256]{1,0:T(8,128)} %test.1, ...), custom_call_target="tpu_custom_call" | custom-call | flops 251658240 | bytes 524288 | tf_op jit(solution)/shard_map/sketches/pallas_call | solution.py:99
  15.3 1.8 %collective-permute-done = f32[256,256]{1,0:T(8,128)S(1)} collective-permute-done((f32[256,256]{1,0:T(8,128)S(1)}, f32[256,256]{1,0:T(8,128)S(1)}, u32[]{:S(2)}, u32[]{:S(2)}) %collective-permute-start) | collective-permute-done | bytes 262176 | tf_op jit(solution)/shard_map/ppermute | solution.py:384
  17.2 2.6 %collective-permute-start.3 = (f32[64,256]{1,0:T(8,128)S(1)}, f32[64,256]{1,0:T(8,128)S(1)}, u32[]{:S(2)}, u32[]{:S(2)}) collective-permute-start(f32[64,256]{1,0:T(8,128)S(1)} %get-tuple-element.115), channel_id=1, source_target_pairs={{0,2},{1,3},{2,0},{3,1},{4,6},{5,7},{6,4},{7,5},{8,10},{9,11},{10,... | collective-permute-start | bytes 196616 | tf_op jit(solution)/shard_map/ppermute | solution.py:384
  19.9 1.5 %collective-permute-start.4 = (f32[64,256]{1,0:T(8,128)S(1)}, f32[64,256]{1,0:T(8,128)S(1)}, u32[]{:S(2)}, u32[]{:S(2)}) collective-permute-start(f32[64,256]{1,0:T(8,128)S(1)} %get-tuple-element.117), channel_id=1, source_target_pairs={{0,4},{4,0},{8,12},{12,8},{16,20},{20,16},{24,28},{28,24},{1,5},{5... | collective-permute-start | bytes 196616 | tf_op jit(solution)/shard_map/ppermute | solution.py:384
  21.5 1.9 %collective-permute-start.2 = (f32[256,256]{1,0:T(8,128)S(1)}, f32[256,256]{1,0:T(8,128)S(1)}, u32[]{:S(2)}, u32[]{:S(2)}) collective-permute-start(f32[256,256]{1,0:T(8,128)S(1)} %get-tuple-element.63), channel_id=1, source_target_pairs={{0,2},{1,3},{2,0},{3,1},{4,6},{5,7},{6,4},{7,5},{8,10},{9,11},{10,... | collective-permute-start | bytes 786440 | tf_op jit(solution)/shard_map/ppermute | solution.py:384
  24.1 3.2 %collective-permute-done.5 = f32[64,256]{1,0:T(8,128)S(1)} collective-permute-done((f32[64,256]{1,0:T(8,128)S(1)}, f32[64,256]{1,0:T(8,128)S(1)}, u32[]{:S(2)}, u32[]{:S(2)}) %collective-permute-start.5) | collective-permute-done | bytes 65568 | tf_op jit(solution)/shard_map/ppermute | solution.py:418
  27.3 3.7 %collective-permute-start.10 = (f32[64,256]{1,0:T(8,128)S(1)}, f32[64,256]{1,0:T(8,128)S(1)}, u32[]{:S(2)}, u32[]{:S(2)}) collective-permute-start(f32[64,256]{1,0:T(8,128)S(1)} %add_add_fusion.2), channel_id=1, source_target_pairs={{0,24},{4,28},{8,16},{12,20},{16,8},{20,12},{24,0},{28,4},{1,25},{... | collective-permute-start | bytes 196616 | tf_op jit(solution)/shard_map/ppermute | solution.py:384
  37.4 2.4 %collective-permute-start.14 = (f32[64,256]{1,0:T(8,128)S(1)}, f32[64,256]{1,0:T(8,128)S(1)}, u32[]{:S(2)}, u32[]{:S(2)}) collective-permute-start(f32[64,256]{1,0:T(8,128)S(1)} %add_add_fusion.1), channel_id=1, source_target_pairs={{0,6},{1,7},{2,4},{3,5},{4,2},{5,3},{6,0},{7,1},{8,14},{9,15},{10,... | collective-permute-start | bytes 196616 | tf_op jit(solution)/shard_map/ppermute | solution.py:418
  42.6 1.5 %collective-permute-start.16 = (f32[128,256]{1,0:T(8,128)S(1)}, f32[128,256]{1,0:T(8,128)S(1)}, u32[]{:S(2)}, u32[]{:S(2)}) collective-permute-start(f32[128,256]{1,0:T(8,128)S(1)} %add.63), channel_id=1, source_target_pairs={{0,2},{1,3},{2,0},{3,1},{4,6},{5,7},{6,4},{7,5},{8,10},{9,11},{10,... | collective-permute-start | bytes 393224 | tf_op jit(solution)/shard_map/ppermute | solution.py:384
  44.1 4.5 %collective-permute-done.16 = f32[128,256]{1,0:T(8,128)S(1)} collective-permute-done((f32[128,256]{1,0:T(8,128)S(1)}, f32[128,256]{1,0:T(8,128)S(1)}, u32[]{:S(2)}, u32[]{:S(2)}) %collective-permute-start.16) | collective-permute-done | bytes 131104 | tf_op jit(solution)/shard_map/ppermute | solution.py:384
  48.6 1.6 %collective-permute-start.17 = (f32[128,256]{1,0:T(8,128)S(1)}, f32[128,256]{1,0:T(8,128)S(1)}, u32[]{:S(2)}, u32[]{:S(2)}) collective-permute-start(f32[128,256]{1,0:T(8,128)S(1)} %add.64), channel_id=1, source_target_pairs={{0,4},{4,0},{8,12},{12,8},{16,20},{20,16},{24,28},{28,24},{1,5},{5... | collective-permute-start | bytes 393224 | tf_op jit(solution)/shard_map/ppermute | solution.py:384
  50.2 2.2 %copy-done.1 = bf16[1024,2048]{1,0:T(8,128)(2,1)S(1)} copy-done((bf16[1024,2048]{1,0:T(8,128)(2,1)S(1)}, bf16[1024,2048]{1,0:T(8,128)(2,1)}, u32[]{:S(2)}) %copy-start.1) | copy-done | bytes 4194328
  52.3 3.3 %rhs.2 = (f32[256,256]{1,0:T(8,128)S(1)}, f32[256,256]{1,0:T(8,128)S(1)}, f32[256,256]{1,0:T(8,128)S(1)}, f32[256,256]{1,0:T(8,128)S(1)}, bf16[256,1024]{1,0:T(8,128)(2,1)S(1)}, /*index=5*/bf16[256,1024]{1,0:T(8,128)(2,1)S(1)}) custom-call(s32[11]{0:T(128)S(1)} %pad_add_fusion.table, f32[256,256]{1,0:T(8,128)S(1)} %constant_dynamic-update-slice_fusion.refs_0_.m_near, ...), custom_call_target="tpu_custom_call" | custom-call | flops 100663296 | bytes 262144 | tf_op jit(solution)/shard_map/rhs/pallas_call | solution.py:176
  56.2 1.5 %collective-permute-start.21 = (f32[256,256]{1,0:T(8,128)S(1)}, f32[256,256]{1,0:T(8,128)S(1)}, u32[]{:S(2)}, u32[]{:S(2)}) collective-permute-start(f32[256,256]{1,0:T(8,128)S(1)} %get-tuple-element.85), channel_id=1, source_target_pairs={{0,4},{4,0},{8,12},{12,8},{16,20},{20,16},{24,28},{28,24},{1,5},{5... | collective-permute-start | bytes 786440 | tf_op jit(solution)/shard_map/ppermute | solution.py:384
  58.3 2.1 %collective-permute-start.18 = (f32[128,256]{1,0:T(8,128)S(1)}, f32[128,256]{1,0:T(8,128)S(1)}, u32[]{:S(2)}, u32[]{:S(2)}) collective-permute-start(f32[128,256]{1,0:T(8,128)S(1)} %add.65), channel_id=1, source_target_pairs={{0,8},{4,12},{8,0},{12,4},{16,24},{20,28},{24,16},{28,20},{1,9},{5... | collective-permute-start | bytes 393224 | tf_op jit(solution)/shard_map/ppermute | solution.py:384
  60.6 4.3 %collective-permute-done.25 = f32[256,256]{1,0:T(8,128)S(1)} collective-permute-done((f32[256,256]{1,0:T(8,128)S(1)}, f32[256,256]{1,0:T(8,128)S(1)}, u32[]{:S(2)}, u32[]{:S(2)}) %collective-permute-start.25) | collective-permute-done | bytes 262176 | tf_op jit(solution)/shard_map/ppermute | solution.py:384
  64.9 1.6 %collective-permute-start.20 = (f32[128,256]{1,0:T(8,128)S(1)}, f32[128,256]{1,0:T(8,128)S(1)}, u32[]{:S(2)}, u32[]{:S(2)}) collective-permute-start(f32[128,256]{1,0:T(8,128)S(1)} %add.65), channel_id=1, source_target_pairs={{0,24},{4,28},{8,16},{12,20},{16,8},{20,12},{24,0},{28,4},{1,25},{... | collective-permute-start | bytes 393224 | tf_op jit(solution)/shard_map/ppermute | solution.py:384
  66.6 4.0 %collective-permute-done.21 = f32[256,256]{1,0:T(8,128)S(1)} collective-permute-done((f32[256,256]{1,0:T(8,128)S(1)}, f32[256,256]{1,0:T(8,128)S(1)}, u32[]{:S(2)}, u32[]{:S(2)}) %collective-permute-start.21) | collective-permute-done | bytes 262176 | tf_op jit(solution)/shard_map/ppermute | solution.py:384
  72.0 2.3 %rhs.3 = (f32[256,256]{1,0:T(8,128)S(1)}, f32[256,256]{1,0:T(8,128)S(1)}, f32[256,256]{1,0:T(8,128)S(1)}, f32[256,256]{1,0:T(8,128)S(1)}) custom-call(s32[11]{0:T(128)S(1)} %pad_add_fusion.table, bf16[256,1024]{1,0:T(8,128)(2,1)S(1)} %get-tuple-element.82.refs_0_, bf16[256,1024]{1,0:T(8,128)(2,1)S(1)} %get-tuple-element.83.refs_1_, ...), custom_call_target="tpu_custom_call" | custom-call | flops 100663296 | bytes 262144 | tf_op jit(solution)/shard_map/rhs/pallas_call | solution.py:176
  76.4 3.0 %collective-permute-start.24 = (f32[256,256]{1,0:T(8,128)S(1)}, f32[256,256]{1,0:T(8,128)S(1)}, u32[]{:S(2)}, u32[]{:S(2)}) collective-permute-start(f32[256,256]{1,0:T(8,128)S(1)} %add.66), channel_id=1, source_target_pairs={{0,24},{4,28},{8,16},{12,20},{16,8},{20,12},{24,0},{28,4},{1,25},{... | collective-permute-start | bytes 786440 | tf_op jit(solution)/shard_map/ppermute | solution.py:384
  81.3 7.4 %factor.2 = (f32[256,512]{1,0:T(8,128)S(1)}, f32[256,512]{1,0:T(8,128)S(1)}) custom-call(s32[11]{0:T(128)S(1)} %pad_add_fusion.table, f32[128,256]{1,0:T(8,128)S(1)} %add_add_fusion.g_near, f32[128,256]{1,0:T(8,128)S(1)} %collective-permute-done.22.g_far, f32[256,256]{1,0:T(8,128)S(1)} %constant_dynamic-update-slice_fusion.refs_0_.m_near, ...), custom_call_target="tpu_custom_call" | custom-call | flops 375000000 | bytes 131072 | tf_op jit(solution)/shard_map/factor/pallas_call | solution.py:269
  88.7 5.9 %factor.3 = (f32[256,256]{1,0:T(8,128)S(1)}, f32[256,256]{1,0:T(8,128)S(1)}, f32[256,256]{1,0:T(8,128)S(1)}) custom-call(f32[256,512]{1,0:T(8,128)S(1)} %get-tuple-element.95.head1, f32[256,512]{1,0:T(8,128)S(1)} %get-tuple-element.96.head2), custom_call_target="tpu_custom_call" | custom-call | flops 375000000 | bytes 131072 | tf_op jit(solution)/shard_map/factor/pallas_call | solution.py:282
  95.0 3.3 %collective-permute-start.30 = (f32[256,256]{1,0:T(8,128)S(1)}, f32[256,256]{1,0:T(8,128)S(1)}, u32[]{:S(2)}, u32[]{:S(2)}) collective-permute-start(f32[256,256]{1,0:T(8,128)S(1)} %solve.1.refs_6_), channel_id=1, source_target_pairs={{0,8},{4,12},{8,0},{12,4},{16,24},{20,28},{24,16},{28,20},{1,9},{5... | collective-permute-start | bytes 786440 | tf_op jit(solution)/shard_map/ppermute | solution.py:384
  98.7 2.1 %collective-permute-start.33 = (f32[256,256]{1,0:T(8,128)S(1)}, f32[256,256]{1,0:T(8,128)S(1)}, u32[]{:S(2)}, u32[]{:S(2)}) collective-permute-start(f32[256,256]{1,0:T(8,128)S(1)} %solve.1.refs_6_), channel_id=1, source_target_pairs={{0,24},{4,28},{8,16},{12,20},{16,8},{20,12},{24,0},{28,4},{1,25},{... | collective-permute-start | bytes 786440 | tf_op jit(solution)/shard_map/ppermute | solution.py:384
  100.8 1.5 %collective-permute-start.29 = (f32[256,256]{1,0:T(8,128)S(1)}, f32[256,256]{1,0:T(8,128)S(1)}, u32[]{:S(2)}, u32[]{:S(2)}) collective-permute-start(f32[256,256]{1,0:T(8,128)S(1)} %solve.1.refs_6_), channel_id=1, source_target_pairs={{0,4},{4,0},{8,12},{12,8},{16,20},{20,16},{24,28},{28,24},{1,5},{5... | collective-permute-start | bytes 786440 | tf_op jit(solution)/shard_map/ppermute | solution.py:384
  102.3 5.9 %collective-permute-done.30.refs_8_ = f32[256,256]{1,0:T(8,128)S(1)} collective-permute-done((f32[256,256]{1,0:T(8,128)S(1)}, f32[256,256]{1,0:T(8,128)S(1)}, u32[]{:S(2)}, u32[]{:S(2)}) %collective-permute-start.30) | collective-permute-done | bytes 262176 | tf_op jit(solution)/shard_map/ppermute | solution.py:384
  108.2 1.6 %collective-permute-start.35 = (f32[256,256]{1,0:T(8,128)S(1)}, f32[256,256]{1,0:T(8,128)S(1)}, u32[]{:S(2)}, u32[]{:S(2)}) collective-permute-start(f32[256,256]{1,0:T(8,128)S(1)} %collective-permute-done.30.refs_8_), channel_id=1, source_target_pairs={{0,4},{4,0},{8,12},{12,8},{16,20},{20,16},{24,28},{28,24},{1,5},{5... | collective-permute-start | bytes 786440 | tf_op jit(solution)/shard_map/ppermute | solution.py:384
  109.7 10.0 %collective-permute-done.31.refs_3_ = f32[256,256]{1,0:T(8,128)S(1)} collective-permute-done((f32[256,256]{1,0:T(8,128)S(1)}, f32[256,256]{1,0:T(8,128)S(1)}, u32[]{:S(2)}, u32[]{:S(2)}) %collective-permute-start.31) | collective-permute-done | bytes 262176 | tf_op jit(solution)/shard_map/ppermute | solution.py:384
  119.7 1.5 %collective-permute-start.32 = (f32[256,256]{1,0:T(8,128)S(1)}, f32[256,256]{1,0:T(8,128)S(1)}, u32[]{:S(2)}, u32[]{:S(2)}) collective-permute-start(f32[256,256]{1,0:T(8,128)S(1)} %collective-permute-done.31.refs_3_), channel_id=1, source_target_pairs={{0,4},{4,0},{8,12},{12,8},{16,20},{20,16},{24,28},{28,24},{1,5},{5... | collective-permute-start | bytes 786440 | tf_op jit(solution)/shard_map/ppermute | solution.py:384
  121.8 5.3 %outputs.3 = (f32[1024,256]{1,0:T(8,128)}, bf16[1024,768]{1,0:T(8,128)(2,1)S(1)}, bf16[256,768]{1,0:T(8,128)(2,1)S(1)}, f32[256,2048]{1,0:T(8,128)}, f32[1024,2048]{1,0:T(8,128)}) custom-call(s32[11]{0:T(128)S(1)} %pad_add_fusion.table, f32[256,256]{1,0:T(8,128)S(1)} %get-tuple-element.66.refs_0_, f32[256,256]{1,0:T(8,128)S(1)} %collective-permute-done.6.refs_1_, ...), custom_call_target="tpu_custom_call" | custom-call | flops 75497472 | bytes 393216 | tf_op jit(solution)/shard_map/outputs/pallas_call | solution.py:356
  127.1 4.1 %outputs.4 = (f32[256,2048]{1,0:T(8,128)}, f32[1024,2048]{1,0:T(8,128)}) custom-call(s32[11]{0:T(128)S(1)} %pad_add_fusion.table, bf16[1024,768]{1,0:T(8,128)(2,1)S(1)} %get-tuple-element.105.refs_0_, bf16[256,768]{1,0:T(8,128)(2,1)S(1)} %get-tuple-element.106.refs_1_, f32[1024,2048]{1,0:T(8,128)S(1)} %bitcast.4, ...), custom_call_target="tpu_custom_call", output_to_operand_aliasing={{0}: (7, {}), {1}: (8, {})} | custom-call | flops 75497472 | bytes 393216 | tf_op jit(solution)/shard_map/outputs/pallas_call | solution.py:356
  131.2 3.2 %outputs.5 = (f32[256,2048]{1,0:T(8,128)}, f32[1024,2048]{1,0:T(8,128)}) custom-call(s32[11]{0:T(128)S(1)} %pad_add_fusion.table, bf16[1024,768]{1,0:T(8,128)(2,1)S(1)} %get-tuple-element.105.refs_0_, bf16[256,768]{1,0:T(8,128)(2,1)S(1)} %get-tuple-element.106.refs_1_, f32[1024,2048]{1,0:T(8,128)S(1)} %bitcast.4, ...), custom_call_target="tpu_custom_call", output_to_operand_aliasing={{0}: (6, {}), {1}: (7, {})} | custom-call | flops 50331648 | bytes 262144 | tf_op jit(solution)/shard_map/outputs/pallas_call | solution.py:356
  (80 shorter events, 19.0 us)
Async XLA Ops:
  17.2 6.1 %collective-permute-start.3 = (f32[64,256]{1,0:T(8,128)S(1)}, f32[64,256]{1,0:T(8,128)S(1)}, u32[]{:S(2)}, u32[]{:S(2)}) collective-permute-start(f32[64,256]{1,0:T(8,128)S(1)} %get-tuple-element.115), channel_id=1, source_target_pairs={{0,2},{1,3},{2,0},{3,1},{4,6},{5,7},{6,4},{7,5},{8,10},{9,11},{10,... | collective-permute-start | bytes 196616 | tf_op jit(solution)/shard_map/ppermute | solution.py:384
  19.9 4.3 %collective-permute-start.4 = (f32[64,256]{1,0:T(8,128)S(1)}, f32[64,256]{1,0:T(8,128)S(1)}, u32[]{:S(2)}, u32[]{:S(2)}) collective-permute-start(f32[64,256]{1,0:T(8,128)S(1)} %get-tuple-element.117), channel_id=1, source_target_pairs={{0,4},{4,0},{8,12},{12,8},{16,20},{20,16},{24,28},{28,24},{1,5},{5... | collective-permute-start | bytes 196616 | tf_op jit(solution)/shard_map/ppermute | solution.py:384
  21.4 5.9 %collective-permute-start.5 = (f32[64,256]{1,0:T(8,128)S(1)}, f32[64,256]{1,0:T(8,128)S(1)}, u32[]{:S(2)}, u32[]{:S(2)}) collective-permute-start(f32[64,256]{1,0:T(8,128)S(1)} %get-tuple-element.116), channel_id=1, source_target_pairs={{0,6},{1,7},{2,4},{3,5},{4,2},{5,3},{6,0},{7,1},{8,14},{9,15},{10,... | collective-permute-start | bytes 196616 | tf_op jit(solution)/shard_map/ppermute | solution.py:418
  21.5 10.3 %collective-permute-start.2 = (f32[256,256]{1,0:T(8,128)S(1)}, f32[256,256]{1,0:T(8,128)S(1)}, u32[]{:S(2)}, u32[]{:S(2)}) collective-permute-start(f32[256,256]{1,0:T(8,128)S(1)} %get-tuple-element.63), channel_id=1, source_target_pairs={{0,2},{1,3},{2,0},{3,1},{4,6},{5,7},{6,4},{7,5},{8,10},{9,11},{10,... | collective-permute-start | bytes 786440 | tf_op jit(solution)/shard_map/ppermute | solution.py:384
  27.3 6.6 %collective-permute-start.10 = (f32[64,256]{1,0:T(8,128)S(1)}, f32[64,256]{1,0:T(8,128)S(1)}, u32[]{:S(2)}, u32[]{:S(2)}) collective-permute-start(f32[64,256]{1,0:T(8,128)S(1)} %add_add_fusion.2), channel_id=1, source_target_pairs={{0,24},{4,28},{8,16},{12,20},{16,8},{20,12},{24,0},{28,4},{1,25},{... | collective-permute-start | bytes 196616 | tf_op jit(solution)/shard_map/ppermute | solution.py:384
  31.0 4.3 %collective-permute-start.8 = (f32[64,256]{1,0:T(8,128)S(1)}, f32[64,256]{1,0:T(8,128)S(1)}, u32[]{:S(2)}, u32[]{:S(2)}) collective-permute-start(f32[64,256]{1,0:T(8,128)S(1)} %add_add_fusion.2), channel_id=1, source_target_pairs={{0,8},{4,12},{8,0},{12,4},{16,24},{20,28},{24,16},{28,20},{1,9},{5... | collective-permute-start | bytes 196616 | tf_op jit(solution)/shard_map/ppermute | solution.py:384
  31.0 5.2 %collective-permute-start.9 = (f32[64,256]{1,0:T(8,128)S(1)}, f32[64,256]{1,0:T(8,128)S(1)}, u32[]{:S(2)}, u32[]{:S(2)}) collective-permute-start(f32[64,256]{1,0:T(8,128)S(1)} %add_add_fusion.2), channel_id=1, source_target_pairs={{0,16},{4,20},{8,24},{12,28},{16,0},{20,4},{24,8},{28,12},{1,17},{... | collective-permute-start | bytes 196616 | tf_op jit(solution)/shard_map/ppermute | solution.py:384
  36.2 4.3 %collective-permute-start.12 = (f32[64,256]{1,0:T(8,128)S(1)}, f32[64,256]{1,0:T(8,128)S(1)}, u32[]{:S(2)}, u32[]{:S(2)}) collective-permute-start(f32[64,256]{1,0:T(8,128)S(1)} %add_add_fusion.1), channel_id=1, source_target_pairs={{0,2},{1,3},{2,0},{3,1},{4,6},{5,7},{6,4},{7,5},{8,10},{9,11},{10,... | collective-permute-start | bytes 196616 | tf_op jit(solution)/shard_map/ppermute | solution.py:384
  36.9 4.3 %collective-permute-start.13 = (f32[64,256]{1,0:T(8,128)S(1)}, f32[64,256]{1,0:T(8,128)S(1)}, u32[]{:S(2)}, u32[]{:S(2)}) collective-permute-start(f32[64,256]{1,0:T(8,128)S(1)} %add_add_fusion.1), channel_id=1, source_target_pairs={{0,4},{4,0},{8,12},{12,8},{16,20},{20,16},{24,28},{28,24},{1,5},{5... | collective-permute-start | bytes 196616 | tf_op jit(solution)/shard_map/ppermute | solution.py:384
  37.4 5.2 %collective-permute-start.14 = (f32[64,256]{1,0:T(8,128)S(1)}, f32[64,256]{1,0:T(8,128)S(1)}, u32[]{:S(2)}, u32[]{:S(2)}) collective-permute-start(f32[64,256]{1,0:T(8,128)S(1)} %add_add_fusion.1), channel_id=1, source_target_pairs={{0,6},{1,7},{2,4},{3,5},{4,2},{5,3},{6,0},{7,1},{8,14},{9,15},{10,... | collective-permute-start | bytes 196616 | tf_op jit(solution)/shard_map/ppermute | solution.py:418
  42.5 7.6 %collective-permute-start.15 = (f32[256,256]{1,0:T(8,128)S(1)}, f32[256,256]{1,0:T(8,128)S(1)}, u32[]{:S(2)}, u32[]{:S(2)}) collective-permute-start(f32[256,256]{1,0:T(8,128)S(1)} %constant_dynamic-update-slice_fusion.refs_0_.m_near), channel_id=1, source_target_pairs={{0,1},{1,0},{2,3},{3,2},{4,5},{5,4},{6,7},{7,6},{8,9},{9,8},{10,11... | collective-permute-start | bytes 786440 | tf_op jit(solution)/shard_map/ppermute | solution.py:384
  42.6 6.0 %collective-permute-start.16 = (f32[128,256]{1,0:T(8,128)S(1)}, f32[128,256]{1,0:T(8,128)S(1)}, u32[]{:S(2)}, u32[]{:S(2)}) collective-permute-start(f32[128,256]{1,0:T(8,128)S(1)} %add.63), channel_id=1, source_target_pairs={{0,2},{1,3},{2,0},{3,1},{4,6},{5,7},{6,4},{7,5},{8,10},{9,11},{10,... | collective-permute-start | bytes 393224 | tf_op jit(solution)/shard_map/ppermute | solution.py:384
  48.6 7.1 %collective-permute-start.17 = (f32[128,256]{1,0:T(8,128)S(1)}, f32[128,256]{1,0:T(8,128)S(1)}, u32[]{:S(2)}, u32[]{:S(2)}) collective-permute-start(f32[128,256]{1,0:T(8,128)S(1)} %add.64), channel_id=1, source_target_pairs={{0,4},{4,0},{8,12},{12,8},{16,20},{20,16},{24,28},{28,24},{1,5},{5... | collective-permute-start | bytes 393224 | tf_op jit(solution)/shard_map/ppermute | solution.py:384
  55.6 9.3 %collective-permute-start.25 = (f32[256,256]{1,0:T(8,128)S(1)}, f32[256,256]{1,0:T(8,128)S(1)}, u32[]{:S(2)}, u32[]{:S(2)}) collective-permute-start(f32[256,256]{1,0:T(8,128)S(1)} %get-tuple-element.101), channel_id=1, source_target_pairs={{0,4},{4,0},{8,12},{12,8},{16,20},{20,16},{24,28},{28,24},{1,5},{5... | collective-permute-start | bytes 786440 | tf_op jit(solution)/shard_map/ppermute | solution.py:384
  56.2 14.4 %collective-permute-start.21 = (f32[256,256]{1,0:T(8,128)S(1)}, f32[256,256]{1,0:T(8,128)S(1)}, u32[]{:S(2)}, u32[]{:S(2)}) collective-permute-start(f32[256,256]{1,0:T(8,128)S(1)} %get-tuple-element.85), channel_id=1, source_target_pairs={{0,4},{4,0},{8,12},{12,8},{16,20},{20,16},{24,28},{28,24},{1,5},{5... | collective-permute-start | bytes 786440 | tf_op jit(solution)/shard_map/ppermute | solution.py:384
  57.7 21.7 %collective-permute-start.23 = (f32[256,256]{1,0:T(8,128)S(1)}, f32[256,256]{1,0:T(8,128)S(1)}, u32[]{:S(2)}, u32[]{:S(2)}) collective-permute-start(f32[256,256]{1,0:T(8,128)S(1)} %get-tuple-element.91), channel_id=1, source_target_pairs={{0,4},{4,0},{8,12},{12,8},{16,20},{20,16},{24,28},{28,24},{1,5},{5... | collective-permute-start | bytes 786440 | tf_op jit(solution)/shard_map/ppermute | solution.py:384
  58.3 16.2 %collective-permute-start.18 = (f32[128,256]{1,0:T(8,128)S(1)}, f32[128,256]{1,0:T(8,128)S(1)}, u32[]{:S(2)}, u32[]{:S(2)}) collective-permute-start(f32[128,256]{1,0:T(8,128)S(1)} %add.65), channel_id=1, source_target_pairs={{0,8},{4,12},{8,0},{12,4},{16,24},{20,28},{24,16},{28,20},{1,9},{5... | collective-permute-start | bytes 393224 | tf_op jit(solution)/shard_map/ppermute | solution.py:384
  60.3 14.7 %collective-permute-start.19 = (f32[128,256]{1,0:T(8,128)S(1)}, f32[128,256]{1,0:T(8,128)S(1)}, u32[]{:S(2)}, u32[]{:S(2)}) collective-permute-start(f32[128,256]{1,0:T(8,128)S(1)} %add.65), channel_id=1, source_target_pairs={{0,16},{4,20},{8,24},{12,28},{16,0},{20,4},{24,8},{28,12},{1,17},{... | collective-permute-start | bytes 393224 | tf_op jit(solution)/shard_map/ppermute | solution.py:384
  64.9 11.5 %collective-permute-start.20 = (f32[128,256]{1,0:T(8,128)S(1)}, f32[128,256]{1,0:T(8,128)S(1)}, u32[]{:S(2)}, u32[]{:S(2)}) collective-permute-start(f32[128,256]{1,0:T(8,128)S(1)} %add.65), channel_id=1, source_target_pairs={{0,24},{4,28},{8,16},{12,20},{16,8},{20,12},{24,0},{28,4},{1,25},{... | collective-permute-start | bytes 393224 | tf_op jit(solution)/shard_map/ppermute | solution.py:384
  70.6 9.2 %collective-permute-start.6 = (f32[256,256]{1,0:T(8,128)S(1)}, f32[256,256]{1,0:T(8,128)S(1)}, u32[]{:S(2)}, u32[]{:S(2)}) collective-permute-start(f32[256,256]{1,0:T(8,128)S(1)} %get-tuple-element.66.refs_0_), channel_id=1, source_target_pairs={{0,2},{1,3},{2,0},{3,1},{4,6},{5,7},{6,4},{7,5},{8,10},{9,11},{10,... | collective-permute-start | bytes 786440 | tf_op jit(solution)/shard_map/ppermute | solution.py:384
  74.4 20.2 %collective-permute-start.28 = (f32[256,256]{1,0:T(8,128)S(1)}, f32[256,256]{1,0:T(8,128)S(1)}, u32[]{:S(2)}, u32[]{:S(2)}) collective-permute-start(f32[256,256]{1,0:T(8,128)S(1)} %get-tuple-element.103), channel_id=1, source_target_pairs={{0,4},{4,0},{8,12},{12,8},{16,20},{20,16},{24,28},{28,24},{1,5},{5... | collective-permute-start | bytes 786440 | tf_op jit(solution)/shard_map/ppermute | solution.py:384
  75.0 19.6 %collective-permute-start.26 = (f32[256,256]{1,0:T(8,128)S(1)}, f32[256,256]{1,0:T(8,128)S(1)}, u32[]{:S(2)}, u32[]{:S(2)}) collective-permute-start(f32[256,256]{1,0:T(8,128)S(1)} %add.71), channel_id=1, source_target_pairs={{0,16},{4,20},{8,24},{12,28},{16,0},{20,4},{24,8},{28,12},{1,17},{... | collective-permute-start | bytes 786440 | tf_op jit(solution)/shard_map/ppermute | solution.py:384
  76.4 18.2 %collective-permute-start.24 = (f32[256,256]{1,0:T(8,128)S(1)}, f32[256,256]{1,0:T(8,128)S(1)}, u32[]{:S(2)}, u32[]{:S(2)}) collective-permute-start(f32[256,256]{1,0:T(8,128)S(1)} %add.66), channel_id=1, source_target_pairs={{0,24},{4,28},{8,16},{12,20},{16,8},{20,12},{24,0},{28,4},{1,25},{... | collective-permute-start | bytes 786440 | tf_op jit(solution)/shard_map/ppermute | solution.py:384
  79.6 15.0 %collective-permute-start.27 = (f32[256,256]{1,0:T(8,128)S(1)}, f32[256,256]{1,0:T(8,128)S(1)}, u32[]{:S(2)}, u32[]{:S(2)}) collective-permute-start(f32[256,256]{1,0:T(8,128)S(1)} %add.70), channel_id=1, source_target_pairs={{0,8},{4,12},{8,0},{12,4},{16,24},{20,28},{24,16},{28,20},{1,9},{5... | collective-permute-start | bytes 786440 | tf_op jit(solution)/shard_map/ppermute | solution.py:384
  81.2 40.6 %collective-permute-start.7 = (f32[512,256]{1,0:T(8,128)S(1)}, f32[512,256]{1,0:T(8,128)S(1)}, u32[]{:S(2)}, u32[]{:S(2)}) collective-permute-start(f32[512,256]{1,0:T(8,128)S(1)} %pad_maximum_fusion), channel_id=1, source_target_pairs={{0,1},{1,0},{2,3},{3,2},{4,5},{5,4},{6,7},{7,6},{8,9},{9,8},{10,11... | collective-permute-start | bytes 1572872 | tf_op jit(solution)/shard_map/ppermute | solution.py:384
  95.0 13.2 %collective-permute-start.30 = (f32[256,256]{1,0:T(8,128)S(1)}, f32[256,256]{1,0:T(8,128)S(1)}, u32[]{:S(2)}, u32[]{:S(2)}) collective-permute-start(f32[256,256]{1,0:T(8,128)S(1)} %solve.1.refs_6_), channel_id=1, source_target_pairs={{0,8},{4,12},{8,0},{12,4},{16,24},{20,28},{24,16},{28,20},{1,9},{5... | collective-permute-start | bytes 786440 | tf_op jit(solution)/shard_map/ppermute | solution.py:384
  98.3 21.4 %collective-permute-start.31 = (f32[256,256]{1,0:T(8,128)S(1)}, f32[256,256]{1,0:T(8,128)S(1)}, u32[]{:S(2)}, u32[]{:S(2)}) collective-permute-start(f32[256,256]{1,0:T(8,128)S(1)} %solve.1.refs_6_), channel_id=1, source_target_pairs={{0,16},{4,20},{8,24},{12,28},{16,0},{20,4},{24,8},{28,12},{1,17},{... | collective-permute-start | bytes 786440 | tf_op jit(solution)/shard_map/ppermute | solution.py:384
  98.7 22.5 %collective-permute-start.33 = (f32[256,256]{1,0:T(8,128)S(1)}, f32[256,256]{1,0:T(8,128)S(1)}, u32[]{:S(2)}, u32[]{:S(2)}) collective-permute-start(f32[256,256]{1,0:T(8,128)S(1)} %solve.1.refs_6_), channel_id=1, source_target_pairs={{0,24},{4,28},{8,16},{12,20},{16,8},{20,12},{24,0},{28,4},{1,25},{... | collective-permute-start | bytes 786440 | tf_op jit(solution)/shard_map/ppermute | solution.py:384
  100.8 21.0 %collective-permute-start.29 = (f32[256,256]{1,0:T(8,128)S(1)}, f32[256,256]{1,0:T(8,128)S(1)}, u32[]{:S(2)}, u32[]{:S(2)}) collective-permute-start(f32[256,256]{1,0:T(8,128)S(1)} %solve.1.refs_6_), channel_id=1, source_target_pairs={{0,4},{4,0},{8,12},{12,8},{16,20},{20,16},{24,28},{28,24},{1,5},{5... | collective-permute-start | bytes 786440 | tf_op jit(solution)/shard_map/ppermute | solution.py:384
  108.2 18.9 %collective-permute-start.35 = (f32[256,256]{1,0:T(8,128)S(1)}, f32[256,256]{1,0:T(8,128)S(1)}, u32[]{:S(2)}, u32[]{:S(2)}) collective-permute-start(f32[256,256]{1,0:T(8,128)S(1)} %collective-permute-done.30.refs_8_), channel_id=1, source_target_pairs={{0,4},{4,0},{8,12},{12,8},{16,20},{20,16},{24,28},{28,24},{1,5},{5... | collective-permute-start | bytes 786440 | tf_op jit(solution)/shard_map/ppermute | solution.py:384
  119.7 11.5 %collective-permute-start.32 = (f32[256,256]{1,0:T(8,128)S(1)}, f32[256,256]{1,0:T(8,128)S(1)}, u32[]{:S(2)}, u32[]{:S(2)}) collective-permute-start(f32[256,256]{1,0:T(8,128)S(1)} %collective-permute-done.31.refs_3_), channel_id=1, source_target_pairs={{0,4},{4,0},{8,12},{12,8},{16,20},{20,16},{24,28},{28,24},{1,5},{5... | collective-permute-start | bytes 786440 | tf_op jit(solution)/shard_map/ppermute | solution.py:384
  121.2 10.0 %collective-permute-start.34 = (f32[256,256]{1,0:T(8,128)S(1)}, f32[256,256]{1,0:T(8,128)S(1)}, u32[]{:S(2)}, u32[]{:S(2)}) collective-permute-start(f32[256,256]{1,0:T(8,128)S(1)} %collective-permute-done.33.refs_4_), channel_id=1, source_target_pairs={{0,4},{4,0},{8,12},{12,8},{16,20},{20,16},{24,28},{28,24},{1,5},{5... | collective-permute-start | bytes 786440 | tf_op jit(solution)/shard_map/ppermute | solution.py:384
  (9 other events, 196.2 us)
